TPU v7x, 32 devices: a whole 2x2x4 slice. The times are simulated.
32 devices in a mesh: wide: 8 (over z, x), narrow: 4 (over y, core).
Axes of the slice: x: 2, y: 2, z: 4, core: 2. Of those that a mesh axis runs over, the one named last changes fastest.
Arguments:
- enc_ids: int32 [2, 8, 1024], P(None, 'wide'), may hold values from 0 to 32127
- enc_len: int32 [2, 8], P(None, 'wide'), may hold values from 512 to 1024
- tgt_ids: int32 [2, 8, 256], replicated, may hold values from 0 to 32127
- tgt_len: int32 [2, 8], replicated, may hold values from 53 to 256, as said below
- span_mask: int32 [2, 8, 256], replicated, may hold values 0 or 1
- buckets: int32 [2047], replicated, may hold values from 0 to 31
- attn_in: float32 [3, 768, 2304], P(None, 'wide', 'narrow'), may hold values from -0.0625 to 0.0625
- attn_out: float32 [3, 768, 768], P(None, 'narrow', 'wide'), may hold values from -4 to 4
- ff_in: float32 [2, 768, 3072], P(None, 'wide', 'narrow'), may hold values from -0.21875 to 0.21875
- ff_out: float32 [2, 3072, 768], P(None, 'narrow', 'wide'), may hold values from -0.21875 to 0.21875
- table: float32 [32128, 768], P('wide')
- gains: float32 [7, 768], P(None, 'narrow')
- rel: float32 [2, 32, 12], P(None, None, 'narrow'), may hold values from -6 to 6
- mom_attn_in: float32 [3, 768, 2304], P(None, 'wide', 'narrow'), may hold values from -5.340576e-05 to 5.340576e-05
- mom_attn_out: float32 [3, 768, 768], P(None, 'narrow', 'wide'), may hold values from -5.340576e-05 to 5.340576e-05
- mom_ff_in: float32 [2, 768, 3072], P(None, 'wide', 'narrow'), may hold values from -5.340576e-05 to 5.340576e-05
- mom_ff_out: float32 [2, 3072, 768], P(None, 'narrow', 'wide'), may hold values from -5.340576e-05 to 5.340576e-05
- mom_table: float32 [32128, 768], P('wide'), may hold values from -5.340576e-05 to 5.340576e-05
- mom_gains: float32 [7, 768], P(None, 'narrow'), may hold values from -0.00024414062 to 0.00024414062
- mom_rel: float32 [2, 32, 12], P(None, None, 'narrow'), may hold values from -0.00024414062 to 0.00024414062
- avg_attn_in: float32 [3, 768, 2304], P(None, 'wide', 'narrow'), may hold values from -0.0625 to 0.0625
- avg_attn_out: float32 [3, 768, 768], P(None, 'narrow', 'wide'), may hold values from -4 to 4
- avg_ff_in: float32 [2, 768, 3072], P(None, 'wide', 'narrow'), may hold values from -0.21875 to 0.21875
- avg_ff_out: float32 [2, 3072, 768], P(None, 'narrow', 'wide'), may hold values from -0.21875 to 0.21875
- avg_table: float32 [32128, 768], P('wide'), may hold values from -6 to 6
- avg_gains: float32 [7, 768], P(None, 'narrow'), may hold values from 0.5 to 1.5
- avg_rel: float32 [2, 32, 12], P(None, None, 'narrow'), may hold values from -6 to 6
Outputs:
- loss_sum: float32 [], replicated
- loss_count: float32 [], replicated
- grad_norm: float32 [], replicated
- new_attn_in: float32 [3, 768, 2304], P(None, 'wide', 'narrow')
- new_attn_out: float32 [3, 768, 768], P(None, 'narrow', 'wide')
- new_ff_in: float32 [2, 768, 3072], P(None, 'wide', 'narrow')
- new_ff_out: float32 [2, 3072, 768], P(None, 'narrow', 'wide')
- new_table: float32 [32128, 768], P('wide')
- new_gains: float32 [7, 768], P(None, 'narrow')
- new_rel: float32 [2, 32, 12], P(None, None, 'narrow')
- clipped_attn_in: float32 [3, 768, 2304], P(None, 'wide', 'narrow')
- clipped_attn_out: float32 [3, 768, 768], P(None, 'narrow', 'wide')
- clipped_ff_in: float32 [2, 768, 3072], P(None, 'wide', 'narrow')
- clipped_ff_out: float32 [2, 3072, 768], P(None, 'narrow', 'wide')
- clipped_table: float32 [32128, 768], P('wide')
- clipped_gains: float32 [7, 768], P(None, 'narrow')
- clipped_rel: float32 [2, 32, 12], P(None, None, 'narrow')
- average_attn_in: float32 [3, 768, 2304], P(None, 'wide', 'narrow')
- average_attn_out: float32 [3, 768, 768], P(None, 'narrow', 'wide')
- average_ff_in: float32 [2, 768, 3072], P(None, 'wide', 'narrow')
- average_ff_out: float32 [2, 3072, 768], P(None, 'narrow', 'wide')
- average_table: float32 [32128, 768], P('wide')
- average_gains: float32 [7, 768], P(None, 'narrow')
- average_rel: float32 [2, 32, 12], P(None, None, 'narrow')
Inputs may be any that keep to these rules, and one draw needn't show every extreme that they name: `tgt_len`: target lengths rise with the example's place in the micro-batch; the last example of each micro-batch has the full padded length.
All inputs are finite; a program needn't handle non-finite values.
Results may differ from a plain program's by a relative error of at most 0.011.
Values may be sent and summed in bfloat16 or wider, within the bound.
A program may use at most 512 MiB of HBM per device.

v0:
```python
import math

import jax
import jax.numpy as jnp
from jax import lax
from jax.sharding import PartitionSpec as P

D = 768
DH = 64
PARAMS = 41195520


epsilon = 1e-06
masked_score = -1000000000.0
momentum_decay = 0.9
average_decay = 0.9
clip_norm = 0.02
highest = lax.Precision.HIGHEST
contract_rows = (((0,), (0,)), ((), ()))


def to_low(values):
    return lax.optimization_barrier(values.astype(jnp.bfloat16)).astype(jnp.float32)


def matmul(left, right):
    return jnp.dot(left, right, preferred_element_type=jnp.float32)


def outer_rows(left, right):
    return lax.dot_general(left, right, contract_rows, preferred_element_type=jnp.float32)


def rms_forward(inputs, gain_row):
    width = inputs.shape[-1] * lax.axis_size("narrow")
    squares = lax.psum(jnp.sum(inputs * inputs, axis=-1), "narrow")
    inverse = lax.rsqrt(squares / width + epsilon)
    return (inputs * inverse[:, None] * gain_row, inverse)


def rms_backward(inputs, gain_row, inverse, upstream):
    width = inputs.shape[-1] * lax.axis_size("narrow")
    gain_grad = jnp.sum(upstream * inputs * inverse[:, None], axis=0)
    inner = lax.psum(jnp.sum(upstream * gain_row * inputs, axis=-1), "narrow")
    result = inverse[:, None] * gain_row * upstream - inputs * (inverse**3 * inner / width)[:, None]
    return (result, gain_grad)


def widen(values):
    return lax.all_gather(values.astype(jnp.bfloat16), "narrow", axis=1, tiled=True)


def narrow_sum(partial_value):
    return lax.psum_scatter(partial_value, "narrow", scatter_dimension=1, tiled=True)


def widen_grad(upstream):
    return lax.all_gather(upstream.astype(jnp.bfloat16), "narrow", axis=1, tiled=True)


def narrow_grad(partial_value):
    return lax.psum_scatter(partial_value, "narrow", scatter_dimension=1, tiled=True)


def bias_rows(rel_vec, length):
    centre = (rel_vec.shape[0] + 1) // 2 - 1
    heads = rel_vec.shape[1]
    part = rel_vec[centre - length + 1 : centre + length]
    padded = jnp.concatenate([part, jnp.zeros((1, heads), jnp.float32)], axis=0)
    rolled = jnp.concatenate([padded[length - 1 :], padded[: length - 1]], axis=0)
    tiled = jnp.tile(rolled.T, (1, length))
    skewed = tiled[:, : length * (2 * length - 1)].reshape(heads, length, 2 * length - 1)
    return skewed[:, :, :length]


def attend(queries, key_rows, value_rows, base_bias, key_valid):
    bias = base_bias + jnp.where(key_valid, 0.0, masked_score)[None, None, :]
    scores = (
        jnp.einsum("qhx,khx->hqk", queries, key_rows, preferred_element_type=jnp.float32) + bias
    )
    top = jnp.max(scores, axis=-1, keepdims=True)
    expo = jnp.exp(scores - top)
    total = jnp.sum(expo, axis=-1, keepdims=True)
    weights = (expo / total).astype(jnp.bfloat16)
    mixed = jnp.einsum(
        "hqk,khx->qhx", weights, value_rows, preferred_element_type=jnp.float32
    ).astype(jnp.bfloat16)
    return (mixed, (top + jnp.log(total))[:, :, 0])


def attend_back(queries, key_rows, value_rows, base_bias, key_valid, log_total, mixed_grad):
    bias = base_bias + jnp.where(key_valid, 0.0, masked_score)[None, None, :]
    scores = (
        jnp.einsum("qhx,khx->hqk", queries, key_rows, preferred_element_type=jnp.float32) + bias
    )
    weights = jnp.exp(scores - log_total[:, :, None])
    value_grad = jnp.einsum(
        "hqk,qhx->khx", weights.astype(jnp.bfloat16), mixed_grad, preferred_element_type=jnp.float32
    )
    weight_grad = to_low(
        jnp.einsum("qhx,khx->hqk", mixed_grad, value_rows, preferred_element_type=jnp.float32)
    )
    score_grad = (
        weights * (weight_grad - jnp.sum(weights * weight_grad, axis=-1, keepdims=True))
    ).astype(jnp.bfloat16)
    query_grad = jnp.einsum(
        "hqk,khx->qhx", score_grad, key_rows, preferred_element_type=jnp.float32
    )
    key_grad = jnp.einsum("hqk,qhx->khx", score_grad, queries, preferred_element_type=jnp.float32)
    return (query_grad, key_grad, value_grad, score_grad)


def attn_forward(state, gain_row, weight_in, weight_out, source_full, base_bias, key_valid):
    normed, inverse = rms_forward(state, gain_row)
    full = widen(normed)
    examples = key_valid.shape[0]
    heads = weight_out.shape[0] // DH
    width = weight_in.shape[0]
    if source_full is None:
        packed = matmul(full, weight_in).astype(jnp.bfloat16).reshape(examples, -1, heads, 3, DH)
        queries, key_rows, value_rows = (packed[:, :, :, 0], packed[:, :, :, 1], packed[:, :, :, 2])
    else:
        grouped = weight_in.reshape(width, heads, 3, DH)
        queries = (
            matmul(full, grouped[:, :, 0].reshape(width, -1))
            .astype(jnp.bfloat16)
            .reshape(examples, -1, heads, DH)
        )
        pairs = matmul(source_full, grouped[:, :, 1:].reshape(width, -1)).astype(jnp.bfloat16)
        pairs = pairs.reshape(examples, -1, heads, 2, DH)
        key_rows, value_rows = (pairs[:, :, :, 0], pairs[:, :, :, 1])
    mixed, log_total = jax.vmap(attend, (0, 0, 0, None, 0))(
        queries, key_rows, value_rows, base_bias, key_valid
    )
    update = narrow_sum(matmul(mixed.reshape(full.shape[0], -1), weight_out))
    return (state + update, (state, inverse, full, queries, key_rows, value_rows, mixed, log_total))


def attn_backward(
    saved, upstream, gain_row, weight_in, weight_out, source_full, base_bias, key_valid
):
    state, inverse, full, queries, key_rows, value_rows, mixed, log_total = saved
    rows = full.shape[0]
    heads = weight_out.shape[0] // DH
    width = weight_in.shape[0]
    up_full = widen_grad(upstream)
    out_grad = outer_rows(mixed.reshape(rows, -1), up_full)
    mixed_grad = matmul(up_full, weight_out.T).astype(jnp.bfloat16).reshape(mixed.shape)
    query_grad, key_grad, value_grad, score_grad = jax.vmap(attend_back, (0, 0, 0, None, 0, 0, 0))(
        queries, key_rows, value_rows, base_bias, key_valid, log_total, mixed_grad
    )
    bias_grad = jnp.sum(score_grad.astype(jnp.float32), axis=0)
    if source_full is None:
        packed = (
            jnp.stack([query_grad, key_grad, value_grad], axis=3)
            .astype(jnp.bfloat16)
            .reshape(rows, -1)
        )
        in_grad = outer_rows(full, packed)
        full_grad = matmul(packed, weight_in.T)
        source_grad = None
    else:
        grouped = weight_in.reshape(width, heads, 3, DH)
        query_flat = query_grad.astype(jnp.bfloat16).reshape(rows, -1)
        pair_flat = (
            jnp.stack([key_grad, value_grad], axis=3)
            .astype(jnp.bfloat16)
            .reshape(source_full.shape[0], -1)
        )
        query_part = outer_rows(full, query_flat).reshape(width, heads, 1, DH)
        pair_part = outer_rows(source_full, pair_flat).reshape(width, heads, 2, DH)
        in_grad = jnp.concatenate([query_part, pair_part], axis=2).reshape(width, -1)
        full_grad = matmul(query_flat, grouped[:, :, 0].reshape(width, -1).T)
        source_grad = matmul(pair_flat, grouped[:, :, 1:].reshape(width, -1).T)
    normed_grad = to_low(narrow_grad(full_grad))
    state_grad, gain_grad = rms_backward(state, gain_row, inverse, normed_grad)
    return (upstream + state_grad, gain_grad, in_grad, out_grad, bias_grad, source_grad)


def ff_forward(state, gain_row, weight_in, weight_out):
    normed, inverse = rms_forward(state, gain_row)
    full = widen(normed)
    pre = matmul(full, weight_in)
    hidden = jax.nn.gelu(pre).astype(jnp.bfloat16)
    return (state + narrow_sum(matmul(hidden, weight_out)), (state, inverse, full, pre, hidden))


def ff_backward(saved, upstream, gain_row, weight_in, weight_out):
    state, inverse, full, pre, hidden = saved
    up_full = widen_grad(upstream)
    out_grad = outer_rows(hidden, up_full)
    hidden_grad = to_low(matmul(up_full, weight_out.T))
    unused, gelu_back = jax.vjp(jax.nn.gelu, pre)
    pre_grad = gelu_back(hidden_grad)[0].astype(jnp.bfloat16)
    in_grad = outer_rows(full, pre_grad)
    normed_grad = to_low(narrow_grad(matmul(pre_grad, weight_in.T)))
    state_grad, gain_grad = rms_backward(state, gain_row, inverse, normed_grad)
    return (upstream + state_grad, gain_grad, in_grad, out_grad)


def body(
    enc_ids,
    enc_len,
    tgt_ids,
    tgt_len,
    span_mask,
    buckets,
    attn_in,
    attn_out,
    ff_in,
    ff_out,
    table,
    gains,
    rel,
    mom_attn_in,
    mom_attn_out,
    mom_ff_in,
    mom_ff_out,
    mom_table,
    mom_gains,
    mom_rel,
    avg_attn_in,
    avg_attn_out,
    avg_ff_in,
    avg_ff_out,
    avg_table,
    avg_gains,
    avg_rel,
):
    narrow_index = lax.axis_index("narrow")
    column_width = table.shape[1] // lax.axis_size("narrow")
    table_cols = lax.dynamic_slice_in_dim(table, narrow_index * column_width, column_width, 1)
    in_full, out_full, up_full, down_full, table_rows = (
        lax.all_gather(attn_in.astype(jnp.bfloat16), "wide", axis=1, tiled=True),
        lax.all_gather(attn_out.astype(jnp.bfloat16), "wide", axis=2, tiled=True),
        lax.all_gather(ff_in.astype(jnp.bfloat16), "wide", axis=1, tiled=True),
        lax.all_gather(ff_out.astype(jnp.bfloat16), "wide", axis=2, tiled=True),
        lax.all_gather(table_cols.astype(jnp.bfloat16), "wide", axis=0, tiled=True),
    )
    wide_index = lax.axis_index("wide")
    enc_size = enc_ids.shape[2]
    dec_size = tgt_ids.shape[2]
    exd = enc_ids.shape[1]
    heads = out_full.shape[1] // DH
    table_slice = widen(table_rows)
    onehot_buckets = (buckets[:, None] == jnp.arange(rel.shape[1])[None, :]).astype(jnp.float32)
    rel_enc = jnp.dot(onehot_buckets, rel[0], precision=highest)
    rel_dec = jnp.dot(onehot_buckets, rel[1], precision=highest)
    causal = jnp.where(
        jnp.arange(dec_size)[None, :] <= jnp.arange(dec_size)[:, None], 0.0, masked_score
    )
    base_enc, enc_bias_back = jax.vjp(lambda vec: bias_rows(vec, enc_size), rel_enc)
    base_dec, dec_bias_back = jax.vjp(lambda vec: bias_rows(vec, dec_size) + causal[None], rel_dec)
    base_cross = jnp.zeros((heads, dec_size, enc_size), jnp.float32)
    row_weight = (jnp.arange(dec_size)[None, None, :] < tgt_len[:, :, None]).astype(
        jnp.float32
    ) * span_mask.astype(jnp.float32)
    count = jnp.sum(row_weight)
    final_gain = gains[6] * D ** (-0.5)
    grad_in = [jnp.zeros(in_full.shape[1:], jnp.float32) for unused in range(3)]
    grad_out = [jnp.zeros(out_full.shape[1:], jnp.float32) for unused in range(3)]
    grad_up = [jnp.zeros(up_full.shape[1:], jnp.float32) for unused in range(2)]
    grad_down = [jnp.zeros(down_full.shape[1:], jnp.float32) for unused in range(2)]
    gain_grads = [jnp.zeros(gains.shape[1:], jnp.float32) for unused in range(7)]
    grad_table = jnp.zeros(table_rows.shape, jnp.float32)
    rel_enc_grad = jnp.zeros(rel_enc.shape, jnp.float32)
    rel_dec_grad = jnp.zeros(rel_dec.shape, jnp.float32)
    loss_part = jnp.zeros((), jnp.float32)
    lookup_ids = []
    lookup_grads = []
    for micro in range(enc_ids.shape[0]):
        my_enc = enc_ids[micro]
        my_tgt = lax.dynamic_slice_in_dim(tgt_ids[micro], wide_index * exd, exd, 0)
        dec_ids = jnp.concatenate([jnp.zeros((exd, 1), jnp.int32), my_tgt[:, :-1]], axis=1)
        enc_valid = jnp.arange(enc_size)[None, :] < enc_len[micro][:, None]
        dec_valid = jnp.ones((exd, dec_size), bool)
        micro_ids = jnp.concatenate([my_enc.reshape(-1), dec_ids.reshape(-1)])
        embedded = table_rows[micro_ids].astype(jnp.float32)
        enc0 = embedded[: exd * enc_size]
        dec0 = embedded[exd * enc_size :]
        enc1, saved_a = attn_forward(
            enc0, gains[0], in_full[0], out_full[0], None, base_enc, enc_valid
        )
        enc2, saved_b = ff_forward(enc1, gains[1], up_full[0], down_full[0])
        enc_normed, enc_inverse = rms_forward(enc2, gains[2])
        encoded = widen(enc_normed)
        dec1, saved_c = attn_forward(
            dec0, gains[3], in_full[1], out_full[1], None, base_dec, dec_valid
        )
        dec2, saved_d = attn_forward(
            dec1, gains[4], in_full[2], out_full[2], encoded, base_cross, enc_valid
        )
        dec3, saved_e = ff_forward(dec2, gains[5], up_full[1], down_full[1])
        final_normed, final_inverse = rms_forward(dec3, final_gain)
        final_full = widen(final_normed)
        quarter = final_full.shape[0] // lax.axis_size("narrow")
        my_rows = lax.dynamic_slice_in_dim(final_full, narrow_index * quarter, quarter, 0)
        micro_targets = tgt_ids[micro]
        micro_weights = row_weight[micro]
        own_targets = lax.dynamic_index_in_dim(micro_targets, wide_index, 0, keepdims=False)
        own_weights = lax.dynamic_index_in_dim(micro_weights, wide_index, 0, keepdims=False)
        targets = lax.dynamic_slice_in_dim(own_targets, narrow_index * quarter, quarter, 0)
        weights_now = lax.dynamic_slice_in_dim(own_weights, narrow_index * quarter, quarter, 0)
        logits = matmul(my_rows, table_slice.T)
        vocab_ids = jnp.arange(table_slice.shape[0])
        top = jnp.max(logits, axis=-1)
        log_total = top + jnp.log(jnp.sum(jnp.exp(logits - top[:, None]), axis=-1))
        target_hot = (vocab_ids[None, :] == targets[:, None]).astype(jnp.float32)
        hits = jnp.sum(target_hot * logits, axis=-1)
        loss_part = loss_part + jnp.sum(weights_now * (log_total - hits))
        logit_grad = (
            (weights_now / count)[:, None] * (jnp.exp(logits - log_total[:, None]) - target_hot)
        ).astype(jnp.bfloat16)
        rows_grad = matmul(logit_grad, table_slice)
        grad_table = grad_table + narrow_grad(outer_rows(logit_grad, my_rows))
        placed = lax.dynamic_update_slice_in_dim(
            jnp.zeros(final_full.shape, jnp.float32), rows_grad, narrow_index * quarter, 0
        )
        final_grad = to_low(narrow_grad(placed))
        dec_grad, gain_raw = rms_backward(dec3, final_gain, final_inverse, final_grad)
        gain_grads[6] = gain_grads[6] + gain_raw * D ** (-0.5)
        dec_grad, gain_now, in_now, out_now = ff_backward(
            saved_e, dec_grad, gains[5], up_full[1], down_full[1]
        )
        gain_grads[5] = gain_grads[5] + gain_now
        grad_up[1] = grad_up[1] + in_now
        grad_down[1] = grad_down[1] + out_now
        dec_grad, gain_now, in_now, out_now, unused, source_grad = attn_backward(
            saved_d, dec_grad, gains[4], in_full[2], out_full[2], encoded, base_cross, enc_valid
        )
        gain_grads[4] = gain_grads[4] + gain_now
        grad_in[2] = grad_in[2] + in_now
        grad_out[2] = grad_out[2] + out_now
        dec_grad, gain_now, in_now, out_now, bias_now, unused = attn_backward(
            saved_c, dec_grad, gains[3], in_full[1], out_full[1], None, base_dec, dec_valid
        )
        gain_grads[3] = gain_grads[3] + gain_now
        grad_in[1] = grad_in[1] + in_now
        grad_out[1] = grad_out[1] + out_now
        rel_dec_grad = rel_dec_grad + dec_bias_back(bias_now)[0]
        enc_grad, gain_now = rms_backward(
            enc2, gains[2], enc_inverse, to_low(narrow_grad(source_grad))
        )
        gain_grads[2] = gain_grads[2] + gain_now
        enc_grad, gain_now, in_now, out_now = ff_backward(
            saved_b, enc_grad, gains[1], up_full[0], down_full[0]
        )
        gain_grads[1] = gain_grads[1] + gain_now
        grad_up[0] = grad_up[0] + in_now
        grad_down[0] = grad_down[0] + out_now
        enc_grad, gain_now, in_now, out_now, bias_now, unused = attn_backward(
            saved_a, enc_grad, gains[0], in_full[0], out_full[0], None, base_enc, enc_valid
        )
        gain_grads[0] = gain_grads[0] + gain_now
        grad_in[0] = grad_in[0] + in_now
        grad_out[0] = grad_out[0] + out_now
        rel_enc_grad = rel_enc_grad + enc_bias_back(bias_now)[0]
        lookup_ids.append(micro_ids)
        lookup_grads.append(jnp.concatenate([enc_grad, dec_grad], axis=0))
    grad_table = grad_table.at[jnp.concatenate(lookup_ids)].add(
        jnp.concatenate(lookup_grads, axis=0)
    )
    rel_grad = jnp.stack(
        [
            jnp.dot(onehot_buckets.T, rel_enc_grad, precision=highest),
            jnp.dot(onehot_buckets.T, rel_dec_grad, precision=highest),
        ]
    )
    reduced = (
        lax.psum_scatter(jnp.stack(grad_in), "wide", scatter_dimension=1, tiled=True),
        lax.psum_scatter(jnp.stack(grad_out), "wide", scatter_dimension=2, tiled=True),
        lax.psum_scatter(jnp.stack(grad_up), "wide", scatter_dimension=1, tiled=True),
        lax.psum_scatter(jnp.stack(grad_down), "wide", scatter_dimension=2, tiled=True),
        lax.psum_scatter(grad_table, "wide", scatter_dimension=0, tiled=True),
    )
    gain_total, rel_total = lax.psum((jnp.stack(gain_grads), rel_grad), "wide")
    table_part = reduced[4]
    owner = (wide_index == 0).astype(jnp.float32)
    squares = sum((jnp.sum(grad * grad) for grad in reduced[:4])) + jnp.sum(table_part * table_part)
    squares = squares + owner * (jnp.sum(gain_total * gain_total) + jnp.sum(rel_total * rel_total))
    square_sum, loss_sum = lax.psum((squares, loss_part), ("wide", "narrow"))
    table_grad = lax.all_gather(
        table_part.astype(jnp.bfloat16), "narrow", axis=1, tiled=True
    ).astype(table_part.dtype)
    grads = (reduced[0], reduced[1], reduced[2], reduced[3], table_grad, gain_total, rel_total)
    norm = jnp.sqrt(square_sum)
    scale = jnp.minimum(1.0, clip_norm / norm)
    base_rate = math.sqrt(PARAMS) / (3.0 * clip_norm)
    matrix_rate = base_rate / math.sqrt(D)
    rates = (
        matrix_rate,
        16.0 * matrix_rate,
        matrix_rate,
        matrix_rate,
        base_rate,
        0.3 * base_rate,
        0.3 * base_rate,
    )
    params = (attn_in, attn_out, ff_in, ff_out, table, gains, rel)
    moms = (mom_attn_in, mom_attn_out, mom_ff_in, mom_ff_out, mom_table, mom_gains, mom_rel)
    avgs = (avg_attn_in, avg_attn_out, avg_ff_in, avg_ff_out, avg_table, avg_gains, avg_rel)
    fresh, scaled_grads, averages = ([], [], [])
    for index in range(7):
        clipped = grads[index] * scale
        moment = momentum_decay * moms[index] + clipped
        weight = params[index] - rates[index] * (clipped + momentum_decay * moment)
        fresh.append(weight)
        scaled_grads.append(clipped)
        averages.append(average_decay * avgs[index] + (1.0 - average_decay) * weight)
    return (
        loss_sum,
        count,
        norm,
        fresh[0],
        fresh[1],
        fresh[2],
        fresh[3],
        fresh[4],
        fresh[5],
        fresh[6],
        scaled_grads[0],
        scaled_grads[1],
        scaled_grads[2],
        scaled_grads[3],
        scaled_grads[4],
        scaled_grads[5],
        scaled_grads[6],
        averages[0],
        averages[1],
        averages[2],
        averages[3],
        averages[4],
        averages[5],
        averages[6],
    )


def solution(mesh):
    in_specs = (
        P(None, "wide", None),
        P(None, "wide"),
        P(),
        P(),
        P(),
        P(),
        P(None, "wide", "narrow"),
        P(None, "narrow", "wide"),
        P(None, "wide", "narrow"),
        P(None, "narrow", "wide"),
        P("wide", None),
        P(None, "narrow"),
        P(None, None, "narrow"),
        P(None, "wide", "narrow"),
        P(None, "narrow", "wide"),
        P(None, "wide", "narrow"),
        P(None, "narrow", "wide"),
        P("wide", None),
        P(None, "narrow"),
        P(None, None, "narrow"),
        P(None, "wide", "narrow"),
        P(None, "narrow", "wide"),
        P(None, "wide", "narrow"),
        P(None, "narrow", "wide"),
        P("wide", None),
        P(None, "narrow"),
        P(None, None, "narrow"),
    )
    out_specs = (
        P(),
        P(),
        P(),
        P(None, "wide", "narrow"),
        P(None, "narrow", "wide"),
        P(None, "wide", "narrow"),
        P(None, "narrow", "wide"),
        P("wide", None),
        P(None, "narrow"),
        P(None, None, "narrow"),
        P(None, "wide", "narrow"),
        P(None, "narrow", "wide"),
        P(None, "wide", "narrow"),
        P(None, "narrow", "wide"),
        P("wide", None),
        P(None, "narrow"),
        P(None, None, "narrow"),
        P(None, "wide", "narrow"),
        P(None, "narrow", "wide"),
        P(None, "wide", "narrow"),
        P(None, "narrow", "wide"),
        P("wide", None),
        P(None, "narrow"),
        P(None, None, "narrow"),
    )
    return jax.shard_map(body, mesh=mesh, in_specs=in_specs, out_specs=out_specs, check_vma=False)
```

profile of v0, /device:TPU:0, one launch (start us, length us, event | category | flops | bytes accessed | tf_op | source)
XLA Modules:
  0.0 4531.8 jit_solution(3059359087718801745)
XLA Ops:
  97.2 105.4 %all-gather.48.cloned.1.call-done = bf16[8,4016,192]{1,2,0:T(8,128)(2,1)} async-done(((bf16[1,4016,192]{1,2,0:T(8,128)(2,1)}), bf16[8,4016,192]{1,2,0:T(8,128)(2,1)}) %all-gather.48.cloned.1.call-update) | async-done | bytes 12337168 | tf_op jit(solution)/shard_map/all_gather | solution.py:238
  254.2 467.0 %while.3 = (u32[]{:T(128)}, f32[1,3,2096128]{2,1,0:T(4,128)}, f32[6288384]{0:T(1024)}, u32[]{}, f32[]{:T(128)}, /*index=5*/u32[]{}, u32[]{}, u32[]{}) while((u32[]{:T(128)}, f32[1,3,2096128]{2,1,0:T(4,128)}, f32[6288384]{0:T(1024)}, u32[]{}, f32[]{:T(128)}, /*index=5*/u32[]{}, u32[]{}, u32[]{}) %tuple.148), condition=%wide.cond, body=%wide.body.sunk | while | flops 9 | bytes 33538248
  254.7 83.9 %dynamic-slice_reduce_fusion.2 = f32[2096128]{0:T(1024)} fusion(f32[]{:T(128)} %broadcast.653, f32[1,3,2096128]{2,1,0:T(4,128)} %get-tuple-element.480, u32[]{:T(128)S(6)} %multiply.64, u32[]{:T(128)S(6)} %multiply.65), kind=kLoop, calls=%fused_computation.680.clone.1 | loop fusion | bytes 16769036
  338.6 71.3 %dynamic-update-slice.6 = f32[6288384]{0:T(1024)} dynamic-update-slice(f32[6288384]{0:T(1024)} %get-tuple-element.473, f32[2096128]{0:T(1024)} %dynamic-slice_reduce_fusion.2, u32[]{:T(128)S(6)} %add.1236) | dynamic-update-slice | bytes 16769028
  410.4 83.9 %dynamic-slice_reduce_fusion.2 = f32[2096128]{0:T(1024)} fusion(f32[]{:T(128)} %broadcast.653, f32[1,3,2096128]{2,1,0:T(4,128)} %get-tuple-element.480, u32[]{:T(128)S(6)} %multiply.64, u32[]{:T(128)S(6)} %multiply.65), kind=kLoop, calls=%fused_computation.680.clone.1 | loop fusion | bytes 16769036
  494.3 71.2 %dynamic-update-slice.6 = f32[6288384]{0:T(1024)} dynamic-update-slice(f32[6288384]{0:T(1024)} %get-tuple-element.473, f32[2096128]{0:T(1024)} %dynamic-slice_reduce_fusion.2, u32[]{:T(128)S(6)} %add.1236) | dynamic-update-slice | bytes 16769028
  566.0 83.9 %dynamic-slice_reduce_fusion.2 = f32[2096128]{0:T(1024)} fusion(f32[]{:T(128)} %broadcast.653, f32[1,3,2096128]{2,1,0:T(4,128)} %get-tuple-element.480, u32[]{:T(128)S(6)} %multiply.64, u32[]{:T(128)S(6)} %multiply.65), kind=kLoop, calls=%fused_computation.680.clone.1 | loop fusion | bytes 16769036
  649.9 71.2 %dynamic-update-slice.6 = f32[6288384]{0:T(1024)} dynamic-update-slice(f32[6288384]{0:T(1024)} %get-tuple-element.473, f32[2096128]{0:T(1024)} %dynamic-slice_reduce_fusion.2, u32[]{:T(128)S(6)} %add.1236) | dynamic-update-slice | bytes 16769028
  721.1 37.4 reshape.1570
  783.3 36.4 all_gather.96
  885.1 39.9 reduce-scatter.48.cloned.1.call-done
  1004.9 49.9 %all-gather.26.cloned.1.call-done = bf16[2,768,768]{1,2,0:T(8,128)(2,1)} async-done(((bf16[2,768,96]{1,2,0:T(8,128)(2,1)}), bf16[2,768,768]{1,2,0:T(8,128)(2,1)}) %all-gather.26.cloned.1.call-update) | async-done | bytes 2359312 | tf_op jit(solution)/shard_map/all_gather | solution.py:237
  1128.3 39.4 reduce-scatter.40.cloned.1.call-done
  1169.0 39.8 reduce-scatter.50.cloned.1.call-done
  1414.1 270.7 %all-gather.30.cloned.1.call-done = bf16[32128,768]{0,1:T(8,128)(2,1)} async-done(((bf16[32128,192]{0,1:T(8,128)(2,1)}), bf16[32128,768]{0,1:T(8,128)(2,1)}) %all-gather.30.cloned.1.call-update) | async-done | bytes 49348624 | tf_op jit(solution)/shard_map/all_gather | solution.py:50
  1951.2 38.6 reduce-scatter.60.cloned.1.call-done
  2099.4 37.8 reduce-scatter.70.cloned.1.call-done
  2138.4 39.3 reduce-scatter.62.cloned.1.call-done
  2260.6 37.9 fusion.258
  2333.4 69.0 %convolution_add_fusion = f32[32128,768]{0,1:T(8,128)} fusion(f32[32128,768]{0,1:T(8,128)} %fusion.258, bf16[256,768]{0,1:T(8,128)(2,1)S(1)} %copy-done.142, s32[]{:T(128)S(6)} %select_n.98, f32[64,32128]{1,0:T(8,128)} %copy-done.2, f32[64]{0:T(128)S(1)} %copy-done.255, f32[64]{0:T(128)S(1)} %copy-done.257, s32[64]{0:T(128)S(1)} %copy-done.230), kind=kOutput, calls=%fused_computation.3 | convolution fusion | flops 3195322368 | bytes 205817344 | tf_op jit(solution)/shard_map/dot_general | solution.py:31
  2456.8 603.0 %reduce-scatter.86.cloned.1.call-done = f32[32128,192]{0,1:T(8,128)} async-done(((f32[32128,768]{0,1:T(8,128)}), f32[32128,192]{0,1:T(8,128)}) %reduce-scatter.86.cloned.1.call-update) | async-done | bytes 24674320 | tf_op jit(solution)/shard_map/reduce_scatter | solution.py:62
  3087.9 35.8 scatter_fusion
  3161.0 72.5 %all-reduce.35.cloned.1.call-done = f32[2,768,768]{1,0,2:T(2,128)} async-done(((f32[2,768,768]{1,0,2:T(2,128)}), f32[2,768,768]{1,0,2:T(2,128)}) %all-reduce.35.cloned.1.call-update) | async-done | bytes 4718608
  3327.5 446.9 %while.4 = (u32[]{:T(128)}, bf16[6288384]{0:T(1024)(128)(2,1)}, bf16[1,3,2096128]{2,1,0:T(4,128)(2,1)}, u32[]{}, u32[]{}, /*index=5*/u32[]{}, u32[]{}, u32[]{}) while((u32[]{:T(128)}, bf16[6288384]{0:T(1024)(128)(2,1)}, bf16[1,3,2096128]{2,1,0:T(4,128)(2,1)}, u32[]{}, u32[]{}, /*index=5*/u32[]{}, u32[]{}, u32[]{}) %tuple.151), condition=%wide.cond.1, body=%wide.body.1.sunk | while | flops 9 | bytes 25153720
  3336.4 139.9 %dynamic-update-slice.7 = bf16[1,3,2096128]{2,1,0:T(4,128)(2,1)} dynamic-update-slice(bf16[1,3,2096128]{2,1,0:T(4,128)(2,1)} %get-tuple-element.497, bf16[1,1,2096128]{2,1,0:T(2,128)(2,1)} %reshape.1681, u32[]{:T(128)S(6)} %multiply.68, u32[]{:T(128)S(6)} %multiply.70, u32[]{} %constant.661..sunk) | dynamic-update-slice | bytes 8384516
  3485.5 139.9 %dynamic-update-slice.7 = bf16[1,3,2096128]{2,1,0:T(4,128)(2,1)} dynamic-update-slice(bf16[1,3,2096128]{2,1,0:T(4,128)(2,1)} %get-tuple-element.497, bf16[1,1,2096128]{2,1,0:T(2,128)(2,1)} %reshape.1681, u32[]{:T(128)S(6)} %multiply.68, u32[]{:T(128)S(6)} %multiply.70, u32[]{} %constant.661..sunk) | dynamic-update-slice | bytes 8384516
  3634.5 139.8 %dynamic-update-slice.7 = bf16[1,3,2096128]{2,1,0:T(4,128)(2,1)} dynamic-update-slice(bf16[1,3,2096128]{2,1,0:T(4,128)(2,1)} %get-tuple-element.497, bf16[1,1,2096128]{2,1,0:T(2,128)(2,1)} %reshape.1681, u32[]{:T(128)S(6)} %multiply.68, u32[]{:T(128)S(6)} %multiply.70, u32[]{} %constant.661..sunk) | dynamic-update-slice | bytes 8384516
  3831.0 445.8 %while.5 = (u32[]{:T(128)}, bf16[6288384]{0:T(1024)(128)(2,1)}, bf16[1,3,2096128]{2,1,0:T(4,128)(2,1)}, u32[]{}, u32[]{}, /*index=5*/u32[]{}, u32[]{}, u32[]{}) while((u32[]{:T(128)}, bf16[6288384]{0:T(1024)(128)(2,1)}, bf16[1,3,2096128]{2,1,0:T(4,128)(2,1)}, u32[]{}, u32[]{}, /*index=5*/u32[]{}, u32[]{}, u32[]{}) %tuple.154), condition=%wide.cond.2, body=%wide.body.2.sunk | while | flops 9 | bytes 25153720
  3839.9 139.8 %dynamic-update-slice.8 = bf16[1,3,2096128]{2,1,0:T(4,128)(2,1)} dynamic-update-slice(bf16[1,3,2096128]{2,1,0:T(4,128)(2,1)} %get-tuple-element.521, bf16[1,1,2096128]{2,1,0:T(2,128)(2,1)} %reshape.1682, u32[]{:T(128)S(6)} %multiply.72, u32[]{:T(128)S(6)} %multiply.74, u32[]{} %constant.661..sunk.1) | dynamic-update-slice | bytes 8384516
  3988.5 139.8 %dynamic-update-slice.8 = bf16[1,3,2096128]{2,1,0:T(4,128)(2,1)} dynamic-update-slice(bf16[1,3,2096128]{2,1,0:T(4,128)(2,1)} %get-tuple-element.521, bf16[1,1,2096128]{2,1,0:T(2,128)(2,1)} %reshape.1682, u32[]{:T(128)S(6)} %multiply.72, u32[]{:T(128)S(6)} %multiply.74, u32[]{} %constant.661..sunk.1) | dynamic-update-slice | bytes 8384516
  4137.1 139.7 %dynamic-update-slice.8 = bf16[1,3,2096128]{2,1,0:T(4,128)(2,1)} dynamic-update-slice(bf16[1,3,2096128]{2,1,0:T(4,128)(2,1)} %get-tuple-element.521, bf16[1,1,2096128]{2,1,0:T(2,128)(2,1)} %reshape.1682, u32[]{:T(128)S(6)} %multiply.72, u32[]{:T(128)S(6)} %multiply.74, u32[]{} %constant.661..sunk.1) | dynamic-update-slice | bytes 8384516
  4400.3 37.0 all-reduce.21
  (1209 shorter events, 1610.6 us)
Async XLA Ops:
  7.2 195.4 %all-gather.48.cloned.1.call-start = ((), (), s32[]{:S(2)}) async-start(), calls=%async_computation.70 | async-start | bytes 14155776 | tf_op jit(solution)/shard_map/all_gather | solution.py:238
  23.3 800.8 %all-gather.18.cloned.1.call-start = ((), (), s32[]{:S(2)}) async-start(), calls=%async_computation.29 | async-start | bytes 3317760 | tf_op jit(solution)/shard_map/all_gather | solution.py:234
  24.1 800.0 %all-gather.20.cloned.1.call-start = ((), (), s32[]{:S(2)}) async-start(), calls=%async_computation.31 | async-start | bytes 1966080 | tf_op jit(solution)/shard_map/all_gather | solution.py:50
  253.6 590.8 %all-gather.32.cloned.1.call-start = ((), (), s32[]{:S(2)}) async-start(), calls=%async_computation.42 | async-start | bytes 1966080 | tf_op jit(solution)/shard_map/all_gather | solution.py:50
  864.2 121.9 %all-gather.24.cloned.1.call-start = ((), (), s32[]{:S(2)}) async-start(), calls=%async_computation.34 | async-start | bytes 2654208 | tf_op jit(solution)/shard_map/all_gather | solution.py:236
  865.0 135.0 %all-gather.22.cloned.1.call-start = ((), (), s32[]{:S(2)}) async-start(), calls=%async_computation.33 | async-start | bytes 1966080 | tf_op jit(solution)/shard_map/all_gather | solution.py:50
  940.7 114.1 %all-gather.26.cloned.1.call-start = ((), (), s32[]{:S(2)}) async-start(), calls=%async_computation.35 | async-start | bytes 2654208 | tf_op jit(solution)/shard_map/all_gather | solution.py:237
  942.6 132.5 %all-gather.34.cloned.1.call-start = ((), (), s32[]{:S(2)}) async-start(), calls=%async_computation.44 | async-start | bytes 1966080 | tf_op jit(solution)/shard_map/all_gather | solution.py:50
  944.2 156.6 %reduce-scatter.46.cloned.1.call-start = ((), (), s32[]{:S(2)}) async-start(), calls=%async_computation.41 | async-start | bytes 983040 | tf_op jit(solution)/shard_map/reduce_scatter | solution.py:54
  972.3 154.4 %reduce-scatter.36.cloned.1.call-start = ((), (), s32[]{:S(2)}) async-start(), calls=%async_computation.30 | async-start | bytes 983040 | tf_op jit(solution)/shard_map/reduce_scatter | solution.py:54
  986.1 181.7 %reduce-scatter.40.cloned.1.call-start = ((), (), s32[]{:S(2)}) async-start(), calls=%async_computation.36 | async-start | bytes 3932160 | tf_op jit(solution)/shard_map/reduce_scatter | solution.py:54
  1060.2 148.6 %reduce-scatter.50.cloned.1.call-start = ((), (), s32[]{:S(2)}) async-start(), calls=%async_computation.45 | async-start | bytes 3932160 | tf_op jit(solution)/shard_map/reduce_scatter | solution.py:54
  1083.3 163.0 %all-gather.36.cloned.1.call-start = ((), (), s32[]{:S(2)}) async-start(), calls=%async_computation.46 | async-start | bytes 1966080 | tf_op jit(solution)/shard_map/all_gather | solution.py:50
  1273.9 100.4 %reduce-scatter.54.cloned.1.call-start = ((), (), s32[]{:S(2)}) async-start(), calls=%async_computation.48 | async-start | bytes 983040 | tf_op jit(solution)/shard_map/reduce_scatter | solution.py:54
  1354.0 330.7 %all-gather.30.cloned.1.call-start = ((), (), s32[]{:S(2)}) async-start(), calls=%async_computation.40 | async-start | bytes 61685760 | tf_op jit(solution)/shard_map/all_gather | solution.py:50
  1372.8 407.3 %reduce-scatter.64.cloned.1.call-start = ((), (), s32[]{:S(2)}) async-start(), calls=%async_computation.55 | async-start | bytes 983040 | tf_op jit(solution)/shard_map/reduce_scatter | solution.py:62
  1842.8 106.5 %reduce-scatter.68.cloned.1.call-start = ((), (), s32[]{:S(2)}) async-start(), calls=%async_computation.57 | async-start | bytes 3932160 | tf_op jit(solution)/shard_map/reduce_scatter | solution.py:62
  2010.6 126.6 %reduce-scatter.70.cloned.1.call-start = ((), (), s32[]{:S(2)}) async-start(), calls=%async_computation.59 | async-start | bytes 3932160 | tf_op jit(solution)/shard_map/reduce_scatter | solution.py:62
  2033.1 144.7 %reduce-scatter.62.cloned.1.call-start = ((), (), s32[]{:S(2)}) async-start(), calls=%async_computation.53 | async-start | bytes 3932160 | tf_op jit(solution)/shard_map/reduce_scatter | solution.py:62
  2054.4 172.2 %all-gather.40.cloned.1.call-start = ((), (), s32[]{:S(2)}) async-start(), calls=%async_computation.54 | async-start | bytes 1966080 | tf_op jit(solution)/shard_map/all_gather | solution.py:58
  2196.4 102.0 %all-gather.44.cloned.1.call-start = ((), (), s32[]{:S(2)}) async-start(), calls=%async_computation.60 | async-start | bytes 1966080 | tf_op jit(solution)/shard_map/all_gather | solution.py:58
  2200.7 224.6 %reduce-scatter.84.cloned.1.call-start = ((), (), s32[]{:S(2)}) async-start(), calls=%async_computation.67 | async-start | bytes 983040 | tf_op jit(solution)/shard_map/reduce_scatter | solution.py:62
  2222.3 204.0 %reduce-scatter.80.cloned.1.call-start = ((), (), s32[]{:S(2)}) async-start(), calls=%async_computation.65 | async-start | bytes 983040 | tf_op jit(solution)/shard_map/reduce_scatter | solution.py:62
  2226.5 201.6 %reduce-scatter.78.cloned.1.call-start = ((), (), s32[]{:S(2)}) async-start(), calls=%async_computation.64 | async-start | bytes 3932160 | tf_op jit(solution)/shard_map/reduce_scatter | solution.py:62
  2259.6 170.0 %reduce-scatter.82.cloned.1.call-start = ((), (), s32[]{:S(2)}) async-start(), calls=%async_computation.66 | async-start | bytes 3932160 | tf_op jit(solution)/shard_map/reduce_scatter | solution.py:62
  2332.4 727.4 %reduce-scatter.86.cloned.1.call-start = ((), (), s32[]{:S(2)}) async-start(), calls=%async_computation.69 | async-start | bytes 123371520 | tf_op jit(solution)/shard_map/reduce_scatter | solution.py:62
  2402.5 831.1 %all-reduce.35.cloned.1.call-start = ((), (), s32[]{:S(2)}) async-start(), calls=%async_computation.74 | async-start | bytes 9437184
  2424.1 1852.7 %reduce-scatter.92.cloned.1.call-start = ((), (), s32[]{:S(2)}) async-start(), calls=%async_computation.73 | async-start | bytes 37011456
  3123.8 1217.0 %reduce-scatter.76.cloned.1.call-start = ((), (), s32[]{:S(2)}) async-start(), calls=%async_computation.63 | async-start | bytes 5308416 | tf_op jit(solution)/shard_map/reduce_scatter | solution.py:372
  3160.5 1182.1 %reduce-scatter.90.cloned.1.call-start = ((), (), s32[]{:S(2)}) async-start(), calls=%async_computation.72 | async-start | bytes 2211840
  3254.9 1126.6 %reduce-scatter.88.cloned.1.call-start = ((), (), s32[]{:S(2)}) async-start(), calls=%async_computation.71 | async-start | bytes 6193152
  3774.4 683.3 %all-gather.46.cloned.1.call-start = ((), (), s32[]{:S(2)}) async-start(), calls=%async_computation.68 | async-start | bytes 7864320 | tf_op jit(solution)/shard_map/all_gather | solution.py:382
  (343 other events, 10969.6 us)
Sparse Core Ops, SparseCore 0:
  23.4 179.1 all-gather.47
  205.3 56.5 all-gather.17
  845.9 37.9 reduce-scatter.37
  887.0 37.9 reduce-scatter.47
  927.7 51.9 all-gather.23
  1002.8 51.9 all-gather.25
  1103.4 23.2 reduce-scatter.35
  1129.8 37.9 reduce-scatter.39
  1170.9 37.9 reduce-scatter.49
  1222.3 23.4 all-gather.35
  1296.9 23.2 reduce-scatter.41
  1341.2 23.9 reduce-scatter.53
  1393.2 291.5 all-gather.29
  1732.1 23.5 reduce-scatter.63
  1780.1 23.9 reduce-scatter.55
  1829.3 23.9 reduce-scatter.65
  1856.0 23.2 reduce-scatter.57
  1910.6 38.6 reduce-scatter.67
  1951.8 37.9 reduce-scatter.59
  2099.2 37.9 reduce-scatter.69
  2139.8 37.9 reduce-scatter.61
  2243.8 23.2 reduce-scatter.83
  2269.7 23.2 reduce-scatter.79
  2295.5 37.9 reduce-scatter.77
  2336.1 37.9 reduce-scatter.81
  2402.6 657.1 reduce-scatter.85
  3063.8 169.6 all-reduce.34
  3237.7 527.6 reduce-scatter.91
  3769.4 94.3 reduce-scatter.75
  3867.6 66.4 reduce-scatter.89
  3937.6 105.1 reduce-scatter.87
  4283.1 44.5 all-gather.45
  (14 shorter events, 291.7 us)
where the time goes:
time: 4620 us; the launch traced here: 4530 us
  local copies, waits for them, and re-layouts  1890 us (41%)
  waiting for transfers between devices  1640 us (35%)
  matrix products  356 us (8%)
  other arithmetic  325 us (7%)
  blocking collectives  290 us (6%)
    unnamed x727, local copies, waits for them, and re-layouts  1710 us
    reduce_scatter x15, waiting for transfers between devices, narrow_grad(): lax.psum_scatter(partial_value, 'narrow', scatter_dimension=1, tiled=True)  838 us
    all_gather x7, waiting for transfers between devices, widen(): lax.all_gather(values.astype(jnp.bfloat16), 'narrow', axis=1, tiled=True)  315 us
    reduce_scatter x10, waiting for transfers between devices, narrow_sum(): lax.psum_scatter(partial_value, 'narrow', scatter_dimension=1, tiled=True)  238 us
    dot_general x48, matrix products, matmul(): return jnp.dot(left, right, preferred_element_type=jnp.float32)  172 us
    dot_general x24, matrix products, outer_rows(): lax.dot_general(left, right, contract_rows, preferred_element_type=jnp.fl...  129 us
    all_gather x1, waiting for transfers between devices, body(): lax.all_gather(table_cols.astype(jnp.bfloat16), 'wide', axis=0, tiled=True)  105 us
  transfers between devices with their start and end apart: 46, of which 28 were waited for; matrix products, arithmetic and copies ran while one was open for 52% of the time, Pallas kernels for 0%

commit v1 on v0

v1 whole, which is shorter than its diff:
```python
import functools
import math

import jax
import jax.numpy as jnp
from jax import lax
from jax.experimental import pallas as pl
from jax.experimental.pallas import tpu as pltpu
from jax.sharding import PartitionSpec as P

DH = 64
PARAMS = 41195520

epsilon = 1e-06
masked_score = -1000000000.0
momentum_decay = 0.9
average_decay = 0.9
clip_norm = 0.02
highest = lax.Precision.HIGHEST
bf16 = jnp.bfloat16
f32 = jnp.float32
CHUNK = 256


def dot(left, right, left_dim, right_dim):
    return lax.dot_general(
        left, right, (((left_dim,), (right_dim,)), ((), ())), preferred_element_type=f32
    )


def hop(values, axis, bit):
    size = lax.axis_size(axis)
    return lax.ppermute(values, axis, [(i, i ^ bit) for i in range(size)])


def swap(values):
    return hop(values, "narrow", 1)


def bits_down(axis):
    bit = lax.axis_size(axis) // 2
    while bit:
        yield bit
        bit //= 2


def bits_up(axis):
    return reversed(list(bits_down(axis)))


def gather_sorted(values, axis):
    index = lax.axis_index(axis)
    values = values[None]
    for bit in bits_down(axis):
        other = hop(values, axis, bit)
        upper = (index & bit) != 0
        values = jnp.stack(
            [jnp.where(upper, other, values), jnp.where(upper, values, other)], axis=1
        ).reshape(-1, *values.shape[1:])
    return values


def scatter_sorted(values, axis):
    index = lax.axis_index(axis)
    for bit in bits_up(axis):
        pairs = values.reshape(-1, 2, *values.shape[1:])
        mine = jnp.where((index & bit) != 0, 1, 0)
        kept = lax.dynamic_index_in_dim(pairs, mine, 1, keepdims=False)
        sent = lax.dynamic_index_in_dim(pairs, 1 - mine, 1, keepdims=False)
        other = hop(sent.astype(bf16), axis, bit)
        values = kept.astype(f32) + other.astype(f32)
        if values.shape[0] > 1:
            values = values.astype(bf16)
    return values[0]


def scatter_relative(values, axis, dtype):
    for bit in bits_up(axis):
        pairs = values.reshape(-1, 2, *values.shape[1:])
        other = hop(pairs[:, 1].astype(bf16), axis, bit)
        values = pairs[:, 0].astype(dtype) + other.astype(dtype)
    return values[0]


def gather_relative(values, axis):
    values = values[None]
    for bit in bits_down(axis):
        values = jnp.stack([values, hop(values, axis, bit)], axis=1)
        values = values.reshape(-1, *values.shape[2:])
    return values


def gather_direct(values, axis):
    size = lax.axis_size(axis)
    if size > 8:
        return gather_relative(values, axis)
    return jnp.stack([values] + [hop(values, axis, r) for r in range(1, size)])


def bias_strip(rel_row, base, width):
    length = rel_row.shape[1]
    row = pltpu.roll(jnp.broadcast_to(rel_row, (8, length)), length - base, 1)[:1]
    rows = jnp.broadcast_to(row, (128, length))
    return pltpu.roll(rows, 0, 1, stride=1, stride_axis=0)[:, :width]


def part_scores(keys, queries_h, strip, col, part, core, key_len, causal):
    scores = dot(keys, queries_h, 1, 1)
    rows, cols = scores.shape
    blocks = rows // 128
    if strip is not None:
        shifts = [(blocks - 1 - j) * 128 + col for j in range(blocks)]
        bias = jnp.concatenate([strip[:, s : s + cols] for s in shifts], axis=0)
        scores = scores + bias
    where_core = core if part == 0 else 1 - core
    key_at = where_core * rows + lax.broadcasted_iota(jnp.int32, (rows, 1), 0)
    if causal:
        query_at = lax.broadcasted_iota(jnp.int32, (1, cols), 1) + col + causal * core
        return jnp.where(key_at <= query_at, scores, masked_score)
    return jnp.where(key_at < key_len, scores, masked_score)


def bases_of(size, rows, core, centre):
    own = centre - (rows // 128 - 1) * 128
    other = own - rows + core * (2 * rows)
    return own, other


def forward_kernel(has_bias, causal, centre, scal, q_ref, kvo_ref, kvt_ref, *rest):
    if has_bias:
        rel_ref, mixed_ref, lse_ref, so_ref, st_ref = rest
    else:
        mixed_ref, lse_ref = rest
    core, key_len, head = scal[0], scal[1], pl.program_id(1)
    q_rows, k_rows = q_ref.shape[1], kvo_ref.shape[1]
    lanes = q_ref.shape[2]
    lane_mask = lax.broadcasted_iota(jnp.int32, (1, lanes), 1) // DH == head
    if has_bias:
        own, other = bases_of(lanes, k_rows, core, centre)
        so_ref[...] = bias_strip(rel_ref[0], own, so_ref.shape[1])
        st_ref[...] = bias_strip(rel_ref[0], other, st_ref.shape[1])
    step = min(CHUNK, q_rows)
    for col in range(0, q_rows, step):
        queries = jnp.where(lane_mask, q_ref[0, col : col + step, :], 0.0).astype(bf16)
        own_s = part_scores(
            kvo_ref[0, :, :lanes], queries, so_ref if has_bias else None,
            col, 0, core, key_len, causal,
        )
        oth_s = part_scores(
            kvt_ref[0, :, :lanes], queries, st_ref if has_bias else None,
            col, 1, core, key_len, causal,
        )
        top = jnp.maximum(
            jnp.max(own_s, axis=0, keepdims=True), jnp.max(oth_s, axis=0, keepdims=True)
        )
        own_e, oth_e = jnp.exp(own_s - top), jnp.exp(oth_s - top)
        total = jnp.sum(own_e, axis=0, keepdims=True) + jnp.sum(oth_e, axis=0, keepdims=True)
        inverse = 1.0 / total
        mixed = dot(kvo_ref[0, :, lanes:], (own_e * inverse).astype(bf16), 0, 0)
        mixed = mixed + dot(kvt_ref[0, :, lanes:], (oth_e * inverse).astype(bf16), 0, 0)
        mixed = mixed.T.astype(bf16)
        mixed_ref[0, col : col + step, :] = jnp.where(
            lane_mask, mixed, mixed_ref[0, col : col + step, :]
        )
        lse_ref[0, 0, :, col : col + step] = top + jnp.log(total)


def turned(i, j):
    return (i + 1 - 2 * (i % 2), 0, 0)


def attend(scal, q, kvo, kvt, rel_rows, centre, causal):
    groups, q_rows, lanes = q.shape
    k_rows = kvo.shape[1]
    heads = lanes // DH
    has_bias = rel_rows is not None
    width = q_rows + (k_rows // 128 - 1) * 128
    in_specs = [
        pl.BlockSpec(memory_space=pltpu.SMEM),
        pl.BlockSpec((1, q_rows, lanes), lambda i, j: (i, 0, 0)),
        pl.BlockSpec((1, k_rows, 2 * lanes), lambda i, j: (i, 0, 0)),
        pl.BlockSpec((1, k_rows, 2 * lanes), turned),
    ]
    args = [scal, q, kvo, kvt]
    scratch = []
    if has_bias:
        in_specs.append(pl.BlockSpec((1, 1, rel_rows.shape[2]), lambda i, j: (i * heads + j, 0, 0)))
        args.append(rel_rows)
        scratch = [pltpu.VMEM((128, width), f32)] * 2
    return pl.pallas_call(
        functools.partial(forward_kernel, has_bias, causal, centre),
        grid=(groups, heads),
        in_specs=in_specs,
        out_specs=[
            pl.BlockSpec((1, q_rows, lanes), lambda i, j: (i, 0, 0)),
            pl.BlockSpec((1, 1, 1, q_rows), lambda i, j: (i, j, 0, 0)),
        ],
        out_shape=[
            jax.ShapeDtypeStruct((groups, q_rows, lanes), bf16),
            jax.ShapeDtypeStruct((groups, heads, 1, q_rows), f32),
        ],
        scratch_shapes=scratch,
        compiler_params=pltpu.CompilerParams(vmem_limit_bytes=40 * 2**20),
    )(*args)


def fold(strip):
    rows, width = strip.shape
    while rows > 8:
        rows //= 2
        strip = strip[:rows] + pltpu.roll(strip[rows:], width - rows, 1)
    return strip


def backward_kernel(has_bias, causal, centre, scal, q_ref, kvo_ref, kvt_ref, up_ref, lse_ref, *rest):
    if has_bias:
        rel_ref, dq_ref, dkvo_ref, dkvt_ref, drel_ref, so_ref, st_ref, go_ref, gt_ref = rest[:9]
        dq_acc, ko_acc, vo_acc, kt_acc, vt_acc = rest[9:]
    else:
        dq_ref, dkvo_ref, dkvt_ref, dq_acc, ko_acc, vo_acc, kt_acc, vt_acc = rest
    core, key_len, head = scal[0], scal[1], pl.program_id(1)
    q_rows, k_rows = q_ref.shape[1], kvo_ref.shape[1]
    lanes = q_ref.shape[2]
    lane_mask = lax.broadcasted_iota(jnp.int32, (1, lanes), 1) // DH == head
    if has_bias:
        own, other = bases_of(lanes, k_rows, core, centre)
        so_ref[...] = bias_strip(rel_ref[0], own, so_ref.shape[1])
        st_ref[...] = bias_strip(rel_ref[0], other, st_ref.shape[1])
        go_ref[...] = jnp.zeros_like(go_ref)
        gt_ref[...] = jnp.zeros_like(gt_ref)

    @pl.when(head == 0)
    def clear():
        for acc in (ko_acc, vo_acc, kt_acc, vt_acc):
            acc[...] = jnp.zeros_like(acc)

    step = min(CHUNK, q_rows)
    for col in range(0, q_rows, step):
        queries = jnp.where(lane_mask, q_ref[0, col : col + step, :], 0.0).astype(bf16)
        ups = jnp.where(lane_mask, up_ref[0, col : col + step, :], 0.0).astype(bf16)
        lse = lse_ref[0, 0, :, col : col + step]
        sides = []
        delta = jnp.zeros((1, step), f32)
        for part, kv_ref, s_ref, k_acc, v_acc in (
            (0, kvo_ref, so_ref if has_bias else None, ko_acc, vo_acc),
            (1, kvt_ref, st_ref if has_bias else None, kt_acc, vt_acc),
        ):
            scores = part_scores(
                kv_ref[0, :, :lanes], queries, s_ref, col, part, core, key_len, causal
            )
            probs = jnp.exp(scores - lse)
            v_acc[...] += dot(probs.astype(bf16), ups, 1, 0)
            dprobs = dot(kv_ref[0, :, lanes:], ups, 1, 1).astype(bf16).astype(f32)
            delta = delta + jnp.sum(probs * dprobs, axis=0, keepdims=True)
            sides.append((probs, dprobs))
        dq = jnp.zeros((lanes, step), f32)
        for (probs, dprobs), kv_ref, g_ref, k_acc in (
            (sides[0], kvo_ref, go_ref if has_bias else None, ko_acc),
            (sides[1], kvt_ref, gt_ref if has_bias else None, kt_acc),
        ):
            ds = (probs * (dprobs - delta)).astype(bf16)
            k_acc[...] += dot(ds, queries, 1, 0)
            dq = dq + dot(kv_ref[0, :, :lanes], ds, 0, 0)
            if has_bias:
                wide_ds = ds.astype(f32)
                blocks = k_rows // 128
                for j in range(blocks):
                    at = (blocks - 1 - j) * 128 + col
                    g_ref[:, at : at + step] += wide_ds[j * 128 : (j + 1) * 128]
        dq_acc[col : col + step, :] = jnp.where(
            lane_mask, dq.T, dq_acc[col : col + step, :]
        )
    if has_bias:
        drel_ref[0, 0, 0] = fold(go_ref[...])
        drel_ref[0, 0, 1] = fold(gt_ref[...])

    @pl.when(head == pl.num_programs(1) - 1)
    def write():
        dq_ref[0] = dq_acc[...].astype(bf16)
        dkvo_ref[0] = jnp.concatenate([ko_acc[...], vo_acc[...]], axis=1)
        dkvt_ref[0] = jnp.concatenate([kt_acc[...], vt_acc[...]], axis=1).astype(bf16)


def attend_back(scal, q, kvo, kvt, up, lse, rel_rows, centre, causal):
    groups, q_rows, lanes = q.shape
    k_rows = kvo.shape[1]
    heads = lanes // DH
    has_bias = rel_rows is not None
    width = q_rows + (k_rows // 128 - 1) * 128
    gwidth = width + 128
    per_group = lambda i, j: (i, 0, 0)
    in_specs = [
        pl.BlockSpec(memory_space=pltpu.SMEM),
        pl.BlockSpec((1, q_rows, lanes), per_group),
        pl.BlockSpec((1, k_rows, 2 * lanes), per_group),
        pl.BlockSpec((1, k_rows, 2 * lanes), turned),
        pl.BlockSpec((1, q_rows, lanes), per_group),
        pl.BlockSpec((1, 1, 1, q_rows), lambda i, j: (i, j, 0, 0)),
    ]
    args = [scal, q, kvo, kvt, up, lse]
    out_specs = [
        pl.BlockSpec((1, q_rows, lanes), per_group),
        pl.BlockSpec((1, k_rows, 2 * lanes), per_group),
        pl.BlockSpec((1, k_rows, 2 * lanes), turned),
    ]
    out_shape = [
        jax.ShapeDtypeStruct((groups, q_rows, lanes), bf16),
        jax.ShapeDtypeStruct((groups, k_rows, 2 * lanes), f32),
        jax.ShapeDtypeStruct((groups, k_rows, 2 * lanes), bf16),
    ]
    scratch = []
    if has_bias:
        in_specs.append(pl.BlockSpec((1, 1, rel_rows.shape[2]), lambda i, j: (i * heads + j, 0, 0)))
        args.append(rel_rows)
        out_specs.append(pl.BlockSpec((1, 1, 2, 8, gwidth), lambda i, j: (i, j, 0, 0, 0)))
        out_shape.append(jax.ShapeDtypeStruct((groups, heads, 2, 8, gwidth), f32))
        scratch = [pltpu.VMEM((128, width), f32)] * 2 + [pltpu.VMEM((128, gwidth), f32)] * 2
    scratch = scratch + [pltpu.VMEM((q_rows, lanes), f32)] + [pltpu.VMEM((k_rows, lanes), f32)] * 4
    return pl.pallas_call(
        functools.partial(backward_kernel, has_bias, causal, centre),
        grid=(groups, heads),
        in_specs=in_specs,
        out_specs=out_specs,
        out_shape=out_shape,
        scratch_shapes=scratch,
        compiler_params=pltpu.CompilerParams(vmem_limit_bytes=40 * 2**20),
    )(*args)


def rel_grad_rows(drel, core, k_rows, centre, length):
    groups, heads, parts, eight, gwidth = drel.shape
    drel = drel.reshape(groups * heads, parts, eight, gwidth)
    line = sum(jnp.roll(drel[:, :, r, :], -r, axis=-1) for r in range(eight))
    line = jnp.roll(line, 127, axis=-1)
    own, other = bases_of(0, k_rows, core, centre)
    total = jnp.zeros((line.shape[0], length + gwidth + 128), f32)
    for part, base in ((0, own), (1, other)):
        old = lax.dynamic_slice_in_dim(total, base + 1, gwidth, 1)
        total = lax.dynamic_update_slice_in_dim(total, old + line[:, part], base + 1, 1)
    return total[:, 128 : 128 + length]


def rms_forward(inputs, gain_row):
    inverse = lax.rsqrt(jnp.mean(inputs * inputs, axis=-1, keepdims=True) + epsilon)
    return ((inputs * inverse * gain_row).astype(bf16), inverse)


def rms_backward(inputs, gain_row, inverse, upstream):
    upstream = upstream.astype(bf16).astype(f32)
    gain_grad = jnp.sum(upstream * inputs * inverse, axis=0)
    inner = jnp.sum(upstream * gain_row * inputs, axis=-1, keepdims=True)
    result = inverse * gain_row * upstream - inputs * (inverse**3 * inner / inputs.shape[-1])
    return (result, gain_grad)


def project(rows, weights):
    return jnp.einsum("rk,nkc->nrc", rows, weights, preferred_element_type=f32)


def project_back(grads, weights):
    return jnp.einsum("nrc,nkc->rk", grads, weights, preferred_element_type=f32)


def outer(rows, grads):
    return jnp.einsum("rk,nrc->nkc", rows, grads, preferred_element_type=f32)


MESH = pl.DeviceIdType.MESH


def greet(peers):
    barrier = pltpu.get_barrier_semaphore()
    for peer in peers:
        pl.semaphore_signal(barrier, inc=1, device_id=peer, device_id_type=MESH)
    pl.semaphore_wait(barrier, len(peers))


def remote(src, dst, send_sem, recv_sem, peer):
    return pltpu.make_async_remote_copy(
        src_ref=src, dst_ref=dst, send_sem=send_sem, recv_sem=recv_sem,
        device_id=peer, device_id_type=MESH,
    )


def start_kernel(
    units, vocab, ids_ref, table_ref, shard_ref, full_ref, mine_ref,
    ids_all, ids_col, looked, from_x, from_z1, from_z2, total,
    own_sem, w_send, w_recv, id_send, id_recv, e_send, e_recv,
):
    wide, narrow = lax.axis_index("wide"), lax.axis_index("narrow")
    flip = lambda bit: wide + bit - 2 * bit * (wide // bit % 2)
    z2, z1, x = wide // 4, wide // 2 % 2, wide % 2
    at_x, at_z1, at_z2 = (flip(1), narrow), (flip(2), narrow), (flip(4), narrow)
    at_core = (wide, narrow + 1 - 2 * (narrow % 2))
    at_y = (wide, narrow + 2 - 4 * (narrow // 2))
    others = []
    for r in range(1, 8):
        there = wide
        for bit in (1, 2, 4):
            if r & bit:
                there = there + bit - 2 * bit * (wide // bit % 2)
        others.append((there, narrow))
    greet(others + [at_core, at_y])

    def own(j):
        return pltpu.make_async_copy(shard_ref.at[j], full_ref.at[j, 0, z2, z1, x], own_sem.at[j])

    def copy(j, stage):
        if stage == 0:
            src, dst, peer = shard_ref.at[j], full_ref.at[j, 0, z2, z1, x], at_z2
        elif stage == 1:
            src = dst = full_ref.at[j, 0, :, z1, x]
            peer = at_z1
        elif stage == 2:
            src = dst = full_ref.at[j, 0, :, :, x]
            peer = at_x
        elif stage == 3:
            src, dst, peer = full_ref.at[j, 0], full_ref.at[j, 2], at_y
        elif stage == 4:
            src, dst, peer = full_ref.at[j, 0], full_ref.at[j, 1], at_core
        else:
            src, dst, peer = full_ref.at[j, 2], full_ref.at[j, 3], at_core
        return remote(src, dst, w_send.at[j, stage], w_recv.at[j, stage], peer)

    def advance(j, stage):
        if stage == 1:
            own(j).wait()
        if stage > 0:
            copy(j, {5: 3}.get(stage, stage - 1)).wait_recv()
        copy(j, stage).start()
        if stage == 3:
            copy(j, 4).start()

    def ids_copy(r):
        return remote(
            ids_all.at[0], ids_all.at[r], id_send.at[r], id_recv.at[r], others[r - 1]
        )

    ids_all[0] = ids_ref[...]
    for r in range(1, 8):
        ids_copy(r).start()
    for j in range(units):
        own(j).start()
    for j in range(min(3, units)):
        advance(j, 0)

    rows = ids_ref.shape[1]
    cut = total.shape[0]

    def look_up(r):
        if r > 0:
            ids_copy(r).wait_recv()
        ids = ids_all[r] - wide * vocab
        for t in range(rows // 128):
            ids_col[t * 128 : (t + 1) * 128] = jnp.broadcast_to(
                ids[:, t * 128 : (t + 1) * 128], (128, 128)
            ).T
        total[...] = jnp.zeros_like(total)

        def add(k, unused):
            lane = lax.broadcasted_iota(jnp.int32, (rows, 128), 1) + k * 512
            col = ids_col[...]
            hot = jnp.concatenate(
                [(col == lane + q * 128).astype(f32) for q in range(4)], axis=1
            ).astype(bf16)
            block = table_ref[pl.ds(pl.multiple_of(k * 512, 512), 512), :]
            total[...] += dot(hot, block, 1, 0)
            return unused

        lax.fori_loop(0, table_ref.shape[0] // 512, add, 0)
        looked[r] = total[...].astype(bf16)

    def e_copy(hop_at, index):
        if hop_at == 0:
            src, dst, peer = looked.at[2 * index + 1], from_x.at[index], at_x
        elif hop_at == 1:
            src, dst, peer = looked.at[4 * index + 2], from_z1.at[index], at_z1
        else:
            src, dst, peer = looked.at[4], from_z2.at[0], at_z2
        slot = (0, 4, 6)[hop_at] + index
        return remote(src, dst, e_send.at[slot], e_recv.at[slot], peer)

    order = (3, 1, 2, 0)
    todo = []
    for j in range(units):
        todo += [(5 * j + 6 * s + s * s, j, s) for s in (1, 2, 3, 5)]
        if j >= 3:
            todo.append((5 * j, j, 0))
    todo = [(j, s) for unused, j, s in sorted(todo)]
    steps = []
    for s in order:
        steps.append(("odd", s))
    for s in order:
        steps.append(("even", s))
    for s in order:
        steps.append(("merge", s))
    share = -(-len(todo) // (len(steps) + 4))
    for kind, s in steps:
        if kind == "odd":
            look_up(2 * s + 1)
            e_copy(0, s).start()
        elif kind == "even":
            look_up(2 * s)
        else:
            e_copy(0, s).wait_recv()
            looked[2 * s] = looked[2 * s] + from_x[s]
            if s % 2 == 1:
                e_copy(1, s // 2).start()
            else:
                e_copy(1, s // 2).wait_recv()
                looked[2 * s] = looked[2 * s] + from_z1[s // 2]
                if s == 2:
                    e_copy(2, 0).start()
        for j, stage in todo[:share]:
            advance(j, stage)
        todo = todo[share:]
    for j, stage in todo:
        advance(j, stage)
    e_copy(2, 0).wait_recv()
    mine_ref[...] = looked[0] + from_z2[0]
    for j in range(units):
        for stage in range(6):
            copy(j, stage).wait_send()
        for stage in (4, 5):
            copy(j, stage).wait_recv()
    for r in range(1, 8):
        ids_copy(r).wait_send()
    for hop_at, count in ((0, 4), (1, 2), (2, 1)):
        for index in range(count):
            e_copy(hop_at, index).wait_send()


def start_phase(ids, table_low, shards):
    units, slim, columns = shards.shape
    rows, (vocab, width) = ids.shape[1], table_low.shape
    padded = -(-vocab // 512) * 512
    table_low = jnp.pad(table_low, ((0, padded - vocab), (0, 0)))
    any_space = pl.BlockSpec(memory_space=pl.ANY)
    vmem = pl.BlockSpec(memory_space=pltpu.VMEM)
    dma = pltpu.SemaphoreType.DMA
    full, mine = pl.pallas_call(
        functools.partial(start_kernel, units, vocab),
        in_specs=[vmem, vmem, any_space],
        out_specs=[any_space, vmem],
        out_shape=[
            jax.ShapeDtypeStruct((units, 4, 2, 2, 2, slim, columns), bf16),
            jax.ShapeDtypeStruct((rows, width), bf16),
        ],
        scratch_shapes=[
            pltpu.VMEM((8, 1, rows), jnp.int32),
            pltpu.VMEM((rows, 128), jnp.int32),
            pltpu.VMEM((8, rows, width), bf16),
            pltpu.VMEM((4, rows, width), bf16),
            pltpu.VMEM((2, rows, width), bf16),
            pltpu.VMEM((1, rows, width), bf16),
            pltpu.VMEM((rows, width), f32),
            dma((units,)),
            dma((units, 6)),
            dma((units, 6)),
            dma((8,)),
            dma((8,)),
            dma((7,)),
            dma((7,)),
        ],
        compiler_params=pltpu.CompilerParams(
            collective_id=0, has_side_effects=True, vmem_limit_bytes=52 * 2**20
        ),
        cost_estimate=pl.CostEstimate(
            flops=2 * 8 * rows * padded * width, bytes_accessed=2 * 4 * 8 * units * slim * columns,
            transcendentals=0,
        ),
    )(ids, table_low, shards)
    return full.reshape(units, 4, 8 * slim, columns), mine


def body(
    enc_ids, enc_len, tgt_ids, tgt_len, span_mask, buckets,
    attn_in, attn_out, ff_in, ff_out, table, gains, rel,
    mom_attn_in, mom_attn_out, mom_ff_in, mom_ff_out, mom_table, mom_gains, mom_rel,
    avg_attn_in, avg_attn_out, avg_ff_in, avg_ff_out, avg_table, avg_gains, avg_rel,
):
    wide_size = lax.axis_size("wide")
    narrow_size = lax.axis_size("narrow")
    wide_index = lax.axis_index("wide")
    narrow_index = lax.axis_index("narrow")
    micro = narrow_index // 2
    core = narrow_index % 2
    width = table.shape[1]
    vocab = table.shape[0]
    enc_rows = enc_ids.shape[2] // 2
    dec_rows = tgt_ids.shape[2] // 2
    centre = (buckets.shape[0] + 1) // 2 - 1
    lanes = attn_out.shape[1]
    heads_here = lanes // DH
    slim = attn_in.shape[1]

    shards = []
    for layer in range(3):
        packed = attn_in[layer].reshape(slim, heads_here, 3, DH).transpose(0, 2, 1, 3)
        shards.append(jnp.concatenate([packed.reshape(slim, -1), attn_out[layer].T], axis=1))
    for layer in range(2):
        shards.append(ff_in[layer])
        shards.append(ff_out[layer].T)
    shards = jnp.stack(shards).astype(bf16)
    groups = narrow_index ^ jnp.arange(narrow_size)
    small = jnp.concatenate([gains.reshape(-1), rel.reshape(-1)])
    small = lax.all_gather(small, "narrow", axis=0, tiled=False)
    cut = gains.size
    gains_full = small[:, :cut].reshape(narrow_size, *gains.shape).transpose(1, 0, 2)
    gains_full = gains_full.reshape(gains.shape[0], -1)
    rel_full = small[:, cut:].reshape(narrow_size, *rel.shape).transpose(1, 2, 0, 3)
    rel_full = rel_full.reshape(rel.shape[0], rel.shape[1], -1)
    onehot_rev = (buckets[::-1][:, None] == jnp.arange(rel.shape[1])[None, :]).astype(f32)
    onehot_rev = jnp.pad(onehot_rev, ((0, 1), (0, 0)))
    rel_rows = [
        jnp.dot(onehot_rev, rel_full[i], precision=highest)
        .T.reshape(narrow_size, heads_here, 1, -1)[groups]
        .reshape(narrow_size * heads_here, 1, -1)
        for i in range(2)
    ]

    my_enc = lax.dynamic_slice(enc_ids, (micro, 0, core * enc_rows), (1, 1, enc_rows))
    others = wide_index ^ jnp.arange(wide_size)
    targets_micro = lax.dynamic_index_in_dim(tgt_ids, micro, 0, keepdims=False)[others]
    shifted = jnp.concatenate(
        [jnp.zeros((wide_size, 1), jnp.int32), targets_micro[:, :-1]], axis=1
    )
    dec_all = lax.dynamic_slice_in_dim(shifted, core * dec_rows, dec_rows, 1)
    table_low = table.astype(bf16)
    enc_all = gather_direct(my_enc.reshape(enc_rows), "wide")
    tokens = jnp.concatenate([enc_all, dec_all], axis=1)
    local = tokens - wide_index * vocab
    held = (local >= 0) & (local < vocab)
    local = jnp.where(held, local, 0)
    if wide_size == 8 and narrow_size == 4:
        my_ids = jnp.concatenate([my_enc.reshape(enc_rows), dec_all[0]])[None]
        gathered, mine = start_phase(my_ids, table_low, shards)
    else:
        gathered = []
        for shard in shards:
            column = gather_sorted(shard, "wide").reshape(width, -1)
            pair = jnp.stack([column, hop(column, "narrow", 2)])
            pair = jnp.stack([pair, swap(pair)], axis=1)
            gathered.append(pair.reshape(narrow_size, width, -1))
        rows = table_low[local.reshape(-1)]
        rows = jnp.where(held.reshape(-1)[:, None], rows, 0).astype(bf16)
        mine = scatter_relative(rows.reshape(*local.shape, width), "wide", bf16)
    low_in = [gathered[i][:, :, : 3 * lanes] for i in range(3)]
    low_out = [gathered[i][:, :, 3 * lanes :] for i in range(3)]
    low_up = [gathered[3], gathered[5]]
    low_down = [gathered[4], gathered[6]]

    enc0 = mine[:enc_rows].astype(f32)
    dec0 = mine[enc_rows:].astype(f32)

    key_len = lax.dynamic_slice(enc_len, (micro, 0), (1, 1)).reshape(())
    scal = jnp.stack([core, key_len]).astype(jnp.int32)

    def attn_forward(state, gain_row, layer, source, rel_row, causal):
        normed, inverse = rms_forward(state, gain_row)
        kv = project(normed if source is None else source, low_in[layer][:, :, lanes:]).astype(bf16)
        kv_other = swap(kv)
        q = project(normed, low_in[layer][:, :, :lanes]).astype(bf16)
        mixed, lse = attend(scal, q, kv, kv_other, rel_row, centre, causal)
        update = project_back(mixed, low_out[layer])
        return (state + update, (state, inverse, normed, q, kv, kv_other, mixed, lse))

    def attn_backward(saved, upstream, gain_row, layer, source, rel_row, causal):
        state, inverse, normed, q, kv, kv_other, mixed, lse = saved
        up = upstream.astype(bf16)
        out_grad = outer(up, mixed)
        mixed_grad = project(up, low_out[layer]).astype(bf16)
        outs = attend_back(scal, q, kv, kv_other, mixed_grad, lse, rel_row, centre, causal)
        dq, dkv_own, dkv_other = outs[:3]
        dkv = (dkv_own + swap(dkv_other).astype(f32)).astype(bf16)
        q_grad = outer(normed, dq)
        kv_grad = outer(normed if source is None else source, dkv)
        normed_grad = project_back(dq, low_in[layer][:, :, :lanes])
        kv_back = project_back(dkv, low_in[layer][:, :, lanes:])
        if source is None:
            normed_grad = normed_grad + kv_back
        state_grad, gain_grad = rms_backward(state, gain_row, inverse, normed_grad)
        grads = jnp.concatenate([q_grad, kv_grad, out_grad], axis=2).astype(bf16)
        return (upstream + state_grad, gain_grad, grads, kv_back, outs[3] if rel_row is not None else None)

    def ff_forward(state, gain_row, layer):
        normed, inverse = rms_forward(state, gain_row)
        pre = project(normed, low_up[layer])
        hidden = jax.nn.gelu(pre).astype(bf16)
        return (state + project_back(hidden, low_down[layer]), (state, inverse, normed, pre, hidden))

    def ff_backward(saved, upstream, gain_row, layer):
        state, inverse, normed, pre, hidden = saved
        up = upstream.astype(bf16)
        out_grad = outer(up, hidden).astype(bf16)
        hidden_grad = project(up, low_down[layer]).astype(bf16).astype(f32)
        unused, gelu_back = jax.vjp(jax.nn.gelu, pre)
        pre_grad = gelu_back(hidden_grad)[0].astype(bf16)
        in_grad = outer(normed, pre_grad).astype(bf16)
        normed_grad = project_back(pre_grad, low_up[layer])
        state_grad, gain_grad = rms_backward(state, gain_row, inverse, normed_grad)
        return (upstream + state_grad, gain_grad, in_grad, out_grad)

    def scatter(grad):
        pairs = grad.reshape(2, 2, width, -1)
        across = pairs[:, 0].astype(f32) + swap(pairs[:, 1]).astype(f32)
        column = across[0] + hop(across[1].astype(bf16), "narrow", 2).astype(f32)
        return scatter_sorted(column.astype(bf16).reshape(wide_size, slim, -1), "wide")

    enc1, saved_a = attn_forward(enc0, gains_full[0], 0, None, rel_rows[0], 0)
    enc2, saved_b = ff_forward(enc1, gains_full[1], 0)
    encoded, enc_inverse = rms_forward(enc2, gains_full[2])
    dec1, saved_c = attn_forward(dec0, gains_full[3], 1, None, rel_rows[1], dec_rows)
    dec2, saved_d = attn_forward(dec1, gains_full[4], 2, encoded, None, 0)
    dec3, saved_e = ff_forward(dec2, gains_full[5], 1)
    final_gain = gains_full[6] * width ** (-0.5)
    final, final_inverse = rms_forward(dec3, final_gain)

    row_weight = (jnp.arange(2 * dec_rows)[None, None, :] < tgt_len[:, :, None]).astype(
        f32
    ) * span_mask.astype(f32)
    count = jnp.sum(row_weight)
    weights_micro = lax.dynamic_index_in_dim(row_weight, micro, 0, keepdims=False)[others]
    weights = lax.dynamic_slice_in_dim(weights_micro, core * dec_rows, dec_rows, 1).reshape(-1)
    targets = lax.dynamic_slice_in_dim(targets_micro, core * dec_rows, dec_rows, 1).reshape(-1)
    targets = targets - wide_index * vocab
    final_all = gather_relative(final, "wide").reshape(-1, width)
    logits = dot(final_all, table_low, 1, 1)
    target_hot = jnp.arange(vocab)[None, :] == targets[:, None]
    top = jnp.max(logits, axis=-1)
    total = jnp.sum(jnp.exp(logits - top[:, None]), axis=-1)
    hits = jnp.sum(jnp.where(target_hot, logits, 0.0), axis=-1)
    stats = jnp.stack([top, total, hits]).reshape(3, wide_size, dec_rows)
    if wide_size > 8:
        stats = lax.all_gather(stats[:, others], "wide", axis=0, tiled=False)[:, :, others]
    else:
        stats = jnp.stack(
            [stats]
            + [
                hop(stats, "wide", r)[:, [q ^ r for q in range(wide_size)]]
                for r in range(1, wide_size)
            ]
        )
    stats = stats.reshape(wide_size, 3, -1)
    best = jnp.max(stats[:, 0], axis=0)
    log_total = best + jnp.log(jnp.sum(stats[:, 1] * jnp.exp(stats[:, 0] - best[None]), axis=0))
    loss_rows = weights * (log_total - jnp.sum(stats[:, 2], axis=0))
    loss_part = jnp.sum(loss_rows[:dec_rows])
    logit_grad = (
        (weights / count)[:, None]
        * (jnp.exp(logits - log_total[:, None]) - target_hot.astype(f32))
    ).astype(bf16)
    final_grad = scatter_relative(
        dot(logit_grad, table_low, 1, 0).reshape(wide_size, dec_rows, width), "wide", f32
    )

    gain_grads = [None] * 7
    dec_grad, gain_raw = rms_backward(dec3, final_gain, final_inverse, final_grad)
    gain_grads[6] = gain_raw * width ** (-0.5)
    dec_grad, gain_grads[5], up1, down1 = ff_backward(saved_e, dec_grad, gains_full[5], 1)
    dec_grad, gain_grads[4], attn2, source_grad, unused = attn_backward(
        saved_d, dec_grad, gains_full[4], 2, encoded, None, 0
    )
    dec_grad, gain_grads[3], attn1, unused, drel_dec = attn_backward(
        saved_c, dec_grad, gains_full[3], 1, None, rel_rows[1], dec_rows
    )
    enc_grad, gain_grads[2] = rms_backward(enc2, gains_full[2], enc_inverse, source_grad)
    enc_grad, gain_grads[1], up0, down0 = ff_backward(saved_b, enc_grad, gains_full[1], 0)
    enc_grad, gain_grads[0], attn0, unused, drel_enc = attn_backward(
        saved_a, enc_grad, gains_full[0], 0, None, rel_rows[0], 0
    )
    reduced = [scatter(grad) for grad in (attn0, attn1, attn2, up0, down0, up1, down1)]

    row_grads = jnp.concatenate([enc_grad, dec_grad], axis=0).astype(bf16)
    padded = -(-vocab // 64) * 64
    slots = jnp.arange(padded)
    local = jnp.where(held, local, -1).reshape(-1, 2, local.shape[1])
    halves, part_grads = [], []
    half = width // 2
    for start in (0, half):
        rows = row_grads[None, :, start : start + half]
        for bit in list(bits_down("wide"))[:-1]:
            rows = jnp.stack([rows, hop(rows, "wide", bit)], axis=1)
            rows = rows.reshape(-1, *rows.shape[2:])
        far = hop(rows, "wide", 1)
        partial = dot(logit_grad, final_all[:, start : start + half], 0, 0)
        partial = jnp.pad(partial, ((0, padded - vocab), (0, 0)))
        for at, values in ((local[:, 0], rows), (local[:, 1], far)):
            token_hot = (slots[:, None] == at.reshape(-1)[None, :]).astype(bf16)
            partial = partial + dot(token_hot, values.reshape(-1, half), 1, 0)
        quarters = partial.astype(bf16).reshape(narrow_size, padded // narrow_size, half)
        part = scatter_sorted(quarters, "narrow").astype(bf16)
        part_grads.append(part.astype(f32))
        halves.append(gather_sorted(part, "narrow").reshape(padded, half)[:vocab])
    table_grad = jnp.concatenate(halves, axis=1).astype(f32)

    length = onehot_rev.shape[0]
    rel_grad = jnp.stack(
        [
            jnp.dot(rel_grad_rows(drel_enc, core, enc_rows, centre, length), onehot_rev, precision=highest),
            jnp.dot(rel_grad_rows(drel_dec, core, dec_rows, centre, length), onehot_rev, precision=highest),
        ]
    )
    rel_grad = rel_grad.reshape(2, narrow_size, heads_here, -1)[:, groups]
    rel_grad = rel_grad.reshape(2, narrow_size * heads_here, -1)
    gain_total, rel_total, loss_sum = lax.psum(
        (jnp.stack(gain_grads), rel_grad, loss_part), ("wide", "narrow")
    )
    squares = sum(jnp.sum(grad * grad) for grad in reduced + part_grads)
    square_sum = lax.psum(squares, ("wide", "narrow"))
    square_sum = square_sum + jnp.sum(gain_total * gain_total) + jnp.sum(rel_total * rel_total)
    gain_mine = lax.dynamic_slice_in_dim(gain_total, narrow_index * lanes, lanes, 1)
    rel_mine = lax.dynamic_slice_in_dim(
        rel_total, narrow_index * heads_here, heads_here, 1
    ).transpose(0, 2, 1)

    def unpack_in(grad):
        grad = grad[:, : 3 * lanes].reshape(slim, 3, heads_here, DH).transpose(0, 2, 1, 3)
        return grad.reshape(slim, -1)

    grads = (
        jnp.stack([unpack_in(reduced[i]) for i in range(3)]),
        jnp.stack([reduced[i][:, 3 * lanes :].T for i in range(3)]),
        jnp.stack([reduced[3], reduced[5]]),
        jnp.stack([reduced[4].T, reduced[6].T]),
        table_grad,
        gain_mine,
        rel_mine,
    )
    norm = jnp.sqrt(square_sum)
    scale = jnp.minimum(1.0, clip_norm / norm)
    base_rate = math.sqrt(PARAMS) / (3.0 * clip_norm)
    matrix_rate = base_rate / math.sqrt(width)
    rates = (
        matrix_rate, 16.0 * matrix_rate, matrix_rate, matrix_rate,
        base_rate, 0.3 * base_rate, 0.3 * base_rate,
    )
    params = (attn_in, attn_out, ff_in, ff_out, table, gains, rel)
    moms = (mom_attn_in, mom_attn_out, mom_ff_in, mom_ff_out, mom_table, mom_gains, mom_rel)
    avgs = (avg_attn_in, avg_attn_out, avg_ff_in, avg_ff_out, avg_table, avg_gains, avg_rel)
    fresh, scaled_grads, averages = ([], [], [])
    for index in range(7):
        clipped = grads[index] * scale
        moment = momentum_decay * moms[index] + clipped
        weight = params[index] - rates[index] * (clipped + momentum_decay * moment)
        fresh.append(weight)
        scaled_grads.append(clipped)
        averages.append(average_decay * avgs[index] + (1.0 - average_decay) * weight)
    return (loss_sum, count, norm, *fresh, *scaled_grads, *averages)


def solution(mesh):
    weights = (
        P(None, "wide", "narrow"),
        P(None, "narrow", "wide"),
        P(None, "wide", "narrow"),
        P(None, "narrow", "wide"),
        P("wide", None),
        P(None, "narrow"),
        P(None, None, "narrow"),
    )
    in_specs = (P(None, "wide", None), P(None, "wide"), P(), P(), P(), P()) + weights * 3
    out_specs = (P(), P(), P()) + weights * 3
    return jax.shard_map(body, mesh=mesh, in_specs=in_specs, out_specs=out_specs, check_vma=False)
```

time: 4620 us -> 1370 us (0.30); the launches traced: 4530 us -> 1370 us
  local copies, waits for them, and re-layouts: 1890 us -> 164 us
  waiting for transfers between devices: 1640 us -> 296 us
  Pallas kernels: 0 us -> 403 us
  blocking collectives: 290 us -> 50.3 us
  other arithmetic: 325 us -> 150 us
  matrix products: 356 us -> 227 us
  starting transfers between devices: 4.36 us -> 64.2 us
    unnamed x727 -> x484, local copies, waits for them, and re-layouts: 1710 us -> 35.4 us
    reduce_scatter x26 -> x0, waiting for transfers between devices: 1080 us -> none  [the longest x15 838 us: narrow_grad(): lax.psum_scatter(partial_value, 'narrow', scatter_dimension=1, tiled=True)]
    all_gather x16 -> x0, waiting for transfers between devices: 493 us -> none  [the longest x7 315 us: widen(): lax.all_gather(values.astype(jnp.bfloat16), 'narrow', axis=1, tiled=True)]
    pallas_call x0 -> x7, Pallas kernels: none -> 403 us  [the longest x1 284 us: start_phase(): pl.pallas_call(functools.partial(start_kernel, units, vocab), in_specs=[v...]
    ppermute x0 -> x75, waiting for transfers between devices: none -> 296 us  [hop(): return lax.ppermute(values, axis, [(i, i ^ bit) for i in range(size)])]
    all_gather x15 -> x1, blocking collectives: 138 us -> 6.21 us  [body(): small = lax.all_gather(small, 'narrow', axis=0, tiled=False)]
    dot_general x112 -> x51, matrix products: 356 us -> 227 us  [the longest x8 93.6 us: dot(): lax.dot_general(left, right, (((left_dim,), (right_dim,)), ((), ())), pre...]
    psum x12 -> x1, blocking collectives: 153 us -> 44.1 us  [body(): lax.psum((jnp.stack(gain_grads), rel_grad, loss_part), ('wide', 'narrow'))]
  transfers between devices with their start and end apart: 46 -> 75, of which waited for: 28 -> 29; matrix products, arithmetic and copies ran while one was open for 52% -> 26% of each run, Pallas kernels for 0% -> 4%
where the time goes in v1:
time: 1370 us
  Pallas kernels  403 us (29%)
  waiting for transfers between devices  296 us (22%)
  matrix products  227 us (17%)
  local copies, waits for them, and re-layouts  164 us (12%)
  other arithmetic  150 us (11%)
  starting transfers between devices  64.2 us (5%)
  blocking collectives  50.3 us (4%)
  between operations  14 us (1%)
    ppermute x75, waiting for transfers between devices, hop(): return lax.ppermute(values, axis, [(i, i ^ bit) for i in range(size)])  296 us
    pallas_call x1, Pallas kernels, start_phase(): pl.pallas_call(functools.partial(start_kernel, units, vocab), in_specs=[v...  284 us
    dot_general x8, matrix products, dot(): lax.dot_general(left, right, (((left_dim,), (right_dim,)), ((), ())), pre...  93.6 us
    pallas_call x3, Pallas kernels, attend_back(): pl.pallas_call(functools.partial(backward_kernel, has_bias, causal, centr...  72.6 us
    ppermute x75, starting transfers between devices, hop(): return lax.ppermute(values, axis, [(i, i ^ bit) for i in range(size)])  64.2 us
    pallas_call x3, Pallas kernels, attend(): pl.pallas_call(functools.partial(forward_kernel, has_bias, causal, centre...  46 us
    dot_general x13, matrix products, project_back(): return jnp.einsum('nrc,nkc->rk', grads, weights, preferred_element_type=f32)  45.9 us
    psum x1, blocking collectives, body(): lax.psum((jnp.stack(gain_grads), rel_grad, loss_part), ('wide', 'narrow'))  44.1 us
  transfers between devices with their start and end apart: 75, of which 29 were waited for; matrix products, arithmetic and copies ran while one was open for 26% of the time, Pallas kernels for 4%

profile of v1, /device:TPU:0, one launch (start us, length us, event | category | flops | bytes accessed | tf_op | source)
XLA Modules:
  0.0 1368.2 jit_solution(18141822820287727121)
XLA Ops:
  28.4 283.9 %shard_map.505 = (bf16[7,4,2,2,2,96,768]{6,5,4,3,2,1,0:T(8,128)(2,1)}, bf16[640,768]{1,0:T(8,128)(2,1)S(1)}) custom-call(s32[1,640]{1,0:T(1,128)S(1)} %broadcast_in_dim.31.ids_ref, bf16[4096,768]{1,0:T(8,128)(2,1)} %pad.21.table_ref, bf16[7,96,768]{2,1,0:T(8,128)(2,1)S(1)} %fusion.254.shard_ref), custom_call_target="tpu_custom_call" | custom-call | flops 32212254720 | bytes 33030144 | tf_op jit(solution)/shard_map/pallas_call | solution.py:541
  312.3 25.0 %fusion.352 = (bf16[1,4,2,2,2,96,768]{6,5,4,3,2,1,0:T(8,128)(2,1)}, bf16[1,4,2,2,2,96,768]{6,5,4,3,2,1,0:T(8,128)(2,1)}, bf16[1,4,2,2,2,96,768]{6,5,4,3,2,1,0:T(...) fusion(bf16[7,4,2,2,2,96,768]{6,5,4,3,2,1,0:T(8,128)(2,1)} %get, ...), kind=kLoop, calls=%fused_computation.634 | loop fusion | bytes 66060288 | tf_op jit(solution)/shard_map/slice | solution.py:650
  350.2 25.5 %shard_map.507 = (bf16[4,512,192]{2,1,0:T(8,128)(2,1)S(1)}, f32[4,3,1,512]{3,2,1,0:T(1,128)S(1)}) custom-call(s32[2]{0:T(128)S(1)} %pad_add_fusion.1.scal, bf16[4,512,192]{2,1,0:T(8,128)(2,1)S(1)} %bitcast.860, bf16[4,512,384]{2,1,0:T(8,128)(2,1)S(1)} %fusion.89.kvo_ref, bf16[4,512,384]{2,1,0:T(8,128)(2,1)} %collective-permute-done.1.kvt_ref, ...), custom_call_target="tpu_custom_call" | custom-call | tf_op jit(solution)/shard_map/pallas_call | solution.py:190
  384.6 8.5 multiply_reduce_fusion
  404.8 8.9 shard_map.506
  420.7 11.7 shard_map.508
  442.7 10.9 collective-permute-done.3
  455.3 10.1 collective-permute-done.4
  475.6 10.3 collective-permute-done.5
  487.5 9.4 fusion.357
  529.5 10.9 fusion.358
  549.0 9.7 collective-permute-done.54
  577.2 9.8 fusion.198
  607.1 16.9 %shard_map.509 = (bf16[4,128,192]{2,1,0:T(8,128)(2,1)S(1)}, f32[4,512,384]{2,1,0:T(8,128)S(1)}, bf16[4,512,384]{2,1,0:T(8,128)(2,1)}) custom-call(s32[2]{0:T(128)S(1)} %pad_add_fusion.1.scal, bf16[4,128,192]{2,1,0:T(8,128)(2,1)S(1)} %bitcast.866, bf16[4,512,384]{2,1,0:T(8,128)(2,1)S(1)} %fusion.86.kvo_ref, ...), custom_call_target="tpu_custom_call" | custom-call | tf_op jit(solution)/shard_map/pallas_call | solution.py:319
  642.2 13.5 shard_map.511
  707.0 8.7 fusion.14
  727.9 42.3 %shard_map.510 = (bf16[4,512,192]{2,1,0:T(8,128)(2,1)S(1)}, f32[4,512,384]{2,1,0:T(8,128)S(1)}, bf16[4,512,384]{2,1,0:T(8,128)(2,1)}, f32[4,3,2,8,1024]{4,3,2,1,0:T(8,128)S(1)}) custom-call(s32[2]{0:T(128)S(1)} %pad_add_fusion.1.scal, bf16[4,512,192]{2,1,0:T(8,128)(2,1)S(1)} %bitcast.861, bf16[4,512,384]{2,1,0:T(8,128)(2,1)S(1)} %copy-done.3, ...), custom_call_target="tpu_custom_call" | custom-call | tf_op jit(solution)/shard_map/pallas_call | solution.py:319
  861.7 20.6 %collective-permute-done.50 = bf16[768,768]{1,0:T(8,128)(2,1)} collective-permute-done((bf16[768,768]{1,0:T(8,128)(2,1)}, bf16[768,768]{1,0:T(8,128)(2,1)}, u32[]{:S(2)}, u32[]{:S(2)}) %collective-permute-start.50) | collective-permute-done | bytes 1179680 | tf_op jit(solution)/shard_map/ppermute | solution.py:33
  887.3 18.6 %collective-permute-done.66 = bf16[1,640,384]{2,1,0:T(8,128)(2,1)S(1)} collective-permute-done((bf16[1,640,384]{2,1,0:T(8,128)(2,1)}, bf16[1,640,384]{2,1,0:T(8,128)(2,1)S(1)}, u32[]{:S(2)}, u32[]{:S(2)}) %collective-permute-start.66) | collective-permute-done | bytes 491552 | tf_op jit(solution)/shard_map/ppermute | solution.py:33
  926.1 8.9 collective-permute-done.51
  935.1 28.5 %collective-permute-done.47 = bf16[2,96,768]{2,1,0:T(8,128)(2,1)S(1)} collective-permute-done((bf16[2,96,768]{2,1,0:T(8,128)(2,1)S(1)}, bf16[2,96,768]{2,1,0:T(8,128)(2,1)S(1)}, u32[]{:S(2)}, u32[]{:S(2)}) %collective-permute-start.47) | collective-permute-done | bytes 294944 | tf_op jit(solution)/shard_map/ppermute | solution.py:33
  993.3 14.6 %fusion.3 = f32[4032,384]{1,0:T(8,128)} fusion(bf16[2560,384]{1,0:T(8,128)(2,1)} %bitcast.249, s32[2560]{0:T(1024)S(1)} %copy-done.138), kind=kOutput, calls=%fused_computation.17 | convolution fusion | flops 7937556480 | bytes 8169472 | tf_op jit(solution)/shard_map/dot_general | solution.py:26
  1012.7 14.4 %fusion.2 = f32[4032,384]{1,0:T(8,128)} fusion(bf16[2560,384]{1,0:T(8,128)(2,1)} %bitcast.261, s32[2560]{0:T(1024)S(1)} %copy-done.138), kind=kOutput, calls=%fused_computation.16 | convolution fusion | flops 7937556480 | bytes 8169472 | tf_op jit(solution)/shard_map/dot_general | solution.py:26
  1037.5 8.9 collective-permute-done.40
  1053.1 74.7 %collective-permute-done.31 = bf16[4,96,768]{2,1,0:T(8,128)(2,1)S(1)} collective-permute-done((bf16[4,96,768]{2,1,0:T(8,128)(2,1)S(1)}, bf16[4,96,768]{2,1,0:T(8,128)(2,1)S(1)}, u32[]{:S(2)}, u32[]{:S(2)}) %collective-permute-start.31) | collective-permute-done | bytes 589856 | tf_op jit(solution)/shard_map/ppermute | solution.py:33
  1130.1 10.4 collective-permute-done.36
  1162.1 8.4 collective-permute-done.33
  1174.9 13.8 %add_convert_fusion = bf16[4032,384]{1,0:T(8,128)(2,1)S(1)} fusion(f32[4032,384]{1,0:T(8,128)} %fusion.2, f32[4016,384]{1,0:T(8,128)} %fusion.196, bf16[2560,384]{1,0:T(8,128)(2,1)S(1)} %bitcast.1071, s32[2560]{0:T(1024)S(1)} %copy-done.137), kind=kOutput, calls=%fused_computation.45 | convolution fusion | flops 7942201344 | bytes 17434624 | tf_op jit(solution)/shard_map/dot_general | solution.py:26
  1189.4 14.1 %add_convert_fusion.1 = bf16[4032,384]{1,0:T(8,128)(2,1)S(1)} fusion(f32[4032,384]{1,0:T(8,128)} %fusion.3, f32[4016,384]{1,0:T(8,128)S(1)} %bitcast.1073, bf16[2560,384]{1,0:T(8,128)(2,1)} %bitcast.251, s32[2560]{0:T(1024)S(1)} %copy-done.137), kind=kOutput, calls=%fused_computation.46 | convolution fusion | flops 7942201344 | bytes 17434624 | tf_op jit(solution)/shard_map/dot_general | solution.py:26
  1241.0 12.3 collective-permute-done.65
  1257.6 44.1 %all-reduce.7 = (f32[]{:T(128)}, f32[]{:T(128)}, f32[7,768]{1,0:T(8,128)S(1)}, f32[2,12,32]{2,0,1:T(2,128)S(1)}) all-reduce(f32[]{:T(128)} %slice_reduce_fusion.9, f32[]{:T(128)S(6)} %add.709, f32[7,768]{1,0:T(8,128)S(1)} %stack.286, f32[2,12,32]{2,0,1:T(2,128)S(1)} %bitcast.1045), channel_id=1, replica_groups=mesh['wide'=8,'narrow'=4] {'wide','narrow'}, use_global_device_ids=true, to_apply=%region_14.15 | all-reduce | flops 6146 | bytes 49168 | tf_op jit(solution)/shard_map/psum | solution.py:806
  1338.4 28.4 %multiply_add_fusion = (f32[4016,768]{1,0:T(8,128)}, f32[4016,768]{1,0:T(8,128)}, f32[4016,768]{1,0:T(8,128)}) fusion(f32[4016,768]{1,0:T(8,128)} %param.58, f32[4016,768]{1,0:T(8,128)} %param.44, f32[4016,768]{1,0:T(8,128)} %param.51, f32[]{:T(128)S(6)} %min.3, bf16[4016,384]{1,0:T(8,128)(2,1)} %slice.842, bf16[4016,384]{1,0:T(8,128)(2,1)} %slice.841), kind=kLoop, calls=%fused_computation.26 | loop fusion | flops 43180032 | bytes 80191488 | tf_op jit(solution)/shard_map/add | solution.py:848
  (999 shorter events, 517.6 us)
Async XLA Ops:
  394.8 25.9 %collective-permute-start.2 = (bf16[4,512,384]{2,1,0:T(8,128)(2,1)S(1)}, bf16[4,512,384]{2,1,0:T(8,128)(2,1)}, u32[]{:S(2)}, u32[]{:S(2)}) collective-permute-start(bf16[4,512,384]{2,1,0:T(8,128)(2,1)S(1)} %fusion.86.kvo_ref), channel_id=1, source_target_pairs={{0,1},{1,0},{2,3},{3,2},{4,5},{5,4},{6,7},{7,6},{8,9},{9,8},{10,11... | collective-permute-start | bytes 4718600 | tf_op jit(solution)/shard_map/ppermute | solution.py:33
  543.1 31.0 %collective-permute-start.13 = (bf16[4,128,768]{2,1,0:T(8,128)(2,1)}, bf16[4,128,768]{2,1,0:T(8,128)(2,1)}, u32[]{:S(2)}, u32[]{:S(2)}) collective-permute-start(bf16[4,128,768]{2,1,0:T(8,128)(2,1)} %fusion.192), channel_id=1, source_target_pairs={{0,4},{4,0},{8,12},{12,8},{16,20},{20,16},{24,28},{28,24},{1,5},{5... | collective-permute-start | bytes 2359304 | tf_op jit(solution)/shard_map/ppermute | solution.py:33
  658.0 44.1 %collective-permute-start.16 = (bf16[4,512,384]{2,1,0:T(8,128)(2,1)}, bf16[4,512,384]{2,1,0:T(8,128)(2,1)}, u32[]{:S(2)}, u32[]{:S(2)}) collective-permute-start(bf16[4,512,384]{2,1,0:T(8,128)(2,1)} %get-tuple-element.50), channel_id=1, source_target_pairs={{0,1},{1,0},{2,3},{3,2},{4,5},{5,4},{6,7},{7,6},{8,9},{9,8},{10,11... | collective-permute-start | bytes 4718600 | tf_op jit(solution)/shard_map/ppermute | solution.py:33
  673.5 145.8 %collective-permute-start.44 = (bf16[2,768,768]{2,1,0:T(8,128)(2,1)}, bf16[2,768,768]{2,1,0:T(8,128)(2,1)}, u32[]{:S(2)}, u32[]{:S(2)}) collective-permute-start(bf16[2,768,768]{2,1,0:T(8,128)(2,1)} %slice_bitcast_fusion.4), channel_id=1, source_target_pairs={{0,1},{1,0},{2,3},{3,2},{4,5},{5,4},{6,7},{7,6},{8,9},{9,8},{10,11... | collective-permute-start | bytes 7077896 | tf_op jit(solution)/shard_map/ppermute | solution.py:33
  676.8 146.3 %collective-permute-start.49 = (bf16[2,768,768]{2,1,0:T(8,128)(2,1)}, bf16[2,768,768]{2,1,0:T(8,128)(2,1)}, u32[]{:S(2)}, u32[]{:S(2)}) collective-permute-start(bf16[2,768,768]{2,1,0:T(8,128)(2,1)} %slice_bitcast_fusion.1), channel_id=1, source_target_pairs={{0,1},{1,0},{2,3},{3,2},{4,5},{5,4},{6,7},{7,6},{8,9},{9,8},{10,11... | collective-permute-start | bytes 7077896 | tf_op jit(solution)/shard_map/ppermute | solution.py:33
  693.7 134.9 %collective-permute-start.24 = (bf16[2,768,768]{2,1,0:T(8,128)(2,1)}, bf16[2,768,768]{2,1,0:T(8,128)(2,1)}, u32[]{:S(2)}, u32[]{:S(2)}) collective-permute-start(bf16[2,768,768]{2,1,0:T(8,128)(2,1)} %slice_bitcast_fusion.16), channel_id=1, source_target_pairs={{0,1},{1,0},{2,3},{3,2},{4,5},{5,4},{6,7},{7,6},{8,9},{9,8},{10,11... | collective-permute-start | bytes 7077896 | tf_op jit(solution)/shard_map/ppermute | solution.py:33
  778.2 54.6 %collective-permute-start.17 = (bf16[4,512,384]{2,1,0:T(8,128)(2,1)}, bf16[4,512,384]{2,1,0:T(8,128)(2,1)}, u32[]{:S(2)}, u32[]{:S(2)}) collective-permute-start(bf16[4,512,384]{2,1,0:T(8,128)(2,1)} %get-tuple-element.54), channel_id=1, source_target_pairs={{0,1},{1,0},{2,3},{3,2},{4,5},{5,4},{6,7},{7,6},{8,9},{9,8},{10,11... | collective-permute-start | bytes 4718600 | tf_op jit(solution)/shard_map/ppermute | solution.py:33
  795.3 110.8 %collective-permute-start.29 = (bf16[2,768,768]{2,1,0:T(8,128)(2,1)}, bf16[2,768,768]{2,1,0:T(8,128)(2,1)}, u32[]{:S(2)}, u32[]{:S(2)}) collective-permute-start(bf16[2,768,768]{2,1,0:T(8,128)(2,1)} %slice_bitcast_fusion.13), channel_id=1, source_target_pairs={{0,1},{1,0},{2,3},{3,2},{4,5},{5,4},{6,7},{7,6},{8,9},{9,8},{10,11... | collective-permute-start | bytes 7077896 | tf_op jit(solution)/shard_map/ppermute | solution.py:33
  819.4 94.7 %collective-permute-start.34 = (bf16[2,768,768]{2,1,0:T(8,128)(2,1)}, bf16[2,768,768]{2,1,0:T(8,128)(2,1)}, u32[]{:S(2)}, u32[]{:S(2)}) collective-permute-start(bf16[2,768,768]{2,1,0:T(8,128)(2,1)} %slice_bitcast_fusion.10), channel_id=1, source_target_pairs={{0,1},{1,0},{2,3},{3,2},{4,5},{5,4},{6,7},{7,6},{8,9},{9,8},{10,11... | collective-permute-start | bytes 7077896 | tf_op jit(solution)/shard_map/ppermute | solution.py:33
  823.1 94.5 %collective-permute-start.39 = (bf16[2,768,768]{2,1,0:T(8,128)(2,1)}, bf16[2,768,768]{2,1,0:T(8,128)(2,1)}, u32[]{:S(2)}, u32[]{:S(2)}) collective-permute-start(bf16[2,768,768]{2,1,0:T(8,128)(2,1)} %slice_bitcast_fusion.7), channel_id=1, source_target_pairs={{0,1},{1,0},{2,3},{3,2},{4,5},{5,4},{6,7},{7,6},{8,9},{9,8},{10,11... | collective-permute-start | bytes 7077896 | tf_op jit(solution)/shard_map/ppermute | solution.py:33
  828.7 29.1 %collective-permute-start.45 = (bf16[768,768]{1,0:T(8,128)(2,1)}, bf16[768,768]{1,0:T(8,128)(2,1)}, u32[]{:S(2)}, u32[]{:S(2)}) collective-permute-start(bf16[768,768]{1,0:T(8,128)(2,1)} %fusion.153), channel_id=1, source_target_pairs={{0,2},{1,3},{2,0},{3,1},{4,6},{5,7},{6,4},{7,5},{8,10},{9,11},{10,... | collective-permute-start | bytes 3538952 | tf_op jit(solution)/shard_map/ppermute | solution.py:33
  832.8 49.6 %collective-permute-start.50 = (bf16[768,768]{1,0:T(8,128)(2,1)}, bf16[768,768]{1,0:T(8,128)(2,1)}, u32[]{:S(2)}, u32[]{:S(2)}) collective-permute-start(bf16[768,768]{1,0:T(8,128)(2,1)} %fusion.154), channel_id=1, source_target_pairs={{0,2},{1,3},{2,0},{3,1},{4,6},{5,7},{6,4},{7,5},{8,10},{9,11},{10,... | collective-permute-start | bytes 3538952 | tf_op jit(solution)/shard_map/ppermute | solution.py:33
  857.8 28.3 %collective-permute-start.61 = (bf16[1,640,384]{2,1,0:T(8,128)(2,1)}, bf16[1,640,384]{2,1,0:T(8,128)(2,1)S(1)}, u32[]{:S(2)}, u32[]{:S(2)}) collective-permute-start(bf16[1,640,384]{2,1,0:T(8,128)(2,1)} %get-tuple-element.247), channel_id=1, source_target_pairs={{0,16},{4,20},{8,24},{12,28},{16,0},{20,4},{24,8},{28,12},{1,17},{... | collective-permute-start | bytes 1474568 | tf_op jit(solution)/shard_map/ppermute | solution.py:33
  886.2 27.0 %collective-permute-start.25 = (bf16[768,768]{1,0:T(8,128)(2,1)S(1)}, bf16[768,768]{1,0:T(8,128)(2,1)S(1)}, u32[]{:S(2)}, u32[]{:S(2)}) collective-permute-start(bf16[768,768]{1,0:T(8,128)(2,1)S(1)} %copy-done.93), channel_id=1, source_target_pairs={{0,2},{1,3},{2,0},{3,1},{4,6},{5,7},{6,4},{7,5},{8,10},{9,11},{10,... | collective-permute-start | bytes 3538952 | tf_op jit(solution)/shard_map/ppermute | solution.py:33
  905.9 142.9 %collective-permute-start.18 = (bf16[2,768,768]{2,1,0:T(8,128)(2,1)}, bf16[2,768,768]{2,1,0:T(8,128)(2,1)}, u32[]{:S(2)}, u32[]{:S(2)}) collective-permute-start(bf16[2,768,768]{2,1,0:T(8,128)(2,1)} %slice_bitcast_fusion.19), channel_id=1, source_target_pairs={{0,1},{1,0},{2,3},{3,2},{4,5},{5,4},{6,7},{7,6},{8,9},{9,8},{10,11... | collective-permute-start | bytes 7077896 | tf_op jit(solution)/shard_map/ppermute | solution.py:33
  914.0 74.8 %collective-permute-start.62 = (bf16[2,640,384]{2,1,0:T(8,128)(2,1)S(1)}, bf16[2,640,384]{2,1,0:T(8,128)(2,1)S(1)}, u32[]{:S(2)}, u32[]{:S(2)}) collective-permute-start(bf16[2,640,384]{2,1,0:T(8,128)(2,1)S(1)} %get-tuple-element.251), channel_id=1, source_target_pairs={{0,8},{4,12},{8,0},{12,4},{16,24},{20,28},{24,16},{28,20},{1,9},{5... | collective-permute-start | bytes 2949128 | tf_op jit(solution)/shard_map/ppermute | solution.py:33
  917.6 90.2 %collective-permute-start.67 = (bf16[2,640,384]{2,1,0:T(8,128)(2,1)S(1)}, bf16[2,640,384]{2,1,0:T(8,128)(2,1)S(1)}, u32[]{:S(2)}, u32[]{:S(2)}) collective-permute-start(bf16[2,640,384]{2,1,0:T(8,128)(2,1)S(1)} %get-tuple-element.245), channel_id=1, source_target_pairs={{0,8},{4,12},{8,0},{12,4},{16,24},{20,28},{24,16},{28,20},{1,9},{5... | collective-permute-start | bytes 2949128 | tf_op jit(solution)/shard_map/ppermute | solution.py:33
  924.4 47.8 %collective-permute-start.26 = (bf16[4,96,768]{2,1,0:T(8,128)(2,1)S(1)}, bf16[4,96,768]{2,1,0:T(8,128)(2,1)S(1)}, u32[]{:S(2)}, u32[]{:S(2)}) collective-permute-start(bf16[4,96,768]{2,1,0:T(8,128)(2,1)S(1)} %dynamic-slice_bitcast_fusion.7), channel_id=1, source_target_pairs={{0,4},{4,0},{8,12},{12,8},{16,20},{20,16},{24,28},{28,24},{1,5},{5... | collective-permute-start | bytes 1769480 | tf_op jit(solution)/shard_map/ppermute | solution.py:33
  935.0 28.7 %collective-permute-start.47 = (bf16[2,96,768]{2,1,0:T(8,128)(2,1)S(1)}, bf16[2,96,768]{2,1,0:T(8,128)(2,1)S(1)}, u32[]{:S(2)}, u32[]{:S(2)}) collective-permute-start(bf16[2,96,768]{2,1,0:T(8,128)(2,1)S(1)} %dynamic-slice_bitcast_fusion.10), channel_id=1, source_target_pairs={{0,8},{4,12},{8,0},{12,4},{16,24},{20,28},{24,16},{28,20},{1,9},{5... | collective-permute-start | bytes 884744 | tf_op jit(solution)/shard_map/ppermute | solution.py:33
  970.4 60.2 %collective-permute-start.30 = (bf16[768,768]{1,0:T(8,128)(2,1)}, bf16[768,768]{1,0:T(8,128)(2,1)}, u32[]{:S(2)}, u32[]{:S(2)}) collective-permute-start(bf16[768,768]{1,0:T(8,128)(2,1)} %fusion.150), channel_id=1, source_target_pairs={{0,2},{1,3},{2,0},{3,1},{4,6},{5,7},{6,4},{7,5},{8,10},{9,11},{10,... | collective-permute-start | bytes 3538952 | tf_op jit(solution)/shard_map/ppermute | solution.py:33
  987.5 46.4 %collective-permute-start.35 = (bf16[768,768]{1,0:T(8,128)(2,1)}, bf16[768,768]{1,0:T(8,128)(2,1)}, u32[]{:S(2)}, u32[]{:S(2)}) collective-permute-start(bf16[768,768]{1,0:T(8,128)(2,1)} %fusion.151), channel_id=1, source_target_pairs={{0,2},{1,3},{2,0},{3,1},{4,6},{5,7},{6,4},{7,5},{8,10},{9,11},{10,... | collective-permute-start | bytes 3538952 | tf_op jit(solution)/shard_map/ppermute | solution.py:33
  1007.9 38.5 %collective-permute-start.40 = (bf16[768,768]{1,0:T(8,128)(2,1)}, bf16[768,768]{1,0:T(8,128)(2,1)}, u32[]{:S(2)}, u32[]{:S(2)}) collective-permute-start(bf16[768,768]{1,0:T(8,128)(2,1)} %fusion.152), channel_id=1, source_target_pairs={{0,2},{1,3},{2,0},{3,1},{4,6},{5,7},{6,4},{7,5},{8,10},{9,11},{10,... | collective-permute-start | bytes 3538952 | tf_op jit(solution)/shard_map/ppermute | solution.py:33
  1027.0 162.3 %collective-permute-start.63 = (bf16[4,640,384]{2,1,0:T(8,128)(2,1)}, bf16[4,640,384]{2,1,0:T(8,128)(2,1)}, u32[]{:S(2)}, u32[]{:S(2)}) collective-permute-start(bf16[4,640,384]{2,1,0:T(8,128)(2,1)} %bitcast.250), channel_id=1, source_target_pairs={{0,4},{4,0},{8,12},{12,8},{16,20},{20,16},{24,28},{28,24},{1,5},{5... | collective-permute-start | bytes 5898248 | tf_op jit(solution)/shard_map/ppermute | solution.py:33
  1030.6 144.3 %collective-permute-start.68 = (bf16[4,640,384]{2,1,0:T(8,128)(2,1)}, bf16[4,640,384]{2,1,0:T(8,128)(2,1)S(1)}, u32[]{:S(2)}, u32[]{:S(2)}) collective-permute-start(bf16[4,640,384]{2,1,0:T(8,128)(2,1)} %bitcast.262), channel_id=1, source_target_pairs={{0,4},{4,0},{8,12},{12,8},{16,20},{20,16},{24,28},{28,24},{1,5},{5... | collective-permute-start | bytes 5898248 | tf_op jit(solution)/shard_map/ppermute | solution.py:33
  1033.9 93.9 %collective-permute-start.31 = (bf16[4,96,768]{2,1,0:T(8,128)(2,1)S(1)}, bf16[4,96,768]{2,1,0:T(8,128)(2,1)S(1)}, u32[]{:S(2)}, u32[]{:S(2)}) collective-permute-start(bf16[4,96,768]{2,1,0:T(8,128)(2,1)S(1)} %dynamic-slice_bitcast_fusion.6), channel_id=1, source_target_pairs={{0,4},{4,0},{8,12},{12,8},{16,20},{20,16},{24,28},{28,24},{1,5},{5... | collective-permute-start | bytes 1769480 | tf_op jit(solution)/shard_map/ppermute | solution.py:33
  1046.4 94.1 %collective-permute-start.36 = (bf16[4,96,768]{2,1,0:T(8,128)(2,1)S(1)}, bf16[4,96,768]{2,1,0:T(8,128)(2,1)S(1)}, u32[]{:S(2)}, u32[]{:S(2)}) collective-permute-start(bf16[4,96,768]{2,1,0:T(8,128)(2,1)S(1)} %dynamic-slice_bitcast_fusion.5), channel_id=1, source_target_pairs={{0,4},{4,0},{8,12},{12,8},{16,20},{20,16},{24,28},{28,24},{1,5},{5... | collective-permute-start | bytes 1769480 | tf_op jit(solution)/shard_map/ppermute | solution.py:33
  1048.8 98.5 %collective-permute-start.41 = (bf16[4,96,768]{2,1,0:T(8,128)(2,1)S(1)}, bf16[4,96,768]{2,1,0:T(8,128)(2,1)S(1)}, u32[]{:S(2)}, u32[]{:S(2)}) collective-permute-start(bf16[4,96,768]{2,1,0:T(8,128)(2,1)S(1)} %dynamic-slice_bitcast_fusion.4), channel_id=1, source_target_pairs={{0,4},{4,0},{8,12},{12,8},{16,20},{20,16},{24,28},{28,24},{1,5},{5... | collective-permute-start | bytes 1769480 | tf_op jit(solution)/shard_map/ppermute | solution.py:33
  1127.9 61.1 %collective-permute-start.19 = (bf16[768,768]{1,0:T(8,128)(2,1)S(1)}, bf16[768,768]{1,0:T(8,128)(2,1)S(1)}, u32[]{:S(2)}, u32[]{:S(2)}) collective-permute-start(bf16[768,768]{1,0:T(8,128)(2,1)S(1)} %fusion.148), channel_id=1, source_target_pairs={{0,2},{1,3},{2,0},{3,1},{4,6},{5,7},{6,4},{7,5},{8,10},{9,11},{10,... | collective-permute-start | bytes 3538952 | tf_op jit(solution)/shard_map/ppermute | solution.py:33
  1170.5 35.6 %collective-permute-start.43 = (bf16[1,96,768]{2,1,0:T(8,128)(2,1)S(1)}, bf16[1,96,768]{2,1,0:T(8,128)(2,1)S(1)}, u32[]{:S(2)}, u32[]{:S(2)}) collective-permute-start(bf16[1,96,768]{2,1,0:T(8,128)(2,1)S(1)} %constant_dynamic-slice_fusion.5), channel_id=1, source_target_pairs={{0,16},{4,20},{8,24},{12,28},{16,0},{20,4},{24,8},{28,12},{1,17},{... | collective-permute-start | bytes 442376 | tf_op jit(solution)/shard_map/ppermute | solution.py:33
  1188.8 25.8 %collective-permute-start.69 = (bf16[2,1008,384]{2,1,0:T(8,128)(2,1)S(1)}, bf16[2,1008,384]{2,1,0:T(8,128)(2,1)S(1)}, u32[]{:S(2)}, u32[]{:S(2)}) collective-permute-start(bf16[2,1008,384]{2,1,0:T(8,128)(2,1)S(1)} %dynamic-slice_bitcast_fusion), channel_id=1, source_target_pairs={{0,1},{1,0},{2,3},{3,2},{4,5},{5,4},{6,7},{7,6},{8,9},{9,8},{10,11... | collective-permute-start | bytes 4644872 | tf_op jit(solution)/shard_map/ppermute | solution.py:33
  1218.6 34.7 %collective-permute-start.65 = (bf16[1,1008,384]{2,1,0:T(8,128)(2,1)}, bf16[1,1008,384]{2,1,0:T(8,128)(2,1)}, u32[]{:S(2)}, u32[]{:S(2)}) collective-permute-start(bf16[1,1008,384]{2,1,0:T(8,128)(2,1)} %constant_dynamic-slice_fusion.2), channel_id=1, source_target_pairs={{0,2},{1,3},{2,0},{3,1},{4,6},{5,7},{6,4},{7,5},{8,10},{9,11},{10,... | collective-permute-start | bytes 2322440 | tf_op jit(solution)/shard_map/ppermute | solution.py:33
  1239.9 70.4 %collective-permute-start.73 = (bf16[1,1008,384]{2,1,0:T(8,128)(2,1)}, bf16[1,1008,384]{2,1,0:T(8,128)(2,1)}, u32[]{:S(2)}, u32[]{:S(2)}) collective-permute-start(bf16[1,1008,384]{2,1,0:T(8,128)(2,1)} %get-tuple-element.211), channel_id=1, source_target_pairs={{0,2},{1,3},{2,0},{3,1},{4,6},{5,7},{6,4},{7,5},{8,10},{9,11},{10,... | collective-permute-start | bytes 2322440 | tf_op jit(solution)/shard_map/ppermute | solution.py:33
  (264 other events, 2951.3 us)

commit v2 on v1

--- a/solution.py
+++ b/solution.py
@@ -573,6 +573,347 @@
     return full.reshape(units, 4, 8 * slim, columns), mine
 
 
+def end_kernel(kinds, *refs):
+    units = len(kinds)
+    lefts = sorted({left for kind in kinds for left, unused in kind})
+    rights = sorted({right for kind in kinds for unused, right in kind})
+    count = len(lefts) + len(rights)
+    inputs = refs[:count]
+    left_refs = {name: inputs[i] for i, name in enumerate(lefts)}
+    right_refs = {name: inputs[len(lefts) + i] for i, name in enumerate(rights)}
+    ids_ref, rows_ref, head_ref, small_ref = refs[count : count + 4]
+    out_ref, table_out, small_out, square_out, c_in, y_in = refs[count + 4 : count + 10]
+    (
+        left_vm, right_a, right_b, right_c, right_d, left_t, send_c, stage, held, x_in, z1_in, z2_in,
+        gathered, table_vm, table_c, table_y, small_all, small_next, square_all, square_next,
+        load_sem, stage_sem, w_send, w_recv, l_send, l_recv, t_send, t_recv, s_send, s_recv, own_sem,
+    ) = refs[count + 10 :]
+    wide, narrow = lax.axis_index("wide"), lax.axis_index("narrow")
+    z2, z1, x = wide // 4, wide // 2 % 2, wide % 2
+    y, core = narrow // 2, narrow % 2
+
+    def flipped(index, bits, r):
+        for bit in bits:
+            if r & bit:
+                index = index + bit - 2 * bit * (index // bit % 2)
+        return index
+
+    wide_peer = lambda r: (flipped(wide, (1, 2, 4), r), narrow)
+    narrow_peer = lambda g: (wide, flipped(narrow, (1, 2), g))
+    greet([wide_peer(r) for r in range(1, 8)] + [narrow_peer(g) for g in range(1, 4)])
+
+    slim, columns = out_ref.shape[1:]
+    width = 8 * slim
+
+    def small_copy(base, src, dst, index, peer):
+        return remote(src, dst, s_send.at[base + index], s_recv.at[base + index], peer)
+
+    def spread(base, value_ref, all_ref):
+        all_ref[0] = value_ref[...]
+        for r in range(1, 8):
+            small_copy(base, all_ref.at[0], all_ref.at[r], r, wide_peer(r)).start()
+
+    def spread_next(base, all_ref, next_ref):
+        for r in range(1, 8):
+            small_copy(base, all_ref.at[0], all_ref.at[r], r, wide_peer(r)).wait()
+        next_ref[0] = jnp.sum(all_ref[...], axis=0)
+        for g in range(1, 4):
+            small_copy(base + 7, next_ref.at[0], next_ref.at[g], g, narrow_peer(g)).start()
+
+    def collect(base, next_ref, result_ref):
+        for g in range(1, 4):
+            small_copy(base + 7, next_ref.at[0], next_ref.at[g], g, narrow_peer(g)).wait()
+        result_ref[...] = jnp.sum(next_ref[...], axis=0)
+
+    def row_copy(r):
+        bit = 1 if r % 2 else (2 if r % 4 else 4)
+        return remote(gathered.at[r - bit], gathered.at[r], l_send.at[r], l_recv.at[r], wide_peer(bit))
+
+    right_space = {}
+
+    def loads(j):
+        copies = []
+        for at, (left, right) in enumerate(kinds[j]):
+            src = left_refs[left]
+            copies.append((src, left_vm.at[at, : src.shape[0]]))
+            src = right_refs[right]
+            cols = src.shape[2]
+            if cols == columns:
+                space = right_d
+            else:
+                space = (right_a, right_b, right_c)[at]
+            copies.append((src, space.at[:, : src.shape[1]]))
+        return [
+            pltpu.make_async_copy(src, dst, load_sem.at[i]) for i, (src, dst) in enumerate(copies)
+        ]
+
+    def product(j, group):
+        parts = []
+        for at, (left, right) in enumerate(kinds[j]):
+            rows = left_refs[left].shape[0]
+            cols = right_refs[right].shape[2]
+            space = right_d if cols == columns else (right_a, right_b, right_c)[at]
+            parts.append(dot(left_t[at, :, :rows], space[group, :rows, :], 1, 0).astype(bf16))
+        whole = parts[0] if len(parts) == 1 else jnp.concatenate(parts, axis=1)
+        return whole
+
+    def w_copy(j, hop_at):
+        slot = j % 3
+        if hop_at == 0:
+            src, dst, peer = send_c, c_in.at[j], narrow_peer(1)
+        elif hop_at == 1:
+            src, dst, peer = held.at[slot, 1], y_in.at[j], narrow_peer(2)
+        elif hop_at == 2:
+            src, dst, peer = held.at[slot, 0, :, :, 1 - x], x_in.at[j], wide_peer(1)
+        elif hop_at == 3:
+            src, dst, peer = x_in.at[j, :, 1 - z1], z1_in.at[j], wide_peer(2)
+        else:
+            src, dst, peer = z1_in.at[j, 1 - z2], z2_in.at[j], wide_peer(4)
+        return remote(src, dst, w_send.at[j, hop_at], w_recv.at[j, hop_at], peer)
+
+    def multiply(j):
+        for copy in loads(j):
+            copy.wait()
+        for at, (left, unused) in enumerate(kinds[j]):
+            rows = left_refs[left].shape[0]
+            left_t[at, :, :rows] = left_vm[at, :rows, :].T
+        if j > 0:
+            w_copy(j - 1, 0).wait_send()
+        for side in range(2):
+            send_c[side] = product(j, 2 * side + 1).reshape(send_c.shape[1:])
+        w_copy(j, 0).start()
+        for side in range(2):
+            held[j % 3, side] = product(j, 2 * side).reshape(held.shape[2:])
+        if j + 1 < units:
+            for copy in loads(j + 1):
+                copy.start()
+
+    def added(a, b):
+        return (a.astype(f32) + b.astype(f32)).astype(bf16)
+
+    def after_core(j):
+        w_copy(j, 0).wait_recv()
+        copy = pltpu.make_async_copy(c_in.at[j], stage, stage_sem.at[0])
+        copy.start()
+        copy.wait()
+        for side in (1, 0):
+            held[j % 3, side] = added(held[j % 3, side], stage[side])
+            if side == 1:
+                w_copy(j, 1).start()
+
+    def after_y(j):
+        w_copy(j, 1).wait()
+        copy = pltpu.make_async_copy(y_in.at[j], stage.at[0], stage_sem.at[0])
+        copy.start()
+        copy.wait()
+        held[j % 3, 0] = added(held[j % 3, 0], stage[0])
+        w_copy(j, 2).start()
+
+    def after_x(j):
+        w_copy(j, 2).wait()
+        x_in[j] = added(x_in[j], held[j % 3, 0, :, :, x])
+        w_copy(j, 3).start()
+
+    def after_z1(j):
+        w_copy(j, 3).wait()
+        z1_in[j] = added(z1_in[j], x_in[j, :, z1])
+        w_copy(j, 4).start()
+
+    def after_z2(j):
+        w_copy(j, 4).wait()
+        total = z2_in[j].astype(f32) + z1_in[j, z2].astype(f32)
+        out_ref[j] = total
+        note(total)
+
+    def note(values):
+        rows = values.shape[0]
+        squares = jnp.sum((values * values).reshape(rows // 8, 8, values.shape[1]), axis=0)
+        for at in range(0, values.shape[1], 128):
+            square_all[0] += squares[:, at : at + 128]
+
+    quarter = table_vm.shape[1]
+    tokens = gathered.shape[1]
+    step = 512
+
+    def scatter_rows():
+        def chunk(k, unused):
+            per = quarter // step
+            at = pl.ds(pl.multiple_of(k % per * step, step), step)
+            slot = lax.broadcasted_iota(jnp.int32, (step, 1), 0) + k * step
+
+            def one(r, total):
+                hot = (slot == ids_ref[r]).astype(f32).astype(bf16)
+                return total + dot(hot, gathered[r], 1, 0)
+
+            total = lax.fori_loop(0, 8, one, table_vm[k // per, at, :].astype(f32))
+            table_vm[k // per, at, :] = total.astype(bf16)
+            return unused
+
+        lax.fori_loop(0, 4 * quarter // step, chunk, 0)
+
+    def t_copy(at):
+        if at == 0:
+            src, dst, peer = table_vm.at[1 - core], table_c.at[0], narrow_peer(1)
+        elif at == 1:
+            src, dst, peer = table_vm.at[3 - core], table_c.at[1], narrow_peer(1)
+        elif at == 2:
+            src, dst, peer = table_vm.at[2 * (1 - y) + core], table_y, narrow_peer(2)
+        elif at == 3:
+            src, dst, peer = table_vm.at[narrow], table_out.at[narrow], narrow_peer(2)
+        elif at == 4:
+            src, dst, peer = table_vm.at[narrow], table_out.at[narrow], narrow_peer(1)
+        else:
+            there = 2 * (1 - y) + core
+            src, dst, peer = table_out.at[there], table_out.at[there], narrow_peer(1)
+        return remote(src, dst, t_send.at[at], t_recv.at[at], peer)
+
+    def own_quarter():
+        return pltpu.make_async_copy(table_vm.at[narrow], table_out.at[narrow], own_sem.at[0])
+
+    def head_load():
+        return pltpu.make_async_copy(head_ref, table_vm, own_sem.at[1])
+
+    def rows_load():
+        return pltpu.make_async_copy(rows_ref, gathered.at[0], own_sem.at[2])
+
+    rows_load().start()
+    head_load().start()
+    for copy in loads(0):
+        copy.start()
+    square_all[0] = jnp.zeros_like(square_all[0])
+    spread(0, small_ref, small_all)
+    rows_load().wait()
+    for r in (1, 4, 2):
+        row_copy(r).start()
+
+    def extra(t):
+        if t == 0:
+            spread_next(0, small_all, small_next)
+        elif t == 1:
+            collect(0, small_next, small_out)
+            row_copy(2).wait_recv()
+            row_copy(3).start()
+            row_copy(4).wait_recv()
+            row_copy(6).start()
+            row_copy(5).start()
+        elif t == 2:
+            row_copy(6).wait_recv()
+            row_copy(7).start()
+            head_load().wait()
+        elif t == 4:
+            for r in (1, 3, 5, 7):
+                row_copy(r).wait_recv()
+            scatter_rows()
+            t_copy(0).start()
+            t_copy(1).start()
+        elif t == 5:
+            for side in range(2):
+                t_copy(side).wait_recv()
+            there = 2 * (1 - y) + core
+            table_vm[there] = added(table_vm[there], table_c[1 - y])
+            t_copy(2).start()
+            table_vm[narrow] = added(table_vm[narrow], table_c[y])
+        elif t == 7:
+            t_copy(2).wait()
+            part = added(table_vm[narrow], table_y[...])
+            table_vm[narrow] = part
+            t_copy(3).start()
+            t_copy(4).start()
+            own_quarter().start()
+            note(part.astype(f32))
+
+    for t in range(units + 4):
+        if t < units:
+            multiply(t)
+            after_core(t)
+        extra(t)
+        for lag, act in ((1, after_y), (2, after_x), (3, after_z1), (4, after_z2)):
+            if 0 <= t - lag < units:
+                act(t - lag)
+    for r in range(1, 8):
+        small_copy(16, square_all.at[0], square_all.at[r], r, wide_peer(r)).start()
+    spread_next(16, square_all, square_next)
+    t_copy(3).wait_recv()
+    t_copy(5).start()
+    collect(16, square_next, square_out)
+    t_copy(4).wait_recv()
+    t_copy(5).wait_recv()
+    for at in (0, 1, 3, 4, 5):
+        t_copy(at).wait_send()
+    own_quarter().wait()
+    w_copy(units - 1, 0).wait_send()
+    for r in range(1, 8):
+        row_copy(r).wait_send()
+
+
+def end_phase(kinds, lefts, rights, ids, rows, head, small):
+    units = len(kinds)
+    names = sorted({left for kind in kinds for left, unused in kind})
+    right_names = sorted({right for kind in kinds for unused, right in kind})
+    tokens, width = rows.shape
+    slim = width // 8
+    quarter = head.shape[1]
+    most = max(value.shape[0] for value in lefts.values())
+    any_space = pl.BlockSpec(memory_space=pl.ANY)
+    vmem = pl.BlockSpec(memory_space=pltpu.VMEM)
+    dma = pltpu.SemaphoreType.DMA
+    narrow_cols = [rights[right].shape[2] for unused, right in max(kinds, key=len)]
+    args = [lefts[name] for name in names] + [rights[name] for name in right_names]
+    outs = pl.pallas_call(
+        functools.partial(end_kernel, kinds),
+        in_specs=[any_space] * len(args) + [vmem, any_space, any_space, vmem],
+        out_specs=[vmem, any_space, vmem, vmem, any_space, any_space],
+        out_shape=[
+            jax.ShapeDtypeStruct((units, slim, width), f32),
+            jax.ShapeDtypeStruct((4, quarter, width), bf16),
+            jax.ShapeDtypeStruct(small.shape, f32),
+            jax.ShapeDtypeStruct((8, 128), f32),
+            jax.ShapeDtypeStruct((units, 2, 2, 2, 2, slim, width), bf16),
+            jax.ShapeDtypeStruct((units, 2, 2, 2, slim, width), bf16),
+        ],
+        scratch_shapes=[
+            pltpu.VMEM((3, most, width), bf16),
+            pltpu.VMEM((4, most, narrow_cols[0]), bf16),
+            pltpu.VMEM((4, most, narrow_cols[1]), bf16),
+            pltpu.VMEM((4, most, narrow_cols[2]), bf16),
+            pltpu.VMEM((4, most, width), bf16),
+            pltpu.VMEM((3, width, most), bf16),
+            pltpu.VMEM((2, 2, 2, 2, slim, width), bf16),
+            pltpu.VMEM((2, 2, 2, 2, slim, width), bf16),
+            pltpu.VMEM((3, 2, 2, 2, 2, slim, width), bf16),
+            pltpu.VMEM((units, 2, 2, slim, width), bf16),
+            pltpu.VMEM((units, 2, slim, width), bf16),
+            pltpu.VMEM((units, slim, width), bf16),
+            pltpu.VMEM((8, tokens, width), bf16),
+            pltpu.VMEM((4, quarter, width), bf16),
+            pltpu.VMEM((2, quarter, width), bf16),
+            pltpu.VMEM((quarter, width), bf16),
+            pltpu.VMEM((8, *small.shape), f32),
+            pltpu.VMEM((4, *small.shape), f32),
+            pltpu.VMEM((8, 8, 128), f32),
+            pltpu.VMEM((4, 8, 128), f32),
+            dma((6,)),
+            dma((1,)),
+            dma((units, 5)),
+            dma((units, 5)),
+            dma((8,)),
+            dma((8,)),
+            dma((6,)),
+            dma((6,)),
+            dma((32,)),
+            dma((32,)),
+            dma((3,)),
+        ],
+        compiler_params=pltpu.CompilerParams(
+            collective_id=1, has_side_effects=True, vmem_limit_bytes=62 * 2**20
+        ),
+        cost_estimate=pl.CostEstimate(
+            flops=2 * 8 * tokens * 4 * quarter * width, bytes_accessed=100 * 2**20, transcendentals=0
+        ),
+    )(*args, ids, rows, head, small)
+    return outs[:4]
+
+
 def body(
     enc_ids, enc_len, tgt_ids, tgt_len, span_mask, buckets,
     attn_in, attn_out, ff_in, ff_out, table, gains, rel,
@@ -668,20 +1009,17 @@
     def attn_backward(saved, upstream, gain_row, layer, source, rel_row, causal):
         state, inverse, normed, q, kv, kv_other, mixed, lse = saved
         up = upstream.astype(bf16)
-        out_grad = outer(up, mixed)
         mixed_grad = project(up, low_out[layer]).astype(bf16)
         outs = attend_back(scal, q, kv, kv_other, mixed_grad, lse, rel_row, centre, causal)
         dq, dkv_own, dkv_other = outs[:3]
         dkv = (dkv_own + swap(dkv_other).astype(f32)).astype(bf16)
-        q_grad = outer(normed, dq)
-        kv_grad = outer(normed if source is None else source, dkv)
         normed_grad = project_back(dq, low_in[layer][:, :, :lanes])
         kv_back = project_back(dkv, low_in[layer][:, :, lanes:])
         if source is None:
             normed_grad = normed_grad + kv_back
         state_grad, gain_grad = rms_backward(state, gain_row, inverse, normed_grad)
-        grads = jnp.concatenate([q_grad, kv_grad, out_grad], axis=2).astype(bf16)
-        return (upstream + state_grad, gain_grad, grads, kv_back, outs[3] if rel_row is not None else None)
+        pieces = ((normed, dq), (normed if source is None else source, dkv), (up, mixed))
+        return (upstream + state_grad, gain_grad, pieces, kv_back, outs[3] if rel_row is not None else None)
 
     def ff_forward(state, gain_row, layer):
         normed, inverse = rms_forward(state, gain_row)
@@ -692,16 +1030,18 @@
     def ff_backward(saved, upstream, gain_row, layer):
         state, inverse, normed, pre, hidden = saved
         up = upstream.astype(bf16)
-        out_grad = outer(up, hidden).astype(bf16)
         hidden_grad = project(up, low_down[layer]).astype(bf16).astype(f32)
         unused, gelu_back = jax.vjp(jax.nn.gelu, pre)
         pre_grad = gelu_back(hidden_grad)[0].astype(bf16)
-        in_grad = outer(normed, pre_grad).astype(bf16)
         normed_grad = project_back(pre_grad, low_up[layer])
         state_grad, gain_grad = rms_backward(state, gain_row, inverse, normed_grad)
-        return (upstream + state_grad, gain_grad, in_grad, out_grad)
-
-    def scatter(grad):
+        return (upstream + state_grad, gain_grad, ((normed, pre_grad),), ((up, hidden),))
+
+    def scatter(pieces):
+        grad = jnp.concatenate([outer(*piece) for piece in pieces], axis=2).astype(bf16)
+        return spread(grad)
+
+    def spread(grad):
         pairs = grad.reshape(2, 2, width, -1)
         across = pairs[:, 0].astype(f32) + swap(pairs[:, 1]).astype(f32)
         column = across[0] + hop(across[1].astype(bf16), "narrow", 2).astype(f32)
@@ -769,31 +1109,6 @@
     enc_grad, gain_grads[0], attn0, unused, drel_enc = attn_backward(
         saved_a, enc_grad, gains_full[0], 0, None, rel_rows[0], 0
     )
-    reduced = [scatter(grad) for grad in (attn0, attn1, attn2, up0, down0, up1, down1)]
-
-    row_grads = jnp.concatenate([enc_grad, dec_grad], axis=0).astype(bf16)
-    padded = -(-vocab // 64) * 64
-    slots = jnp.arange(padded)
-    local = jnp.where(held, local, -1).reshape(-1, 2, local.shape[1])
-    halves, part_grads = [], []
-    half = width // 2
-    for start in (0, half):
-        rows = row_grads[None, :, start : start + half]
-        for bit in list(bits_down("wide"))[:-1]:
-            rows = jnp.stack([rows, hop(rows, "wide", bit)], axis=1)
-            rows = rows.reshape(-1, *rows.shape[2:])
-        far = hop(rows, "wide", 1)
-        partial = dot(logit_grad, final_all[:, start : start + half], 0, 0)
-        partial = jnp.pad(partial, ((0, padded - vocab), (0, 0)))
-        for at, values in ((local[:, 0], rows), (local[:, 1], far)):
-            token_hot = (slots[:, None] == at.reshape(-1)[None, :]).astype(bf16)
-            partial = partial + dot(token_hot, values.reshape(-1, half), 1, 0)
-        quarters = partial.astype(bf16).reshape(narrow_size, padded // narrow_size, half)
-        part = scatter_sorted(quarters, "narrow").astype(bf16)
-        part_grads.append(part.astype(f32))
-        halves.append(gather_sorted(part, "narrow").reshape(padded, half)[:vocab])
-    table_grad = jnp.concatenate(halves, axis=1).astype(f32)
-
     length = onehot_rev.shape[0]
     rel_grad = jnp.stack(
         [
@@ -803,11 +1118,70 @@
     )
     rel_grad = rel_grad.reshape(2, narrow_size, heads_here, -1)[:, groups]
     rel_grad = rel_grad.reshape(2, narrow_size * heads_here, -1)
-    gain_total, rel_total, loss_sum = lax.psum(
-        (jnp.stack(gain_grads), rel_grad, loss_part), ("wide", "narrow")
-    )
-    squares = sum(jnp.sum(grad * grad) for grad in reduced + part_grads)
-    square_sum = lax.psum(squares, ("wide", "narrow"))
+    row_grads = jnp.concatenate([enc_grad, dec_grad], axis=0).astype(bf16)
+    local = jnp.where(held, local, -1)
+    if wide_size == 8 and narrow_size == 4:
+        order = (up1, down1, attn2, attn1, up0, down0, attn0)
+        kinds, lefts, rights = [], {}, {}
+        names = {}
+        for unit in order:
+            kind = []
+            for left, right in unit:
+                name = names.setdefault(id(left), "l%02d" % len(names))
+                lefts[name] = left
+                rights["r%02d" % len(rights)] = right
+                kind.append((name, "r%02d" % (len(rights) - 1)))
+            kinds.append(tuple(kind))
+        quarter = -(-vocab // 2048) * 512
+        head_part = dot(logit_grad, final_all, 0, 0).astype(bf16)
+        head_part = jnp.pad(head_part, ((0, 4 * quarter - vocab), (0, 0)))
+        flat = jnp.concatenate(
+            [jnp.stack(gain_grads).reshape(-1), rel_grad.reshape(-1), loss_part[None]]
+        )
+        small_rows = -(-flat.size // 1024) * 8
+        small_in = jnp.pad(flat, (0, small_rows * 128 - flat.size)).reshape(small_rows, 128)
+        summed, table_grad, small_sum, square_rows = end_phase(
+            tuple(kinds), lefts, rights, local[:, None, :], row_grads,
+            head_part.reshape(4, quarter, width), small_in,
+        )
+        reduced = [summed[i] for i in (6, 3, 2, 4, 5, 0, 1)]
+        table_grad = table_grad.reshape(4 * quarter, width)[:vocab].astype(f32)
+        small_sum = small_sum.reshape(-1)
+        cut = 7 * width
+        gain_total = small_sum[:cut].reshape(7, width)
+        rel_total = small_sum[cut : cut + rel_grad.size].reshape(rel_grad.shape)
+        loss_sum = small_sum[cut + rel_grad.size]
+        square_sum = jnp.sum(square_rows)
+    else:
+        reduced = [scatter(grad) for grad in (attn0, attn1, attn2, up0, down0, up1, down1)]
+
+        padded = -(-vocab // 64) * 64
+        slots = jnp.arange(padded)
+        local = local.reshape(-1, 2, local.shape[1])
+        halves, part_grads = [], []
+        half = width // 2
+        for start in (0, half):
+            rows = row_grads[None, :, start : start + half]
+            for bit in list(bits_down("wide"))[:-1]:
+                rows = jnp.stack([rows, hop(rows, "wide", bit)], axis=1)
+                rows = rows.reshape(-1, *rows.shape[2:])
+            far = hop(rows, "wide", 1)
+            partial = dot(logit_grad, final_all[:, start : start + half], 0, 0)
+            partial = jnp.pad(partial, ((0, padded - vocab), (0, 0)))
+            for at, values in ((local[:, 0], rows), (local[:, 1], far)):
+                token_hot = (slots[:, None] == at.reshape(-1)[None, :]).astype(bf16)
+                partial = partial + dot(token_hot, values.reshape(-1, half), 1, 0)
+            quarters = partial.astype(bf16).reshape(narrow_size, padded // narrow_size, half)
+            part = scatter_sorted(quarters, "narrow").astype(bf16)
+            part_grads.append(part.astype(f32))
+            halves.append(gather_sorted(part, "narrow").reshape(padded, half)[:vocab])
+        table_grad = jnp.concatenate(halves, axis=1).astype(f32)
+
+        gain_total, rel_total, loss_sum = lax.psum(
+            (jnp.stack(gain_grads), rel_grad, loss_part), ("wide", "narrow")
+        )
+        squares = sum(jnp.sum(grad * grad) for grad in reduced + part_grads)
+        square_sum = lax.psum(squares, ("wide", "narrow"))
     square_sum = square_sum + jnp.sum(gain_total * gain_total) + jnp.sum(rel_total * rel_total)
     gain_mine = lax.dynamic_slice_in_dim(gain_total, narrow_index * lanes, lanes, 1)
     rel_mine = lax.dynamic_slice_in_dim(

time: 1370 us -> 1190 us (0.87)
  Pallas kernels: 403 us -> 753 us
  waiting for transfers between devices: 296 us -> 41.5 us
  matrix products: 227 us -> 116 us
  other arithmetic: 150 us -> 92.1 us
  blocking collectives: 50.3 us -> 5.4 us
  starting transfers between devices: 64.2 us -> 29 us
  local copies, waits for them, and re-layouts: 164 us -> 137 us
    pallas_call x0 -> x1, Pallas kernels: none -> 350 us  [end_phase(): pl.pallas_call(functools.partial(end_kernel, kinds), in_specs=[any_space]...]
    ppermute x75 -> x26, waiting for transfers between devices: 296 us -> 41.5 us  [hop(): return lax.ppermute(values, axis, [(i, i ^ bit) for i in range(size)])]
    dot_general x8 -> x3, matrix products: 93.6 us -> 35.5 us  [dot(): lax.dot_general(left, right, (((left_dim,), (right_dim,)), ((), ())), pre...]
    psum x1 -> x0, blocking collectives: 44.1 us -> none  [body(): lax.psum((jnp.stack(gain_grads), rel_grad, loss_part), ('wide', 'narrow'))]
    dot_general x13 -> x0, matrix products: 42.8 us -> none  [outer(): return jnp.einsum('rk,nrc->nkc', rows, grads, preferred_element_type=f32)]
    ppermute x75 -> x26, starting transfers between devices: 64.2 us -> 29 us  [hop(): return lax.ppermute(values, axis, [(i, i ^ bit) for i in range(size)])]
    concatenate x9 -> x0, local copies, waits for them, and re-layouts: 26.2 us -> none  [attn_backward(): grads = jnp.concatenate([q_grad, kv_grad, out_grad], axis=2).astype(bf16)]
    squeeze x32 -> x0, local copies, waits for them, and re-layouts: 21 us -> none  [the longest x7 17.9 us: scatter(): across = pairs[:, 0].astype(f32) + swap(pairs[:, 1]).astype(f32)]
  transfers between devices with their start and end apart: 75 -> 26, of which waited for: 29 -> 5; matrix products, arithmetic and copies ran while one was open for 26% -> 9% of each run, Pallas kernels for 4% -> 1%
where the time goes in v2:
time: 1190 us; the launch traced here: 1180 us
  Pallas kernels  753 us (63%)
  local copies, waits for them, and re-layouts  137 us (12%)
  matrix products  116 us (10%)
  other arithmetic  92.1 us (8%)
  waiting for transfers between devices  41.5 us (3%)
  starting transfers between devices  29 us (2%)
    pallas_call x1, Pallas kernels, end_phase(): pl.pallas_call(functools.partial(end_kernel, kinds), in_specs=[any_space]...  350 us
    pallas_call x1, Pallas kernels, start_phase(): pl.pallas_call(functools.partial(start_kernel, units, vocab), in_specs=[v...  284 us
    pallas_call x3, Pallas kernels, attend_back(): pl.pallas_call(functools.partial(backward_kernel, has_bias, causal, centr...  73.6 us
    unnamed x373, local copies, waits for them, and re-layouts  45.1 us
    pallas_call x3, Pallas kernels, attend(): pl.pallas_call(functools.partial(forward_kernel, has_bias, causal, centre...  45.1 us
    dot_general x13, matrix products, project(): return jnp.einsum('rk,nkc->nrc', rows, weights, preferred_element_type=f32)  41.7 us
    ppermute x26, waiting for transfers between devices, hop(): return lax.ppermute(values, axis, [(i, i ^ bit) for i in range(size)])  41.5 us
    dot_general x13, matrix products, project_back(): return jnp.einsum('nrc,nkc->rk', grads, weights, preferred_element_type=f32)  38.2 us
  transfers between devices with their start and end apart: 26, of which 5 were waited for; matrix products, arithmetic and copies ran while one was open for 9% of the time, Pallas kernels for 1%

profile of v2, /device:TPU:0, one launch (start us, length us, event | category | flops | bytes accessed | tf_op | source)
XLA Modules:
  0.0 1180.9 jit_solution(11300373421980277727)
XLA Ops:
  7.5 7.8 convert_element_type.241
  15.3 5.9 pad.21.table_ref
  21.2 283.8 %shard_map.505 = (bf16[7,4,2,2,2,96,768]{6,5,4,3,2,1,0:T(8,128)(2,1)}, bf16[640,768]{1,0:T(8,128)(2,1)S(1)}) custom-call(s32[1,640]{1,0:T(1,128)S(1)} %broadcast_in_dim.29.ids_ref, bf16[4096,768]{1,0:T(8,128)(2,1)} %pad.21.table_ref, bf16[7,96,768]{2,1,0:T(8,128)(2,1)S(1)} %fusion.195.shard_ref), custom_call_target="tpu_custom_call" | custom-call | flops 32212254720 | bytes 33030144 | tf_op jit(solution)/shard_map/pallas_call | solution.py:541
  306.0 5.4 all-gather.1
  312.2 22.8 %fusion.263 = (bf16[1,4,2,2,2,96,768]{6,5,4,3,2,1,0:T(8,128)(2,1)}, bf16[1,4,2,2,2,96,768]{6,5,4,3,2,1,0:T(8,128)(2,1)}, bf16[1,4,2,2,2,96,768]{6,5,4,3,2,1,0:T(...) fusion(bf16[7,4,2,2,2,96,768]{6,5,4,3,2,1,0:T(8,128)(2,1)} %get, ...), kind=kLoop, calls=%fused_computation.442 | loop fusion | bytes 66060288 | tf_op jit(solution)/shard_map/slice | solution.py:992
  343.4 25.8 %shard_map.507 = (bf16[4,512,192]{2,1,0:T(8,128)(2,1)S(1)}, f32[4,3,1,512]{3,2,1,0:T(1,128)S(1)}) custom-call(s32[2]{0:T(128)S(1)} %pad_add_fusion.1.scal, bf16[4,512,192]{2,1,0:T(8,128)(2,1)S(1)} %bitcast.501, bf16[4,512,384]{2,1,0:T(8,128)(2,1)} %fusion.65.kvo_ref, bf16[4,512,384]{2,1,0:T(8,128)(2,1)} %collective-permute-done.1.kvt_ref, ...), custom_call_target="tpu_custom_call" | custom-call | tf_op jit(solution)/shard_map/pallas_call | solution.py:190
  372.6 5.8 fusion.10
  390.6 7.4 shard_map.506
  406.0 12.0 %shard_map.508 = (bf16[4,128,192]{2,1,0:T(8,128)(2,1)S(1)}, f32[4,3,1,128]{3,2,1,0:T(1,128)S(1)}) custom-call(s32[2]{0:T(128)S(1)} %pad_add_fusion.1.scal, bf16[4,128,192]{2,1,0:T(8,128)(2,1)S(1)} %bitcast.506, bf16[4,512,384]{2,1,0:T(8,128)(2,1)} %fusion.62.kvo_ref, bf16[4,512,384]{2,1,0:T(8,128)(2,1)} %collective-permute-done.2.kvt_ref), custom_call_target="tpu_custom_call" | custom-call | tf_op jit(solution)/shard_map/pallas_call | solution.py:190
  420.6 4.7 fusion.61
  428.0 12.1 %collective-permute-done.3 = bf16[1,128,768]{2,1,0:T(8,128)(2,1)S(1)} collective-permute-done((bf16[1,128,768]{2,1,0:T(8,128)(2,1)S(1)}, bf16[1,128,768]{2,1,0:T(8,128)(2,1)S(1)}, u32[]{:S(2)}, u32[]{:S(2)}) %collective-permute-start.3) | collective-permute-done | bytes 196640 | tf_op jit(solution)/shard_map/ppermute | solution.py:33
  443.1 8.7 collective-permute-done.4
  467.1 5.9 collective-permute-done.5
  474.6 9.4 fusion.270
  484.1 4.4 exponential_reduce_fusion
  494.8 3.2 collective-permute-start.10
  528.7 12.9 %fusion.256 = f32[1024,768]{1,0:T(8,128)S(1)} fusion(bf16[4016,768]{1,0:T(8,128)(2,1)} %convert_element_type.241, f32[1024,4016]{0,1:T(8,128)} %copy-done.21, f32[1024]{0:T(1024)S(1)} %get-tuple-element.237, s32[1024]{0:T(1024)} %subtract_bitcast_fusion, f32[1024]{0:T(1024)S(1)} %get-tuple-element.299), kind=kOutput, calls=%fused_computation.437 | convolution fusion | flops 6341296128 | bytes 25776128 | tf_op jit(solution)/shard_map/dot_general | solution.py:26
  543.5 14.1 %collective-permute-done.13 = bf16[4,128,768]{2,1,0:T(8,128)(2,1)S(1)} collective-permute-done((bf16[4,128,768]{2,1,0:T(8,128)(2,1)S(1)}, bf16[4,128,768]{2,1,0:T(8,128)(2,1)S(1)}, u32[]{:S(2)}, u32[]{:S(2)}) %collective-permute-start.13) | collective-permute-done | bytes 786464 | tf_op jit(solution)/shard_map/ppermute | solution.py:33
  569.5 3.2 collective-permute-start.25
  587.4 13.2 %convolution_convert_fusion = bf16[4016,768]{1,0:T(8,128)(2,1)S(1)} fusion(bf16[1024,768]{1,0:T(8,128)(2,1)S(1)} %bitcast.561, f32[1024,4016]{0,1:T(8,128)} %copy-done.21, f32[1024]{0:T(1024)} %copy-done.127, s32[1024]{0:T(1024)} %subtract_bitcast_fusion, f32[1024]{0:T(1024)} %copy-done.128), kind=kOutput, calls=%fused_computation.21 | convolution fusion | flops 6344380416 | bytes 24203264 | tf_op jit(solution)/shard_map/dot_general | solution.py:26
  606.6 4.0 fusion.35.refs_11_
  614.7 3.2 fusion.145
  621.3 17.1 %shard_map.509 = (bf16[4,128,192]{2,1,0:T(8,128)(2,1)S(1)}, f32[4,512,384]{2,1,0:T(8,128)S(1)}, bf16[4,512,384]{2,1,0:T(8,128)(2,1)}) custom-call(s32[2]{0:T(128)S(1)} %pad_add_fusion.1.scal, bf16[4,128,192]{2,1,0:T(8,128)(2,1)S(1)} %bitcast.507, bf16[4,512,384]{2,1,0:T(8,128)(2,1)} %fusion.62.kvo_ref, bf16[4,512,384]{2,1,0:T(8,128)(2,1)} %collective-permute-done.2.kvt_ref, ...), custom_call_target="tpu_custom_call" | custom-call | tf_op jit(solution)/shard_map/pallas_call | solution.py:319
  644.5 3.2 fusion.139
  648.8 13.8 %shard_map.510 = (bf16[4,128,192]{2,1,0:T(8,128)(2,1)S(1)}, f32[4,128,384]{2,1,0:T(8,128)S(1)}, bf16[4,128,384]{2,1,0:T(8,128)(2,1)}, f32[4,3,2,8,256]{4,3,2,1,0:T(8,128)S(1)}) custom-call(s32[2]{0:T(128)S(1)} %pad_add_fusion.1.scal, bf16[4,128,192]{2,1,0:T(8,128)(2,1)S(1)} %bitcast.505, bf16[4,128,384]{2,1,0:T(8,128)(2,1)S(1)} %fusion.96.kvo_ref, ...), custom_call_target="tpu_custom_call" | custom-call | tf_op jit(solution)/shard_map/pallas_call | solution.py:319
  678.5 4.5 fusion.40
  684.3 6.1 fusion.6.refs_19_
  696.1 3.8 convolution_convert_fusion.1
  701.4 42.7 %shard_map.511 = (bf16[4,512,192]{2,1,0:T(8,128)(2,1)S(1)}, f32[4,512,384]{2,1,0:T(8,128)S(1)}, bf16[4,512,384]{2,1,0:T(8,128)(2,1)}, f32[4,3,2,8,1024]{4,3,2,1,0:T(8,128)S(1)}) custom-call(s32[2]{0:T(128)S(1)} %pad_add_fusion.1.scal, bf16[4,512,192]{2,1,0:T(8,128)(2,1)S(1)} %bitcast.502, bf16[4,512,384]{2,1,0:T(8,128)(2,1)} %fusion.65.kvo_ref, ...), custom_call_target="tpu_custom_call" | custom-call | tf_op jit(solution)/shard_map/pallas_call | solution.py:319
  755.7 5.1 fusion.55
  767.6 350.3 %shard_map.512 = (f32[7,96,768]{2,1,0:T(8,128)}, bf16[4,1024,768]{2,1,0:T(8,128)(2,1)}, f32[56,128]{1,0:T(8,128)}, f32[8,128]{1,0:T(8,128)}, bf16[7,2,2,2,2,96,7...) custom-call(bf16[128,768]{1,0:T(8,128)(2,1)} %copy-done.79, bf16[128,768]{1,0:T(8,128)(2,1)} %copy-done.80, ...), custom_call_target="tpu_custom_call" | custom-call | flops 32212254720 | bytes 104857600 | tf_op jit(solution)/shard_map/pallas_call | solution.py:862
  1146.4 28.5 %multiply_add_fusion = (f32[4016,768]{1,0:T(8,128)}, f32[4016,768]{1,0:T(8,128)}, f32[4016,768]{1,0:T(8,128)}) fusion(f32[4016,768]{1,0:T(8,128)} %param.58, f32[4016,768]{1,0:T(8,128)} %param.44, f32[4016,768]{1,0:T(8,128)} %param.51, f32[]{:T(128)S(6)} %min.3, bf16[4096,768]{1,0:T(8,128)(2,1)} %bitcast.529), kind=kLoop, calls=%fused_computation.16 | loop fusion | flops 33927168 | bytes 80191488 | tf_op jit(solution)/shard_map/add | solution.py:1222
  (666 shorter events, 223.2 us)
Async XLA Ops:
  1.4 339.9 %copy-start.122 = (s32[1024]{0:T(1024)}, s32[1024]{0:T(1024)S(1)}, u32[]{:S(2)}) copy-start(s32[1024]{0:T(1024)S(1)} %get-tuple-element.322) | copy-start | bytes 12292
  21.2 284.1 %copy-start.111 = (f32[2,32,3]{1,0,2:T(2,128)S(1)}, f32[2,32,3]{1,0,2:T(2,128)}, u32[]{:S(2)}) copy-start(f32[2,32,3]{1,0,2:T(2,128)} %param.46) | copy-start | bytes 2308
  21.2 284.6 %copy-start.96 = (f32[7,192]{1,0:T(8,128)S(1)}, f32[7,192]{1,0:T(8,128)}, u32[]{:S(2)}) copy-start(f32[7,192]{1,0:T(8,128)} %param.45) | copy-start | bytes 16132
  338.0 5.4 collective-permute-start.1
  341.1 46.1 %copy-start.46 = (pred[2047,32]{0,1:T(32,128)(4,1)}, pred[2047,32]{0,1:T(32,128)(4,1)S(1)}, u32[]{:S(2)}) copy-start(pred[2047,32]{0,1:T(32,128)(4,1)S(1)} %iota_compare_fusion.1) | copy-start | bytes 196516
  343.3 42.9 %copy-start.77 = (bf16[128,768]{1,0:T(8,128)(2,1)}, bf16[128,768]{1,0:T(8,128)(2,1)S(1)}, u32[]{:S(2)}) copy-start(bf16[128,768]{1,0:T(8,128)(2,1)S(1)} %fusion.169.refs_5_) | copy-start | bytes 589828
  384.6 21.3 %collective-permute-start.2 = (bf16[4,512,384]{2,1,0:T(8,128)(2,1)}, bf16[4,512,384]{2,1,0:T(8,128)(2,1)}, u32[]{:S(2)}, u32[]{:S(2)}) collective-permute-start(bf16[4,512,384]{2,1,0:T(8,128)(2,1)} %fusion.62.kvo_ref), channel_id=1, source_target_pairs={{0,1},{1,0},{2,3},{3,2},{4,5},{5,4},{6,7},{7,6},{8,9},{9,8},{10,11... | collective-permute-start | bytes 4718600 | tf_op jit(solution)/shard_map/ppermute | solution.py:33
  385.9 4.7 collective-permute-start
  427.9 12.2 %collective-permute-start.3 = (bf16[1,128,768]{2,1,0:T(8,128)(2,1)S(1)}, bf16[1,128,768]{2,1,0:T(8,128)(2,1)S(1)}, u32[]{:S(2)}, u32[]{:S(2)}) collective-permute-start(bf16[1,128,768]{2,1,0:T(8,128)(2,1)S(1)} %get-tuple-element.273), channel_id=1, source_target_pairs={{0,16},{4,20},{8,24},{12,28},{16,0},{20,4},{24,8},{28,12},{1,17},{... | collective-permute-start | bytes 589832 | tf_op jit(solution)/shard_map/ppermute | solution.py:33
  441.0 10.7 collective-permute-start.4
  453.9 19.0 %collective-permute-start.5 = (bf16[4,128,768]{2,1,0:T(8,128)(2,1)}, bf16[4,128,768]{2,1,0:T(8,128)(2,1)}, u32[]{:S(2)}, u32[]{:S(2)}) collective-permute-start(bf16[4,128,768]{2,1,0:T(8,128)(2,1)} %bitcast.71), channel_id=1, source_target_pairs={{0,4},{4,0},{8,12},{12,8},{16,20},{20,16},{24,28},{28,24},{1,5},{5... | collective-permute-start | bytes 2359304 | tf_op jit(solution)/shard_map/ppermute | solution.py:33
  490.4 8.2 collective-permute-start.6
  492.1 11.2 collective-permute-start.7
  492.7 16.1 %collective-permute-start.8 = (f32[3,8,128]{2,0,1:T(4,128)}, f32[3,8,128]{2,0,1:T(4,128)}, u32[]{:S(2)}, u32[]{:S(2)}) collective-permute-start(f32[3,8,128]{2,0,1:T(4,128)} %pad_maximum_fusion.5), channel_id=1, source_target_pairs={{0,12},{4,8},{8,4},{12,0},{16,28},{20,24},{24,20},{28,16},{1,13},{... | collective-permute-start | bytes 36872 | tf_op jit(solution)/shard_map/ppermute | solution.py:33
  493.9 18.3 %collective-permute-start.9 = (f32[3,8,128]{2,0,1:T(4,128)}, f32[3,8,128]{2,0,1:T(4,128)}, u32[]{:S(2)}, u32[]{:S(2)}) collective-permute-start(f32[3,8,128]{2,0,1:T(4,128)} %pad_maximum_fusion.5), channel_id=1, source_target_pairs={{0,16},{4,20},{8,24},{12,28},{16,0},{20,4},{24,8},{28,12},{1,17},{... | collective-permute-start | bytes 36872 | tf_op jit(solution)/shard_map/ppermute | solution.py:33
  494.8 20.7 %collective-permute-start.10 = (f32[3,8,128]{2,0,1:T(4,128)}, f32[3,8,128]{2,0,1:T(4,128)}, u32[]{:S(2)}, u32[]{:S(2)}) collective-permute-start(f32[3,8,128]{2,0,1:T(4,128)} %pad_maximum_fusion.5), channel_id=1, source_target_pairs={{0,20},{4,16},{8,28},{12,24},{16,4},{20,0},{24,12},{28,8},{1,21},{... | collective-permute-start | bytes 36872 | tf_op jit(solution)/shard_map/ppermute | solution.py:33
  498.6 20.2 %collective-permute-start.11 = (f32[3,8,128]{2,0,1:T(4,128)}, f32[3,8,128]{2,0,1:T(4,128)}, u32[]{:S(2)}, u32[]{:S(2)}) collective-permute-start(f32[3,8,128]{2,0,1:T(4,128)} %pad_maximum_fusion.5), channel_id=1, source_target_pairs={{0,24},{4,28},{8,16},{12,20},{16,8},{20,12},{24,0},{28,4},{1,25},{... | collective-permute-start | bytes 36872 | tf_op jit(solution)/shard_map/ppermute | solution.py:33
  503.3 18.8 %collective-permute-start.12 = (f32[3,8,128]{2,0,1:T(4,128)}, f32[3,8,128]{2,0,1:T(4,128)}, u32[]{:S(2)}, u32[]{:S(2)}) collective-permute-start(f32[3,8,128]{2,0,1:T(4,128)} %pad_maximum_fusion.5), channel_id=1, source_target_pairs={{0,28},{4,24},{8,20},{12,16},{16,12},{20,8},{24,4},{28,0},{1,29},{... | collective-permute-start | bytes 36872 | tf_op jit(solution)/shard_map/ppermute | solution.py:33
  541.7 15.9 %collective-permute-start.13 = (bf16[4,128,768]{2,1,0:T(8,128)(2,1)S(1)}, bf16[4,128,768]{2,1,0:T(8,128)(2,1)S(1)}, u32[]{:S(2)}, u32[]{:S(2)}) collective-permute-start(bf16[4,128,768]{2,1,0:T(8,128)(2,1)S(1)} %fusion.151), channel_id=1, source_target_pairs={{0,4},{4,0},{8,12},{12,8},{16,20},{20,16},{24,28},{28,24},{1,5},{5... | collective-permute-start | bytes 2359304 | tf_op jit(solution)/shard_map/ppermute | solution.py:33
  559.7 26.2 %collective-permute-start.14 = (bf16[2,128,768]{2,1,0:T(8,128)(2,1)}, bf16[2,128,768]{2,1,0:T(8,128)(2,1)}, u32[]{:S(2)}, u32[]{:S(2)}) collective-permute-start(bf16[2,128,768]{2,1,0:T(8,128)(2,1)} %fusion.166), channel_id=1, source_target_pairs={{0,8},{4,12},{8,0},{12,4},{16,24},{20,28},{24,16},{28,20},{1,9},{5... | collective-permute-start | bytes 1179656 | tf_op jit(solution)/shard_map/ppermute | solution.py:33
  559.7 5.7 collective-permute-start.19
  561.4 6.5 collective-permute-start.20
  563.4 6.1 collective-permute-start.21
  563.4 19.0 %collective-permute-start.22 = (s32[512]{0:T(512)}, s32[512]{0:T(512)}, u32[]{:S(2)}, u32[]{:S(2)}) collective-permute-start(s32[512]{0:T(512)} %bitcast), channel_id=1, source_target_pairs={{0,16},{4,20},{8,24},{12,28},{16,0},{20,4},{24,8},{28,12},{1,17},{... | collective-permute-start | bytes 6152 | tf_op jit(solution)/shard_map/ppermute | solution.py:33
  565.4 17.0 %collective-permute-start.23 = (s32[512]{0:T(512)}, s32[512]{0:T(512)}, u32[]{:S(2)}, u32[]{:S(2)}) collective-permute-start(s32[512]{0:T(512)} %bitcast), channel_id=1, source_target_pairs={{0,20},{4,16},{8,28},{12,24},{16,4},{20,0},{24,12},{28,8},{1,21},{... | collective-permute-start | bytes 6152 | tf_op jit(solution)/shard_map/ppermute | solution.py:33
  567.9 14.5 %collective-permute-start.24 = (s32[512]{0:T(512)}, s32[512]{0:T(512)}, u32[]{:S(2)}, u32[]{:S(2)}) collective-permute-start(s32[512]{0:T(512)} %bitcast), channel_id=1, source_target_pairs={{0,24},{4,28},{8,16},{12,20},{16,8},{20,12},{24,0},{28,4},{1,25},{... | collective-permute-start | bytes 6152 | tf_op jit(solution)/shard_map/ppermute | solution.py:33
  569.5 12.9 %collective-permute-start.25 = (s32[512]{0:T(512)}, s32[512]{0:T(512)}, u32[]{:S(2)}, u32[]{:S(2)}) collective-permute-start(s32[512]{0:T(512)} %bitcast), channel_id=1, source_target_pairs={{0,28},{4,24},{8,20},{12,16},{16,12},{20,8},{24,4},{28,0},{1,29},{... | collective-permute-start | bytes 6152 | tf_op jit(solution)/shard_map/ppermute | solution.py:33
  587.3 17.7 %collective-permute-start.15 = (bf16[1,128,768]{2,1,0:T(8,128)(2,1)S(1)}, bf16[1,128,768]{2,1,0:T(8,128)(2,1)S(1)}, u32[]{:S(2)}, u32[]{:S(2)}) collective-permute-start(bf16[1,128,768]{2,1,0:T(8,128)(2,1)S(1)} %fusion.186), channel_id=1, source_target_pairs={{0,16},{4,20},{8,24},{12,28},{16,0},{20,4},{24,8},{28,12},{1,17},{... | collective-permute-start | bytes 589832 | tf_op jit(solution)/shard_map/ppermute | solution.py:33
  665.1 11.2 collective-permute-start.16
  665.1 5.0 collective-permute-start.17
  701.4 42.9 %copy-start.53 = (f32[128,768]{1,0:T(8,128)S(1)}, f32[128,768]{1,0:T(8,128)}, u32[]{:S(2)}) copy-start(f32[128,768]{1,0:T(8,128)} %get-tuple-element.241) | copy-start | bytes 1179652
  744.2 9.6 collective-permute-start.18
  (158 other events, 1230.6 us)

commit v3 on v2

--- a/solution.py
+++ b/solution.py
@@ -99,9 +99,9 @@
 
 def bias_strip(rel_row, base, width):
     length = rel_row.shape[1]
-    row = pltpu.roll(jnp.broadcast_to(rel_row, (8, length)), length - base, 1)[:1]
-    rows = jnp.broadcast_to(row, (128, length))
-    return pltpu.roll(rows, 0, 1, stride=1, stride_axis=0)[:, :width]
+    row = pltpu.roll(jnp.broadcast_to(rel_row, (8, length)), length + 128 - base, 1)
+    rows = jnp.broadcast_to(row[:1, : width + 128], (128, width + 128))
+    return pltpu.roll(rows, 0, 1, stride=1, stride_axis=0)[:, 128:]
 
 
 def part_scores(keys, queries_h, strip, col, part, core, key_len, causal):
@@ -382,11 +382,27 @@
     )
 
 
+START_ORDER = (
+    (0, 1), (1, 0), (2, 0), (0, 2), (9, 7), (1, 1), (5, 0),
+    (0, 3), (1, 2), (2, 1), (3, 0), (2, 2), (4, 0), (9, 3), (9, 5),
+    (3, 1), (9, 1), (5, 1), (1, 3), (8, 1), (9, 6), (3, 2), (2, 3),
+    (4, 1), (6, 0), (4, 2), (1, 5), (8, 3), (3, 3), (6, 1), (0, 5),
+    (4, 3), (7, 3), (8, 2), (5, 2), (9, 2), (7, 1), (3, 5), (5, 3),
+    (6, 2), (9, 4), (7, 2), (4, 5), (8, 0), (6, 3), (9, 0), (7, 0),
+    (2, 5), (5, 5), (6, 5),
+)
+
+
 def start_kernel(
-    units, vocab, ids_ref, table_ref, shard_ref, full_ref, mine_ref,
-    ids_all, ids_col, looked, from_x, from_z1, from_z2, total,
-    own_sem, w_send, w_recv, id_send, id_recv, e_send, e_recv,
+    units, ids_ref, small_ref, table_in, shard_ref, *refs
 ):
+    full_refs, refs = refs[:units], refs[units:]
+    (
+        mine_ref, table_ref, ids_out, small_out, small_sorted,
+        ids_all, small_all, chunks, chunk_sem, small_send, small_recv, ids_col, looked,
+        from_x, from_z1, from_z2,
+        own_sem, w_send, w_recv, id_send, id_recv, e_send, e_recv,
+    ) = refs
     wide, narrow = lax.axis_index("wide"), lax.axis_index("narrow")
     flip = lambda bit: wide + bit - 2 * bit * (wide // bit % 2)
     z2, z1, x = wide // 4, wide // 2 % 2, wide % 2
@@ -400,26 +416,28 @@
             if r & bit:
                 there = there + bit - 2 * bit * (wide // bit % 2)
         others.append((there, narrow))
-    greet(others + [at_core, at_y])
+    at_both = (wide, 3 - narrow)
+    greet(others + [at_core, at_y, at_both])
+    vocab = table_in.shape[0]
 
     def own(j):
-        return pltpu.make_async_copy(shard_ref.at[j], full_ref.at[j, 0, z2, z1, x], own_sem.at[j])
+        return pltpu.make_async_copy(shard_ref.at[j], full_refs[j].at[0, z2, z1, x], own_sem.at[j])
 
     def copy(j, stage):
         if stage == 0:
-            src, dst, peer = shard_ref.at[j], full_ref.at[j, 0, z2, z1, x], at_z2
+            src, dst, peer = shard_ref.at[j], full_refs[j].at[0, z2, z1, x], at_z2
         elif stage == 1:
-            src = dst = full_ref.at[j, 0, :, z1, x]
+            src = dst = full_refs[j].at[0, :, z1, x]
             peer = at_z1
         elif stage == 2:
-            src = dst = full_ref.at[j, 0, :, :, x]
+            src = dst = full_refs[j].at[0, :, :, x]
             peer = at_x
         elif stage == 3:
-            src, dst, peer = full_ref.at[j, 0], full_ref.at[j, 2], at_y
+            src, dst, peer = full_refs[j].at[0], full_refs[j].at[2], at_y
         elif stage == 4:
-            src, dst, peer = full_ref.at[j, 0], full_ref.at[j, 1], at_core
+            src, dst, peer = full_refs[j].at[0], full_refs[j].at[1], at_core
         else:
-            src, dst, peer = full_ref.at[j, 2], full_ref.at[j, 3], at_core
+            src, dst, peer = full_refs[j].at[2], full_refs[j].at[3], at_core
         return remote(src, dst, w_send.at[j, stage], w_recv.at[j, stage], peer)
 
     def advance(j, stage):
@@ -436,16 +454,37 @@
             ids_all.at[0], ids_all.at[r], id_send.at[r], id_recv.at[r], others[r - 1]
         )
 
+    def small_copy(g):
+        peer = (None, at_core, at_y, at_both)[g]
+        return remote(small_all.at[0], small_all.at[g], small_send.at[g], small_recv.at[g], peer)
+
+    size = chunks.shape[1]
+    spans = [(at, min(size, vocab - at)) for at in range(0, vocab, size)]
+
+    def chunk_copy(k):
+        at, count = spans[k]
+        return pltpu.make_async_copy(
+            table_in.at[at : at + count], chunks.at[k % 2, :count], chunk_sem.at[k % 2]
+        )
+
+    chunk_copy(0).start()
     ids_all[0] = ids_ref[...]
+    small_all[0] = small_ref[...]
+    for j in range(units):
+        own(j).start()
+    advance(0, 0)
     for r in range(1, 8):
         ids_copy(r).start()
-    for j in range(units):
-        own(j).start()
-    for j in range(min(3, units)):
-        advance(j, 0)
+    for g in range(1, 4):
+        small_copy(g).start()
+    for k, (at, count) in enumerate(spans):
+        if k + 1 < len(spans):
+            chunk_copy(k + 1).start()
+        chunk_copy(k).wait()
+        table_ref[at : at + count, :] = chunks[k % 2, :count, :].astype(bf16)
+    table_ref[vocab:, :] = jnp.zeros((table_ref.shape[0] - vocab, table_ref.shape[1]), bf16)
 
     rows = ids_ref.shape[1]
-    cut = total.shape[0]
 
     def look_up(r):
         if r > 0:
@@ -455,20 +494,16 @@
             ids_col[t * 128 : (t + 1) * 128] = jnp.broadcast_to(
                 ids[:, t * 128 : (t + 1) * 128], (128, 128)
             ).T
-        total[...] = jnp.zeros_like(total)
-
-        def add(k, unused):
-            lane = lax.broadcasted_iota(jnp.int32, (rows, 128), 1) + k * 512
-            col = ids_col[...]
-            hot = jnp.concatenate(
-                [(col == lane + q * 128).astype(f32) for q in range(4)], axis=1
-            ).astype(bf16)
-            block = table_ref[pl.ds(pl.multiple_of(k * 512, 512), 512), :]
-            total[...] += dot(hot, block, 1, 0)
-            return unused
-
-        lax.fori_loop(0, table_ref.shape[0] // 512, add, 0)
-        looked[r] = total[...].astype(bf16)
+        col = ids_col[...]
+        lane = lax.broadcasted_iota(jnp.int32, (rows, 128), 1)
+        hot = jnp.concatenate(
+            [
+                (col == lane + at).astype(f32).astype(bf16)
+                for at in range(0, table_ref.shape[0], 128)
+            ],
+            axis=1,
+        )
+        looked[r] = dot(hot, table_ref[...], 1, 0).astype(bf16)
 
     def e_copy(hop_at, index):
         if hop_at == 0:
@@ -480,44 +515,31 @@
         slot = (0, 4, 6)[hop_at] + index
         return remote(src, dst, e_send.at[slot], e_recv.at[slot], peer)
 
-    order = (3, 1, 2, 0)
-    todo = []
-    for j in range(units):
-        todo += [(5 * j + 6 * s + s * s, j, s) for s in (1, 2, 3, 5)]
-        if j >= 3:
-            todo.append((5 * j, j, 0))
-    todo = [(j, s) for unused, j, s in sorted(todo)]
-    steps = []
-    for s in order:
-        steps.append(("odd", s))
-    for s in order:
-        steps.append(("even", s))
-    for s in order:
-        steps.append(("merge", s))
-    share = -(-len(todo) // (len(steps) + 4))
-    for kind, s in steps:
-        if kind == "odd":
-            look_up(2 * s + 1)
-            e_copy(0, s).start()
-        elif kind == "even":
-            look_up(2 * s)
+    for what, index in START_ORDER:
+        if what < 7:
+            advance(what, index)
+        elif what == 9:
+            look_up(index)
+        elif what == 8:
+            e_copy(0, index).start()
         else:
-            e_copy(0, s).wait_recv()
-            looked[2 * s] = looked[2 * s] + from_x[s]
-            if s % 2 == 1:
-                e_copy(1, s // 2).start()
+            e_copy(0, index).wait_recv()
+            looked[2 * index] = looked[2 * index] + from_x[index]
+            if index % 2 == 1:
+                e_copy(1, index // 2).start()
             else:
-                e_copy(1, s // 2).wait_recv()
-                looked[2 * s] = looked[2 * s] + from_z1[s // 2]
-                if s == 2:
+                e_copy(1, index // 2).wait_recv()
+                looked[2 * index] = looked[2 * index] + from_z1[index // 2]
+                if index == 2:
                     e_copy(2, 0).start()
-        for j, stage in todo[:share]:
-            advance(j, stage)
-        todo = todo[share:]
-    for j, stage in todo:
-        advance(j, stage)
     e_copy(2, 0).wait_recv()
     mine_ref[...] = looked[0] + from_z2[0]
+    for g in range(1, 4):
+        small_copy(g).wait()
+    ids_out[...] = ids_all[...]
+    small_out[...] = small_all[...]
+    for g, index in enumerate((narrow, at_core[1], at_y[1], at_both[1])):
+        small_sorted[index] = small_all[g]
     for j in range(units):
         for stage in range(6):
             copy(j, stage).wait_send()
@@ -530,30 +552,37 @@
             e_copy(hop_at, index).wait_send()
 
 
-def start_phase(ids, table_low, shards):
+def start_phase(ids, small, table, shards):
     units, slim, columns = shards.shape
-    rows, (vocab, width) = ids.shape[1], table_low.shape
-    padded = -(-vocab // 512) * 512
-    table_low = jnp.pad(table_low, ((0, padded - vocab), (0, 0)))
+    rows, (vocab, width) = ids.shape[1], table.shape
+    padded = -(-vocab // 2048) * 2048
     any_space = pl.BlockSpec(memory_space=pl.ANY)
     vmem = pl.BlockSpec(memory_space=pltpu.VMEM)
     dma = pltpu.SemaphoreType.DMA
-    full, mine = pl.pallas_call(
-        functools.partial(start_kernel, units, vocab),
-        in_specs=[vmem, vmem, any_space],
-        out_specs=[any_space, vmem],
-        out_shape=[
-            jax.ShapeDtypeStruct((units, 4, 2, 2, 2, slim, columns), bf16),
+    *full, mine, table_pad, ids_all, small_all, small_sorted = pl.pallas_call(
+        functools.partial(start_kernel, units),
+        in_specs=[vmem, vmem, any_space, any_space],
+        out_specs=[any_space] * units + [vmem] * 5,
+        out_shape=[jax.ShapeDtypeStruct((4, 2, 2, 2, slim, columns), bf16)] * units
+        + [
             jax.ShapeDtypeStruct((rows, width), bf16),
+            jax.ShapeDtypeStruct((padded, width), bf16),
+            jax.ShapeDtypeStruct((8, 1, rows), jnp.int32),
+            jax.ShapeDtypeStruct((4, *small.shape), f32),
+            jax.ShapeDtypeStruct((4, *small.shape), f32),
         ],
         scratch_shapes=[
             pltpu.VMEM((8, 1, rows), jnp.int32),
+            pltpu.VMEM((4, *small.shape), f32),
+            pltpu.VMEM((2, 512, width), f32),
+            dma((2,)),
+            dma((4,)),
+            dma((4,)),
             pltpu.VMEM((rows, 128), jnp.int32),
             pltpu.VMEM((8, rows, width), bf16),
             pltpu.VMEM((4, rows, width), bf16),
             pltpu.VMEM((2, rows, width), bf16),
             pltpu.VMEM((1, rows, width), bf16),
-            pltpu.VMEM((rows, width), f32),
             dma((units,)),
             dma((units, 6)),
             dma((units, 6)),
@@ -569,11 +598,233 @@
             flops=2 * 8 * rows * padded * width, bytes_accessed=2 * 4 * 8 * units * slim * columns,
             transcendentals=0,
         ),
-    )(ids, table_low, shards)
-    return full.reshape(units, 4, 8 * slim, columns), mine
-
-
-def end_kernel(kinds, *refs):
+    )(ids, small, table, shards)
+    full = [one.reshape(4, 8 * slim, columns) for one in full]
+    return full, mine, table_pad, ids_all[:, 0], small_all, small_sorted
+
+
+def head_kernel(
+    vocab, final_ref, table_ref, target_ref, weight_ref, scaled_ref,
+    grad_ref, part_ref, loss_ref,
+    finals, table_t, logits, slopes, stats, log_total, partial, from_x, from_z1, from_z2,
+    f_send, f_recv, s_send, s_recv, g_send, g_recv,
+):
+    wide, narrow = lax.axis_index("wide"), lax.axis_index("narrow")
+
+    def peer(r):
+        index = wide
+        for bit in (1, 2, 4):
+            if r & bit:
+                index = index + bit - 2 * bit * (wide // bit % 2)
+        return (index, narrow)
+
+    greet([peer(r) for r in range(1, 8)])
+    rows, width = final_ref.shape
+    padded = table_ref.shape[0]
+    step = 512
+    steps = padded // step
+
+    def f_copy(r):
+        bit = 1 if r % 2 else (2 if r % 4 else 4)
+        return remote(finals.at[r - bit], finals.at[r], f_send.at[r], f_recv.at[r], peer(bit))
+
+    finals[0] = final_ref[...]
+    for r in (4, 2, 1):
+        f_copy(r).start()
+
+    def chunk_at(k):
+        return pl.ds(pl.multiple_of(k * step, step), step)
+
+    def slots(k):
+        return lax.broadcasted_iota(jnp.int32, (step, 1), 0) + k * step
+
+    def pair_of(ref, p):
+        return jnp.concatenate([ref[2 * p : 2 * p + 1, :], ref[2 * p + 1 : 2 * p + 2, :]], axis=1)
+
+    def forward(p):
+        both = jnp.concatenate([finals[2 * p], finals[2 * p + 1]], axis=0)
+        target = pair_of(target_ref, p)
+
+        def first(k, top):
+            scores = dot(table_ref[chunk_at(k), :], both, 1, 1)
+            scores = jnp.where(slots(k) < vocab, scores, -1e30)
+            logits[p, chunk_at(k), :] = scores
+            return jnp.maximum(top, jnp.max(scores, axis=0, keepdims=True))
+
+        top = lax.fori_loop(0, steps, first, jnp.full((1, 2 * rows), -1e30, f32))
+
+        def second(k, carry):
+            total, hits = carry
+            scores = logits[p, chunk_at(k), :]
+            total = total + jnp.sum(jnp.exp(scores - top), axis=0, keepdims=True)
+            hot = jnp.where(slots(k) == target, scores, 0.0)
+            return total, hits + jnp.sum(hot, axis=0, keepdims=True)
+
+        zero = jnp.zeros((1, 2 * rows), f32)
+        total, hits = lax.fori_loop(0, steps, second, (zero, zero))
+        for side in range(2):
+            for at, value in enumerate((top, total, hits)):
+                stats[0, 2 * p + side, at : at + 1, :] = value[:, side * rows : (side + 1) * rows]
+
+    def turn(k, unused):
+        at = pl.ds(pl.multiple_of(k * step, step), step)
+        table_t[:, at] = table_ref[at, :].T
+        return unused
+
+    lax.fori_loop(0, steps, turn, 0)
+    f_copy(2).wait_recv()
+    f_copy(3).start()
+    f_copy(1).wait_recv()
+    forward(0)
+    f_copy(4).wait_recv()
+    f_copy(6).start()
+    f_copy(5).start()
+    f_copy(3).wait_recv()
+    forward(1)
+    f_copy(6).wait_recv()
+    f_copy(7).start()
+    f_copy(5).wait_recv()
+    forward(2)
+    f_copy(7).wait_recv()
+    forward(3)
+
+    def s_copy(r):
+        return remote(stats.at[0], stats.at[r], s_send.at[r], s_recv.at[r], peer(r))
+
+    for r in range(1, 8):
+        s_copy(r).start()
+    for r in range(1, 8):
+        s_copy(r).wait()
+    for q in range(8):
+        tops = [stats[r, q ^ r, 0:1, :] for r in range(8)]
+        best = functools.reduce(jnp.maximum, tops)
+        total = sum(stats[r, q ^ r, 1:2, :] * jnp.exp(tops[r] - best) for r in range(8))
+        log_total[q : q + 1, :] = best + jnp.log(total)
+    hits = sum(stats[r, r, 2:3, :] for r in range(8))
+    loss_ref[...] = weight_ref[...] * (log_total[0:1, :] - hits)
+
+    def backward(p):
+        target, scaled, minus = pair_of(target_ref, p), pair_of(scaled_ref, p), pair_of(log_total, p)
+
+        def one(k, unused):
+            probs = jnp.exp(logits[p, chunk_at(k), :] - minus)
+            slope = scaled * (probs - (slots(k) == target).astype(f32))
+            slopes[p, chunk_at(k), :] = slope.astype(bf16)
+            return unused
+
+        lax.fori_loop(0, steps, one, 0)
+        down = dot(table_t[...], slopes[p], 1, 0).T.astype(bf16)
+        partial[2 * p] = down[:rows]
+        partial[2 * p + 1] = down[rows:]
+
+    def g_copy(hop_at, index):
+        if hop_at == 0:
+            src, dst, bit = partial.at[2 * index + 1], from_x.at[index], 1
+        elif hop_at == 1:
+            src, dst, bit = partial.at[4 * index + 2], from_z1.at[index], 2
+        else:
+            src, dst, bit = partial.at[4], from_z2.at[0], 4
+        slot = (0, 4, 6)[hop_at] + index
+        return remote(src, dst, g_send.at[slot], g_recv.at[slot], peer(bit))
+
+    def added(a, b):
+        return (a.astype(f32) + b.astype(f32)).astype(bf16)
+
+    def parts(start, stop):
+        def one(k, unused):
+            total = jnp.zeros((step, width), f32)
+            for p in range(4):
+                both = jnp.concatenate([finals[2 * p], finals[2 * p + 1]], axis=0)
+                total = total + dot(slopes[p, chunk_at(k), :], both, 1, 0)
+            part_ref[chunk_at(k), :] = total.astype(bf16)
+            return unused
+
+        lax.fori_loop(start, stop, one, 0)
+
+    def merge(s):
+        g_copy(0, s).wait_recv()
+        partial[2 * s] = added(partial[2 * s], from_x[s])
+
+    for p in (3, 1, 2, 0):
+        backward(p)
+        g_copy(0, p).start()
+    for s in (3, 1):
+        merge(s)
+        g_copy(1, s // 2).start()
+    parts(0, steps // 2)
+    merge(2)
+    g_copy(1, 1).wait_recv()
+    partial[4] = added(partial[4], from_z1[1])
+    g_copy(2, 0).start()
+    parts(steps // 2, steps)
+    merge(0)
+    g_copy(1, 0).wait_recv()
+    partial[0] = added(partial[0], from_z1[0])
+    g_copy(2, 0).wait_recv()
+    grad_ref[...] = partial[0].astype(f32) + from_z2[0].astype(f32)
+    for r in range(1, 8):
+        f_copy(r).wait_send()
+    for hop_at, count in ((0, 4), (1, 2), (2, 1)):
+        for index in range(count):
+            g_copy(hop_at, index).wait_send()
+
+
+def head_phase(vocab, final, table_pad, targets, weights, scaled):
+    rows, width = final.shape
+    padded = table_pad.shape[0]
+    vmem = pl.BlockSpec(memory_space=pltpu.VMEM)
+    dma = pltpu.SemaphoreType.DMA
+    return pl.pallas_call(
+        functools.partial(head_kernel, vocab),
+        in_specs=[vmem] * 5,
+        out_specs=[vmem] * 3,
+        out_shape=[
+            jax.ShapeDtypeStruct((rows, width), f32),
+            jax.ShapeDtypeStruct((padded, width), bf16),
+            jax.ShapeDtypeStruct((1, rows), f32),
+        ],
+        scratch_shapes=[
+            pltpu.VMEM((8, rows, width), bf16),
+            pltpu.VMEM((width, padded), bf16),
+            pltpu.VMEM((4, padded, 2 * rows), f32),
+            pltpu.VMEM((4, padded, 2 * rows), bf16),
+            pltpu.VMEM((8, 8, 8, rows), f32),
+            pltpu.VMEM((8, rows), f32),
+            pltpu.VMEM((8, rows, width), bf16),
+            pltpu.VMEM((4, rows, width), bf16),
+            pltpu.VMEM((2, rows, width), bf16),
+            pltpu.VMEM((1, rows, width), bf16),
+            dma((8,)),
+            dma((8,)),
+            dma((8,)),
+            dma((8,)),
+            dma((7,)),
+            dma((7,)),
+        ],
+        compiler_params=pltpu.CompilerParams(
+            collective_id=2, has_side_effects=True, vmem_limit_bytes=60 * 2**20
+        ),
+        cost_estimate=pl.CostEstimate(
+            flops=6 * 8 * rows * padded * width, bytes_accessed=20 * 2**20,
+            transcendentals=2 * 8 * rows * padded,
+        ),
+    )(final, table_pad, targets, weights, scaled)
+
+
+HELD = 4
+X_FIRST = (5, 6, )
+END_ORDER = (
+    (0, 0), (1, 0), (0, 1), (6, 3), (1, 1), (6, 5), (9, 0), (0, 2),
+    (1, 2), (2, 0), (0, 3), (6, 6), (1, 3), (2, 1), (3, 0), (9, 1),
+    (0, 4), (6, 7), (1, 4), (3, 1), (0, 5), (1, 5), (7, 0), (7, 1),
+    (2, 2), (7, 2), (7, 3), (2, 5), (8, 0), (2, 3), (3, 2), (0, 6),
+    (4, 1), (8, 1), (4, 0), (1, 6), (3, 5), (2, 6), (3, 3), (4, 5),
+    (5, 5), (8, 2), (5, 1), (4, 3), (3, 6), (4, 2), (2, 4), (4, 6),
+    (5, 3), (3, 4), (5, 6), (5, 2), (4, 4), (8, 3), (5, 4), (5, 0),
+)
+
+
+def end_kernel(kinds, places, *refs):
     units = len(kinds)
     lefts = sorted({left for kind in kinds for left, unused in kind})
     rights = sorted({right for kind in kinds for unused, right in kind})
@@ -582,12 +833,13 @@
     left_refs = {name: inputs[i] for i, name in enumerate(lefts)}
     right_refs = {name: inputs[len(lefts) + i] for i, name in enumerate(rights)}
     ids_ref, rows_ref, head_ref, small_ref = refs[count : count + 4]
-    out_ref, table_out, small_out, square_out, c_in, y_in = refs[count + 4 : count + 10]
+    attn_in_out, attn_out_out, ff_in_out, ff_out_out = refs[count + 4 : count + 8]
+    table_out, small_out, square_out, c_in, y_in = refs[count + 8 : count + 13]
     (
         left_vm, right_a, right_b, right_c, right_d, left_t, send_c, stage, held, x_in, z1_in, z2_in,
         gathered, table_vm, table_c, table_y, small_all, small_next, square_all, square_next,
         load_sem, stage_sem, w_send, w_recv, l_send, l_recv, t_send, t_recv, s_send, s_recv, own_sem,
-    ) = refs[count + 10 :]
+    ) = refs[count + 13 :]
     wide, narrow = lax.axis_index("wide"), lax.axis_index("narrow")
     z2, z1, x = wide // 4, wide // 2 % 2, wide % 2
     y, core = narrow // 2, narrow % 2
@@ -602,7 +854,7 @@
     narrow_peer = lambda g: (wide, flipped(narrow, (1, 2), g))
     greet([wide_peer(r) for r in range(1, 8)] + [narrow_peer(g) for g in range(1, 4)])
 
-    slim, columns = out_ref.shape[1:]
+    slim, columns = ff_in_out.shape[1:]
     width = 8 * slim
 
     def small_copy(base, src, dst, index, peer):
@@ -658,11 +910,15 @@
         return whole
 
     def w_copy(j, hop_at):
-        slot = j % 3
+        slot = j % HELD
         if hop_at == 0:
             src, dst, peer = send_c, c_in.at[j], narrow_peer(1)
+        elif hop_at == 1 and j in X_FIRST:
+            src, dst, peer = held.at[slot, :, :, :, 1 - x], y_in.at[j], wide_peer(1)
         elif hop_at == 1:
             src, dst, peer = held.at[slot, 1], y_in.at[j], narrow_peer(2)
+        elif hop_at == 2 and j in X_FIRST:
+            src, dst, peer = held.at[slot, 1, :, :, x], x_in.at[j], narrow_peer(2)
         elif hop_at == 2:
             src, dst, peer = held.at[slot, 0, :, :, 1 - x], x_in.at[j], wide_peer(1)
         elif hop_at == 3:
@@ -683,7 +939,7 @@
             send_c[side] = product(j, 2 * side + 1).reshape(send_c.shape[1:])
         w_copy(j, 0).start()
         for side in range(2):
-            held[j % 3, side] = product(j, 2 * side).reshape(held.shape[2:])
+            held[j % HELD, side] = product(j, 2 * side).reshape(held.shape[2:])
         if j + 1 < units:
             for copy in loads(j + 1):
                 copy.start()
@@ -691,27 +947,36 @@
     def added(a, b):
         return (a.astype(f32) + b.astype(f32)).astype(bf16)
 
+    def staged(src, dst):
+        copy = pltpu.make_async_copy(src, dst, stage_sem.at[0])
+        copy.start()
+        copy.wait()
+
     def after_core(j):
         w_copy(j, 0).wait_recv()
-        copy = pltpu.make_async_copy(c_in.at[j], stage, stage_sem.at[0])
-        copy.start()
-        copy.wait()
+        staged(c_in.at[j], stage)
         for side in (1, 0):
-            held[j % 3, side] = added(held[j % 3, side], stage[side])
-            if side == 1:
+            held[j % HELD, side] = added(held[j % HELD, side], stage[side])
+            if side == 1 and j not in X_FIRST:
                 w_copy(j, 1).start()
-
-    def after_y(j):
+        if j in X_FIRST:
+            w_copy(j, 1).start()
+
+    def after_first(j):
         w_copy(j, 1).wait()
-        copy = pltpu.make_async_copy(y_in.at[j], stage.at[0], stage_sem.at[0])
-        copy.start()
-        copy.wait()
-        held[j % 3, 0] = added(held[j % 3, 0], stage[0])
-        w_copy(j, 2).start()
-
-    def after_x(j):
+        staged(y_in.at[j], stage.at[0])
+        if j in X_FIRST:
+            for side in (1, 0):
+                held[j % HELD, side, :, :, x] = added(held[j % HELD, side, :, :, x], stage[0, side])
+                if side == 1:
+                    w_copy(j, 2).start()
+        else:
+            held[j % HELD, 0] = added(held[j % HELD, 0], stage[0])
+            w_copy(j, 2).start()
+
+    def after_second(j):
         w_copy(j, 2).wait()
-        x_in[j] = added(x_in[j], held[j % 3, 0, :, :, x])
+        x_in[j] = added(x_in[j], held[j % HELD, 0, :, :, x])
         w_copy(j, 3).start()
 
     def after_z1(j):
@@ -722,8 +987,21 @@
     def after_z2(j):
         w_copy(j, 4).wait()
         total = z2_in[j].astype(f32) + z1_in[j, z2].astype(f32)
-        out_ref[j] = total
         note(total)
+        what, layer = places[j]
+        if what == 0:
+            lanes = attn_out_out.shape[1]
+            parts = []
+            for head in range(lanes // DH):
+                for which in range(3):
+                    at = which * lanes + head * DH
+                    parts.append(total[:, at : at + DH])
+            attn_in_out[layer] = jnp.concatenate(parts, axis=1)
+            attn_out_out[layer] = total[:, 3 * lanes :].T
+        elif what == 1:
+            ff_in_out[layer] = total
+        else:
+            ff_out_out[layer] = total.T
 
     def note(values):
         rows = values.shape[0]
@@ -733,23 +1011,23 @@
 
     quarter = table_vm.shape[1]
     tokens = gathered.shape[1]
-    step = 512
-
-    def scatter_rows():
+    step = 256
+
+    def scatter_rows(part):
         def chunk(k, unused):
             per = quarter // step
             at = pl.ds(pl.multiple_of(k % per * step, step), step)
             slot = lax.broadcasted_iota(jnp.int32, (step, 1), 0) + k * step
-
-            def one(r, total):
-                hot = (slot == ids_ref[r]).astype(f32).astype(bf16)
-                return total + dot(hot, gathered[r], 1, 0)
-
-            total = lax.fori_loop(0, 8, one, table_vm[k // per, at, :].astype(f32))
+            hot = jnp.concatenate(
+                [(slot == ids_ref[r]).astype(f32).astype(bf16) for r in range(8)], axis=1
+            )
+            total = table_vm[k // per, at, :].astype(f32)
+            total = total + dot(hot, gathered[...].reshape(8 * tokens, width), 1, 0)
             table_vm[k // per, at, :] = total.astype(bf16)
             return unused
 
-        lax.fori_loop(0, 4 * quarter // step, chunk, 0)
+        count = quarter // step
+        lax.fori_loop(part * count, (part + 1) * count, chunk, 0)
 
     def t_copy(at):
         if at == 0:
@@ -786,34 +1064,18 @@
     for r in (1, 4, 2):
         row_copy(r).start()
 
-    def extra(t):
-        if t == 0:
-            spread_next(0, small_all, small_next)
-        elif t == 1:
-            collect(0, small_next, small_out)
-            row_copy(2).wait_recv()
-            row_copy(3).start()
-            row_copy(4).wait_recv()
-            row_copy(6).start()
-            row_copy(5).start()
-        elif t == 2:
-            row_copy(6).wait_recv()
-            row_copy(7).start()
-            head_load().wait()
-        elif t == 4:
-            for r in (1, 3, 5, 7):
-                row_copy(r).wait_recv()
-            scatter_rows()
+    def table_step(at):
+        there = 2 * (1 - y) + core
+        if at == 0:
             t_copy(0).start()
             t_copy(1).start()
-        elif t == 5:
+        elif at == 1:
             for side in range(2):
                 t_copy(side).wait_recv()
-            there = 2 * (1 - y) + core
             table_vm[there] = added(table_vm[there], table_c[1 - y])
             t_copy(2).start()
             table_vm[narrow] = added(table_vm[narrow], table_c[y])
-        elif t == 7:
+        elif at == 2:
             t_copy(2).wait()
             part = added(table_vm[narrow], table_y[...])
             table_vm[narrow] = part
@@ -821,20 +1083,41 @@
             t_copy(4).start()
             own_quarter().start()
             note(part.astype(f32))
-
-    for t in range(units + 4):
-        if t < units:
-            multiply(t)
-            after_core(t)
-        extra(t)
-        for lag, act in ((1, after_y), (2, after_x), (3, after_z1), (4, after_z2)):
-            if 0 <= t - lag < units:
-                act(t - lag)
+        else:
+            t_copy(3).wait_recv()
+            t_copy(5).start()
+
+    arrived = []
+
+    def rows_step(r):
+        needed = {3: 2, 5: 4, 6: 4, 7: 6}[r]
+        if needed not in arrived:
+            arrived.append(needed)
+            row_copy(needed).wait_recv()
+        row_copy(r).start()
+
+    def scatter_step(part):
+        if part == 0:
+            head_load().wait()
+            for r in (1, 3, 5, 7):
+                row_copy(r).wait_recv()
+        scatter_rows(part)
+
+    def small_step(at):
+        if at == 0:
+            spread_next(0, small_all, small_next)
+        else:
+            collect(0, small_next, small_out)
+
+    acts = (
+        multiply, after_core, after_first, after_second, after_z1, after_z2,
+        rows_step, scatter_step, table_step, small_step,
+    )
+    for what, index in END_ORDER:
+        acts[what](index)
     for r in range(1, 8):
         small_copy(16, square_all.at[0], square_all.at[r], r, wide_peer(r)).start()
     spread_next(16, square_all, square_next)
-    t_copy(3).wait_recv()
-    t_copy(5).start()
     collect(16, square_next, square_out)
     t_copy(4).wait_recv()
     t_copy(5).wait_recv()
@@ -846,7 +1129,7 @@
         row_copy(r).wait_send()
 
 
-def end_phase(kinds, lefts, rights, ids, rows, head, small):
+def end_phase(kinds, places, lefts, rights, ids, rows, head, small):
     units = len(kinds)
     names = sorted({left for kind in kinds for left, unused in kind})
     right_names = sorted({right for kind in kinds for unused, right in kind})
@@ -860,11 +1143,14 @@
     narrow_cols = [rights[right].shape[2] for unused, right in max(kinds, key=len)]
     args = [lefts[name] for name in names] + [rights[name] for name in right_names]
     outs = pl.pallas_call(
-        functools.partial(end_kernel, kinds),
+        functools.partial(end_kernel, kinds, places),
         in_specs=[any_space] * len(args) + [vmem, any_space, any_space, vmem],
-        out_specs=[vmem, any_space, vmem, vmem, any_space, any_space],
+        out_specs=[vmem] * 4 + [any_space, vmem, vmem, any_space, any_space],
         out_shape=[
-            jax.ShapeDtypeStruct((units, slim, width), f32),
+            jax.ShapeDtypeStruct((3, slim, 3 * (width // 4)), f32),
+            jax.ShapeDtypeStruct((3, width // 4, slim), f32),
+            jax.ShapeDtypeStruct((2, slim, width), f32),
+            jax.ShapeDtypeStruct((2, width, slim), f32),
             jax.ShapeDtypeStruct((4, quarter, width), bf16),
             jax.ShapeDtypeStruct(small.shape, f32),
             jax.ShapeDtypeStruct((8, 128), f32),
@@ -880,7 +1166,7 @@
             pltpu.VMEM((3, width, most), bf16),
             pltpu.VMEM((2, 2, 2, 2, slim, width), bf16),
             pltpu.VMEM((2, 2, 2, 2, slim, width), bf16),
-            pltpu.VMEM((3, 2, 2, 2, 2, slim, width), bf16),
+            pltpu.VMEM((HELD, 2, 2, 2, 2, slim, width), bf16),
             pltpu.VMEM((units, 2, 2, slim, width), bf16),
             pltpu.VMEM((units, 2, slim, width), bf16),
             pltpu.VMEM((units, slim, width), bf16),
@@ -911,7 +1197,7 @@
             flops=2 * 8 * tokens * 4 * quarter * width, bytes_accessed=100 * 2**20, transcendentals=0
         ),
     )(*args, ids, rows, head, small)
-    return outs[:4]
+    return outs[:4], *outs[4:7]
 
 
 def body(
@@ -945,21 +1231,9 @@
     shards = jnp.stack(shards).astype(bf16)
     groups = narrow_index ^ jnp.arange(narrow_size)
     small = jnp.concatenate([gains.reshape(-1), rel.reshape(-1)])
-    small = lax.all_gather(small, "narrow", axis=0, tiled=False)
     cut = gains.size
-    gains_full = small[:, :cut].reshape(narrow_size, *gains.shape).transpose(1, 0, 2)
-    gains_full = gains_full.reshape(gains.shape[0], -1)
-    rel_full = small[:, cut:].reshape(narrow_size, *rel.shape).transpose(1, 2, 0, 3)
-    rel_full = rel_full.reshape(rel.shape[0], rel.shape[1], -1)
     onehot_rev = (buckets[::-1][:, None] == jnp.arange(rel.shape[1])[None, :]).astype(f32)
     onehot_rev = jnp.pad(onehot_rev, ((0, 1), (0, 0)))
-    rel_rows = [
-        jnp.dot(onehot_rev, rel_full[i], precision=highest)
-        .T.reshape(narrow_size, heads_here, 1, -1)[groups]
-        .reshape(narrow_size * heads_here, 1, -1)
-        for i in range(2)
-    ]
-
     my_enc = lax.dynamic_slice(enc_ids, (micro, 0, core * enc_rows), (1, 1, enc_rows))
     others = wide_index ^ jnp.arange(wide_size)
     targets_micro = lax.dynamic_index_in_dim(tgt_ids, micro, 0, keepdims=False)[others]
@@ -967,25 +1241,39 @@
         [jnp.zeros((wide_size, 1), jnp.int32), targets_micro[:, :-1]], axis=1
     )
     dec_all = lax.dynamic_slice_in_dim(shifted, core * dec_rows, dec_rows, 1)
-    table_low = table.astype(bf16)
-    enc_all = gather_direct(my_enc.reshape(enc_rows), "wide")
-    tokens = jnp.concatenate([enc_all, dec_all], axis=1)
-    local = tokens - wide_index * vocab
-    held = (local >= 0) & (local < vocab)
-    local = jnp.where(held, local, 0)
     if wide_size == 8 and narrow_size == 4:
         my_ids = jnp.concatenate([my_enc.reshape(enc_rows), dec_all[0]])[None]
-        gathered, mine = start_phase(my_ids, table_low, shards)
+        gathered, mine, table_pad, tokens, small, small_sorted = start_phase(
+            my_ids, small.reshape(-1, 128), table, shards
+        )
+        small = small.reshape(narrow_size, -1)
+        small_sorted = small_sorted.reshape(narrow_size, -1)
+        local = tokens - wide_index * vocab
+        held = (local >= 0) & (local < vocab)
     else:
+        small_sorted = lax.all_gather(small, "narrow", axis=0, tiled=False)
+        small = small_sorted[groups]
+        enc_all = gather_direct(my_enc.reshape(enc_rows), "wide")
+        tokens = jnp.concatenate([enc_all, dec_all], axis=1)
+        local = tokens - wide_index * vocab
+        held = (local >= 0) & (local < vocab)
         gathered = []
         for shard in shards:
             column = gather_sorted(shard, "wide").reshape(width, -1)
             pair = jnp.stack([column, hop(column, "narrow", 2)])
             pair = jnp.stack([pair, swap(pair)], axis=1)
             gathered.append(pair.reshape(narrow_size, width, -1))
-        rows = table_low[local.reshape(-1)]
+        table_low = table.astype(bf16)
+        rows = table_low[jnp.where(held, local, 0).reshape(-1)]
         rows = jnp.where(held.reshape(-1)[:, None], rows, 0).astype(bf16)
         mine = scatter_relative(rows.reshape(*local.shape, width), "wide", bf16)
+    gains_full = small_sorted[:, :cut].reshape(narrow_size, *gains.shape).transpose(1, 0, 2)
+    gains_full = gains_full.reshape(gains.shape[0], -1)
+    rel_full = small[:, cut:].reshape(narrow_size, *rel.shape).transpose(1, 2, 0, 3)
+    rel_full = rel_full.reshape(rel.shape[0], rel.shape[1], -1)
+    rel_rows = [
+        jnp.dot(onehot_rev, rel_full[i], precision=highest).T[:, None, :] for i in range(2)
+    ]
     low_in = [gathered[i][:, :, : 3 * lanes] for i in range(3)]
     low_out = [gathered[i][:, :, 3 * lanes :] for i in range(3)]
     low_up = [gathered[3], gathered[5]]
@@ -1064,35 +1352,45 @@
     weights = lax.dynamic_slice_in_dim(weights_micro, core * dec_rows, dec_rows, 1).reshape(-1)
     targets = lax.dynamic_slice_in_dim(targets_micro, core * dec_rows, dec_rows, 1).reshape(-1)
     targets = targets - wide_index * vocab
-    final_all = gather_relative(final, "wide").reshape(-1, width)
-    logits = dot(final_all, table_low, 1, 1)
-    target_hot = jnp.arange(vocab)[None, :] == targets[:, None]
-    top = jnp.max(logits, axis=-1)
-    total = jnp.sum(jnp.exp(logits - top[:, None]), axis=-1)
-    hits = jnp.sum(jnp.where(target_hot, logits, 0.0), axis=-1)
-    stats = jnp.stack([top, total, hits]).reshape(3, wide_size, dec_rows)
-    if wide_size > 8:
-        stats = lax.all_gather(stats[:, others], "wide", axis=0, tiled=False)[:, :, others]
+    if wide_size == 8 and narrow_size == 4:
+        own_weights = weights[None, :dec_rows]
+        shape = (wide_size, dec_rows)
+        final_grad, head_part, loss_row = head_phase(
+            vocab, final, table_pad,
+            jnp.where(targets < vocab, targets, -1).reshape(shape), own_weights,
+            (weights / count).reshape(shape),
+        )
+        loss_part = jnp.sum(loss_row)
     else:
-        stats = jnp.stack(
-            [stats]
-            + [
-                hop(stats, "wide", r)[:, [q ^ r for q in range(wide_size)]]
-                for r in range(1, wide_size)
-            ]
+        final_all = gather_relative(final, "wide").reshape(-1, width)
+        logits = dot(final_all, table_low, 1, 1)
+        target_hot = jnp.arange(vocab)[None, :] == targets[:, None]
+        top = jnp.max(logits, axis=-1)
+        total = jnp.sum(jnp.exp(logits - top[:, None]), axis=-1)
+        hits = jnp.sum(jnp.where(target_hot, logits, 0.0), axis=-1)
+        stats = jnp.stack([top, total, hits]).reshape(3, wide_size, dec_rows)
+        if wide_size > 8:
+            stats = lax.all_gather(stats[:, others], "wide", axis=0, tiled=False)[:, :, others]
+        else:
+            stats = jnp.stack(
+                [stats]
+                + [
+                    hop(stats, "wide", r)[:, [q ^ r for q in range(wide_size)]]
+                    for r in range(1, wide_size)
+                ]
+            )
+        stats = stats.reshape(wide_size, 3, -1)
+        best = jnp.max(stats[:, 0], axis=0)
+        log_total = best + jnp.log(jnp.sum(stats[:, 1] * jnp.exp(stats[:, 0] - best[None]), axis=0))
+        loss_rows = weights * (log_total - jnp.sum(stats[:, 2], axis=0))
+        loss_part = jnp.sum(loss_rows[:dec_rows])
+        logit_grad = (
+            (weights / count)[:, None]
+            * (jnp.exp(logits - log_total[:, None]) - target_hot.astype(f32))
+        ).astype(bf16)
+        final_grad = scatter_relative(
+            dot(logit_grad, table_low, 1, 0).reshape(wide_size, dec_rows, width), "wide", f32
         )
-    stats = stats.reshape(wide_size, 3, -1)
-    best = jnp.max(stats[:, 0], axis=0)
-    log_total = best + jnp.log(jnp.sum(stats[:, 1] * jnp.exp(stats[:, 0] - best[None]), axis=0))
-    loss_rows = weights * (log_total - jnp.sum(stats[:, 2], axis=0))
-    loss_part = jnp.sum(loss_rows[:dec_rows])
-    logit_grad = (
-        (weights / count)[:, None]
-        * (jnp.exp(logits - log_total[:, None]) - target_hot.astype(f32))
-    ).astype(bf16)
-    final_grad = scatter_relative(
-        dot(logit_grad, table_low, 1, 0).reshape(wide_size, dec_rows, width), "wide", f32
-    )
 
     gain_grads = [None] * 7
     dec_grad, gain_raw = rms_backward(dec3, final_gain, final_inverse, final_grad)
@@ -1132,19 +1430,16 @@
                 rights["r%02d" % len(rights)] = right
                 kind.append((name, "r%02d" % (len(rights) - 1)))
             kinds.append(tuple(kind))
-        quarter = -(-vocab // 2048) * 512
-        head_part = dot(logit_grad, final_all, 0, 0).astype(bf16)
-        head_part = jnp.pad(head_part, ((0, 4 * quarter - vocab), (0, 0)))
+        quarter = head_part.shape[0] // 4
         flat = jnp.concatenate(
             [jnp.stack(gain_grads).reshape(-1), rel_grad.reshape(-1), loss_part[None]]
         )
         small_rows = -(-flat.size // 1024) * 8
         small_in = jnp.pad(flat, (0, small_rows * 128 - flat.size)).reshape(small_rows, 128)
-        summed, table_grad, small_sum, square_rows = end_phase(
-            tuple(kinds), lefts, rights, local[:, None, :], row_grads,
+        matrix_grads, table_grad, small_sum, square_rows = end_phase(
+            tuple(kinds), ((1, 1), (2, 1), (0, 2), (0, 1), (1, 0), (2, 0), (0, 0)), lefts, rights, local[:, None, :], row_grads,
             head_part.reshape(4, quarter, width), small_in,
         )
-        reduced = [summed[i] for i in (6, 3, 2, 4, 5, 0, 1)]
         table_grad = table_grad.reshape(4 * quarter, width)[:vocab].astype(f32)
         small_sum = small_sum.reshape(-1)
         cut = 7 * width
@@ -1180,6 +1475,15 @@
         gain_total, rel_total, loss_sum = lax.psum(
             (jnp.stack(gain_grads), rel_grad, loss_part), ("wide", "narrow")
         )
+        unpack = lambda grad: (
+            grad[:, : 3 * lanes].reshape(slim, 3, heads_here, DH).transpose(0, 2, 1, 3)
+        ).reshape(slim, -1)
+        matrix_grads = (
+            jnp.stack([unpack(reduced[i]) for i in range(3)]),
+            jnp.stack([reduced[i][:, 3 * lanes :].T for i in range(3)]),
+            jnp.stack([reduced[3], reduced[5]]),
+            jnp.stack([reduced[4].T, reduced[6].T]),
+        )
         squares = sum(jnp.sum(grad * grad) for grad in reduced + part_grads)
         square_sum = lax.psum(squares, ("wide", "narrow"))
     square_sum = square_sum + jnp.sum(gain_total * gain_total) + jnp.sum(rel_total * rel_total)
@@ -1188,19 +1492,7 @@
         rel_total, narrow_index * heads_here, heads_here, 1
     ).transpose(0, 2, 1)
 
-    def unpack_in(grad):
-        grad = grad[:, : 3 * lanes].reshape(slim, 3, heads_here, DH).transpose(0, 2, 1, 3)
-        return grad.reshape(slim, -1)
-
-    grads = (
-        jnp.stack([unpack_in(reduced[i]) for i in range(3)]),
-        jnp.stack([reduced[i][:, 3 * lanes :].T for i in range(3)]),
-        jnp.stack([reduced[3], reduced[5]]),
-        jnp.stack([reduced[4].T, reduced[6].T]),
-        table_grad,
-        gain_mine,
-        rel_mine,
-    )
+    grads = (*matrix_grads, table_grad, gain_mine, rel_mine)
     norm = jnp.sqrt(square_sum)
     scale = jnp.minimum(1.0, clip_norm / norm)
     base_rate = math.sqrt(PARAMS) / (3.0 * clip_norm)

time: 1190 us -> 933 us (0.78)
  local copies, waits for them, and re-layouts: 137 us -> 47.1 us
  Pallas kernels: 753 us -> 707 us
  waiting for transfers between devices: 41.5 us -> 1.11 us
  other arithmetic: 92.1 us -> 64.4 us
  starting transfers between devices: 29 us -> 2.03 us
  matrix products: 116 us -> 94.1 us
    pallas_call x2 -> x3, Pallas kernels: 634 us -> 589 us  [the longest x1 282 us: end_phase(): pl.pallas_call(functools.partial(end_kernel, kinds, places), in_specs=[an...]
    ppermute x26 -> x6, waiting for transfers between devices: 41.5 us -> 1.11 us  [hop(): return lax.ppermute(values, axis, [(i, i ^ bit) for i in range(size)])]
    dot_general x5 -> x2, matrix products: 36 us -> 1.15 us  [body(): jnp.dot(onehot_rev, rel_full[i], precision=highest).T[:, None, :]]
    ppermute x26 -> x6, starting transfers between devices: 29 us -> 2.03 us  [hop(): return lax.ppermute(values, axis, [(i, i ^ bit) for i in range(size)])]
    slice x8 -> x2, local copies, waits for them, and re-layouts: 26.5 us -> 0.51 us  [the longest x1 0.51 us: body(): own_weights = weights[None, :dec_rows]]
    unnamed x373 -> x303, local copies, waits for them, and re-layouts: 45.1 us -> 28.3 us
    gather x9 -> x0, local copies, waits for them, and re-layouts: 15.5 us -> none  [the longest x7 14.1 us: body(): hop(stats, 'wide', r)[:, [q ^ r for q in range(wide_size)]]]
  transfers between devices with their start and end apart: 26 -> 6, of which waited for: 5 -> 1; matrix products, arithmetic and copies ran while one was open for 9% -> 7% of each run, Pallas kernels for 1% -> 4%
where the time goes in v3:
time: 933 us; the launch traced here: 923 us
  Pallas kernels  707 us (76%)
  matrix products  94.1 us (10%)
  other arithmetic  64.4 us (7%)
  local copies, waits for them, and re-layouts  47.1 us (5%)
    pallas_call x1, Pallas kernels, end_phase(): pl.pallas_call(functools.partial(end_kernel, kinds, places), in_specs=[an...  282 us
    pallas_call x1, Pallas kernels, start_phase(): pl.pallas_call(functools.partial(start_kernel, units), in_specs=[vmem, vm...  228 us
    pallas_call x1, Pallas kernels, head_phase(): pl.pallas_call(functools.partial(head_kernel, vocab), in_specs=[vmem] * 5...  78.4 us
    pallas_call x3, Pallas kernels, attend_back(): pl.pallas_call(functools.partial(backward_kernel, has_bias, causal, centr...  73.4 us
    dot_general x13, matrix products, project(): return jnp.einsum('rk,nkc->nrc', rows, weights, preferred_element_type=f32)  50 us
    pallas_call x3, Pallas kernels, attend(): pl.pallas_call(functools.partial(forward_kernel, has_bias, causal, centre...  45 us
    dot_general x13, matrix products, project_back(): return jnp.einsum('nrc,nkc->rk', grads, weights, preferred_element_type=f32)  42.1 us
    add x7, other arithmetic, body(): average_decay * avgs[index] + (1.0 - average_decay) * weight  36.2 us
  transfers between devices with their start and end apart: 6, of which 1 were waited for; matrix products, arithmetic and copies ran while one was open for 7% of the time, Pallas kernels for 4%

profile of v3, /device:TPU:0, one launch (start us, length us, event | category | flops | bytes accessed | tf_op | source)
XLA Modules:
  0.0 922.8 jit_solution(16628960885438024518)
XLA Ops:
  7.5 228.0 %shard_map.442 = (bf16[4,2,2,2,96,768]{5,4,3,2,1,0:T(8,128)(2,1)}, bf16[4,2,2,2,96,768]{5,4,3,2,1,0:T(8,128)(2,1)}, bf16[4,2,2,2,96,768]{5,4,3,2,1,0:T(8,128)(2,...) custom-call(s32[1,640]{1,0:T(1,128)S(1)} %broadcast_in_dim.14.ids_re, ...), custom_call_target="tpu_custom_call" | custom-call | flops 32212254720 | bytes 33030144 | tf_op jit(solution)/shard_map/pallas_call | solution.py:562
  236.4 4.9 fusion.64.kvo_ref
  242.1 2.9 fusion.95.kvo_ref
  245.2 3.4 convolution_convert_fusion.1
  255.2 2.8 fusion.135
  258.0 25.5 %shard_map.444 = (bf16[4,512,192]{2,1,0:T(8,128)(2,1)S(1)}, f32[4,3,1,512]{3,2,1,0:T(1,128)S(1)}) custom-call(s32[2]{0:T(128)S(1)} %pad_add_fusion.1.scal, bf16[4,512,192]{2,1,0:T(8,128)(2,1)S(1)} %bitcast.347, bf16[4,512,384]{2,1,0:T(8,128)(2,1)} %fusion.64.kvo_ref, bf16[4,512,384]{2,1,0:T(8,128)(2,1)} %collective-permute-done.1.kvt_ref, ...), custom_call_target="tpu_custom_call" | custom-call | tf_op jit(solution)/shard_map/pallas_call | solution.py:190
  283.5 3.0 multiply_reduce_fusion.1
  286.9 5.4 fusion.10
  292.3 2.7 multiply_reduce_fusion
  311.1 7.6 shard_map.443
  322.6 2.8 fusion.141
  326.4 12.0 %shard_map.445 = (bf16[4,128,192]{2,1,0:T(8,128)(2,1)S(1)}, f32[4,3,1,128]{3,2,1,0:T(1,128)S(1)}) custom-call(s32[2]{0:T(128)S(1)} %pad_add_fusion.1.scal, bf16[4,128,192]{2,1,0:T(8,128)(2,1)S(1)} %bitcast.352, bf16[4,512,384]{2,1,0:T(8,128)(2,1)} %fusion.61.kvo_ref, bf16[4,512,384]{2,1,0:T(8,128)(2,1)} %collective-permute-done.2.kvt_ref), custom_call_target="tpu_custom_call" | custom-call | tf_op jit(solution)/shard_map/pallas_call | solution.py:190
  341.1 4.7 fusion.60
  348.3 78.4 %shard_map.446 = (f32[128,768]{1,0:T(8,128)}, bf16[4096,768]{1,0:T(8,128)(2,1)}, f32[1,128]{1,0:T(1,128)}) custom-call(bf16[128,768]{1,0:T(8,128)(2,1)} %multiply_convert_fusion.2.final_ref, bf16[4096,768]{1,0:T(8,128)(2,1)} %get-tuple-element.76.table_ref, s32[8,128]{1,0:T(8,128)} %get-tuple-element.279.target_ref, f32[1,128]{1,0:T(1,128)} %slice.388.weight_ref, ...), custom_call_target="tpu_custom_call" | custom-call | flops 19327352832 | bytes 20971520 | tf_op jit(solution)/shard_map/pallas_call | solution.py:777
  429.5 4.0 fusion.35.refs_11_
  433.5 4.9 multiply_reduce_fusion.2
  440.1 3.2 fusion.144
  446.7 17.2 %shard_map.447 = (bf16[4,128,192]{2,1,0:T(8,128)(2,1)S(1)}, f32[4,512,384]{2,1,0:T(8,128)S(1)}, bf16[4,512,384]{2,1,0:T(8,128)(2,1)}) custom-call(s32[2]{0:T(128)S(1)} %pad_add_fusion.1.scal, bf16[4,128,192]{2,1,0:T(8,128)(2,1)S(1)} %bitcast.353, bf16[4,512,384]{2,1,0:T(8,128)(2,1)} %fusion.61.kvo_ref, bf16[4,512,384]{2,1,0:T(8,128)(2,1)} %collective-permute-done.2.kvt_ref, ...), custom_call_target="tpu_custom_call" | custom-call | tf_op jit(solution)/shard_map/pallas_call | solution.py:319
  464.0 4.0 multiply_reduce_fusion.3
  469.6 3.2 fusion.138
  473.9 13.6 %shard_map.448 = (bf16[4,128,192]{2,1,0:T(8,128)(2,1)S(1)}, f32[4,128,384]{2,1,0:T(8,128)S(1)}, bf16[4,128,384]{2,1,0:T(8,128)(2,1)}, f32[4,3,2,8,256]{4,3,2,1,0:T(8,128)S(1)}) custom-call(s32[2]{0:T(128)S(1)} %pad_add_fusion.1.scal, bf16[4,128,192]{2,1,0:T(8,128)(2,1)S(1)} %bitcast.351, bf16[4,128,384]{2,1,0:T(8,128)(2,1)S(1)} %fusion.95.kvo_ref, ...), custom_call_target="tpu_custom_call" | custom-call | tf_op jit(solution)/shard_map/pallas_call | solution.py:319
  494.0 3.1 fusion.110
  497.2 2.8 fusion.170
  502.2 5.1 fusion.40
  508.7 6.3 fusion.6.refs_19_
  515.1 2.8 fusion.46
  520.7 3.8 convolution_convert_fusion
  526.0 42.6 %shard_map.449 = (bf16[4,512,192]{2,1,0:T(8,128)(2,1)S(1)}, f32[4,512,384]{2,1,0:T(8,128)S(1)}, bf16[4,512,384]{2,1,0:T(8,128)(2,1)}, f32[4,3,2,8,1024]{4,3,2,1,0:T(8,128)S(1)}) custom-call(s32[2]{0:T(128)S(1)} %pad_add_fusion.1.scal, bf16[4,512,192]{2,1,0:T(8,128)(2,1)S(1)} %bitcast.348, bf16[4,512,384]{2,1,0:T(8,128)(2,1)} %fusion.64.kvo_ref, ...), custom_call_target="tpu_custom_call" | custom-call | tf_op jit(solution)/shard_map/pallas_call | solution.py:319
  579.3 4.5 fusion.55
  588.1 282.4 %shard_map.450 = (f32[3,96,576]{2,1,0:T(8,128)}, f32[3,192,96]{2,1,0:T(8,128)}, f32[2,96,768]{2,1,0:T(8,128)}, f32[2,768,96]{2,1,0:T(8,128)}, bf16[4,1024,768]{2...) custom-call(bf16[128,768]{1,0:T(8,128)(2,1)} %copy-done.68, ...), custom_call_target="tpu_custom_call" | custom-call | flops 32212254720 | bytes 104857600 | tf_op jit(solution)/shard_map/pallas_call | solution.py:1145
  878.4 2.8 multiply_add_fusion.1
  886.8 28.8 %multiply_add_fusion = (f32[4016,768]{1,0:T(8,128)}, f32[4016,768]{1,0:T(8,128)}, f32[4016,768]{1,0:T(8,128)}) fusion(f32[4016,768]{1,0:T(8,128)} %param.51, f32[4016,768]{1,0:T(8,128)} %table_in.1, f32[4016,768]{1,0:T(8,128)} %param.44, f32[]{:T(128)S(6)} %min.3, bf16[4096,768]{1,0:T(8,128)(2,1)} %bitcast.360), kind=kLoop, calls=%fused_computation.3 | loop fusion | flops 33927168 | bytes 80191488 | tf_op jit(solution)/shard_map/add | solution.py:1514
  (497 shorter events, 96.7 us)
Async XLA Ops:
  236.4 8.9 copy-start.48
  241.3 16.7 %collective-permute-start.1 = (bf16[4,512,384]{2,1,0:T(8,128)(2,1)}, bf16[4,512,384]{2,1,0:T(8,128)(2,1)}, u32[]{:S(2)}, u32[]{:S(2)}) collective-permute-start(bf16[4,512,384]{2,1,0:T(8,128)(2,1)} %fusion.64.kvo_ref), channel_id=1, source_target_pairs={{0,1},{1,0},{2,3},{3,2},{4,5},{5,4},{6,7},{7,6},{8,9},{9,8},{10,11... | collective-permute-start | bytes 4718600 | tf_op jit(solution)/shard_map/ppermute | solution.py:33
  245.0 66.1 %collective-permute-start = (bf16[4,128,384]{2,1,0:T(8,128)(2,1)S(1)}, bf16[4,128,384]{2,1,0:T(8,128)(2,1)S(1)}, u32[]{:S(2)}, u32[]{:S(2)}) collective-permute-start(bf16[4,128,384]{2,1,0:T(8,128)(2,1)S(1)} %fusion.95.kvo_ref), channel_id=1, source_target_pairs={{0,1},{1,0},{2,3},{3,2},{4,5},{5,4},{6,7},{7,6},{8,9},{9,8},{10,11... | collective-permute-start | bytes 1179656 | tf_op jit(solution)/shard_map/ppermute | solution.py:33
  252.5 34.1 %copy-start.73 = (f32[768]{0:T(1024)}, f32[768]{0:T(1024)S(1)}, u32[]{:S(2)}) copy-start(f32[768]{0:T(1024)S(1)} %mul.834) | copy-start | bytes 9220
  252.6 42.5 %copy-start.70 = (f32[768]{0:T(1024)}, f32[768]{0:T(1024)S(1)}, u32[]{:S(2)}) copy-start(f32[768]{0:T(1024)S(1)} %mul.844) | copy-start | bytes 9220
  298.4 28.0 %collective-permute-start.2 = (bf16[4,512,384]{2,1,0:T(8,128)(2,1)}, bf16[4,512,384]{2,1,0:T(8,128)(2,1)}, u32[]{:S(2)}, u32[]{:S(2)}) collective-permute-start(bf16[4,512,384]{2,1,0:T(8,128)(2,1)} %fusion.61.kvo_ref), channel_id=1, source_target_pairs={{0,1},{1,0},{2,3},{3,2},{4,5},{5,4},{6,7},{7,6},{8,9},{9,8},{10,11... | collective-permute-start | bytes 4718600 | tf_op jit(solution)/shard_map/ppermute | solution.py:33
  326.4 12.0 %copy-start.31 = (f32[128,768]{1,0:T(8,128)S(1)}, f32[128,768]{1,0:T(8,128)}, u32[]{:S(2)}) copy-start(f32[128,768]{1,0:T(8,128)} %copy-done.30) | copy-start | bytes 1179652
  338.5 7.3 slice-start
  446.7 17.3 %copy-start.32 = (f32[128,768]{1,0:T(8,128)S(1)}, f32[128,768]{1,0:T(8,128)}, u32[]{:S(2)}) copy-start(f32[128,768]{1,0:T(8,128)} %copy-done.30) | copy-start | bytes 1179652
  446.7 17.3 %copy-start.78 = (f32[768]{0:T(1024)S(1)}, f32[768]{0:T(1024)}, u32[]{:S(2)}) copy-start(f32[768]{0:T(1024)} %mul.822) | copy-start | bytes 9220
  446.7 17.3 %copy-start.110 = (f32[128]{0:T(128)S(1)}, f32[128]{0:T(128)}, u32[]{:S(2)}) copy-start(f32[128]{0:T(128)} %copy-done.109) | copy-start | bytes 1540
  472.8 17.8 %copy-start.92 = (f32[768]{0:T(1024)S(1)}, f32[768]{0:T(1024)}, u32[]{:S(2)}) copy-start(f32[768]{0:T(1024)} %get-tuple-element.186) | copy-start | bytes 9220
  473.9 16.7 %copy-start.104 = (f32[768]{0:T(1024)S(1)}, f32[768]{0:T(1024)}, u32[]{:S(2)}) copy-start(f32[768]{0:T(1024)} %get-tuple-element.184) | copy-start | bytes 9220
  473.9 16.7 %copy-start.94 = (f32[768]{0:T(1024)S(1)}, f32[768]{0:T(1024)}, u32[]{:S(2)}) copy-start(f32[768]{0:T(1024)} %get-tuple-element.182) | copy-start | bytes 9220
  473.9 17.1 %copy-start.26 = (pred[2047,32]{1,0:T(8,128)(4,1)S(1)}, pred[2047,32]{1,0:T(8,128)(4,1)}, u32[]{:S(2)}) copy-start(pred[2047,32]{1,0:T(8,128)(4,1)} %copy-done.25) | copy-start | bytes 196516
  490.0 10.1 %collective-permute-start.3 = (bf16[4,512,384]{2,1,0:T(8,128)(2,1)}, bf16[4,512,384]{2,1,0:T(8,128)(2,1)}, u32[]{:S(2)}, u32[]{:S(2)}) collective-permute-start(bf16[4,512,384]{2,1,0:T(8,128)(2,1)} %get-tuple-element.81), channel_id=1, source_target_pairs={{0,1},{1,0},{2,3},{3,2},{4,5},{5,4},{6,7},{7,6},{8,9},{9,8},{10,11... | collective-permute-start | bytes 4718600 | tf_op jit(solution)/shard_map/ppermute | solution.py:33
  490.1 3.8 collective-permute-start.4
  500.1 8.6 slice-start.10
  500.1 8.5 slice-start.12
  507.3 7.7 slice-start.6
  526.0 44.0 %copy-start.42 = (f32[128,768]{1,0:T(8,128)S(1)}, f32[128,768]{1,0:T(8,128)}, u32[]{:S(2)}) copy-start(f32[128,768]{1,0:T(8,128)} %get-tuple-element.219) | copy-start | bytes 1179652
  526.0 44.0 %copy-start.60 = (f32[128,768]{1,0:T(8,128)S(1)}, f32[128,768]{1,0:T(8,128)}, u32[]{:S(2)}) copy-start(f32[128,768]{1,0:T(8,128)} %get-tuple-element.277) | copy-start | bytes 1179652
  569.6 7.8 collective-permute-start.5
  588.1 288.5 %copy-start.96 = (f32[2,32,3]{1,0,2:T(2,128)S(1)}, f32[2,32,3]{1,0,2:T(2,128)}, u32[]{:S(2)}) copy-start(f32[2,32,3]{1,0,2:T(2,128)} %param.39) | copy-start | bytes 2308
  588.1 288.5 %copy-start.105 = (f32[2,32,3]{1,0,2:T(2,128)S(1)}, f32[2,32,3]{1,0,2:T(2,128)}, u32[]{:S(2)}) copy-start(f32[2,32,3]{1,0,2:T(2,128)} %param.53) | copy-start | bytes 2308
  588.1 288.5 %copy-start.106 = (f32[2,32,3]{1,0,2:T(2,128)S(1)}, f32[2,32,3]{1,0,2:T(2,128)}, u32[]{:S(2)}) copy-start(f32[2,32,3]{1,0,2:T(2,128)} %param.46) | copy-start | bytes 2308
  588.1 290.3 %copy-start.33 = (f32[2,768,96]{2,1,0:T(8,128)S(1)}, f32[2,768,96]{2,1,0:T(8,128)}, u32[]{:S(2)}) copy-start(f32[2,768,96]{2,1,0:T(8,128)} %copy.252) | copy-start | bytes 1769476
  588.1 290.3 %copy-start.34 = (f32[2,768,96]{2,1,0:T(8,128)S(1)}, f32[2,768,96]{2,1,0:T(8,128)}, u32[]{:S(2)}) copy-start(f32[2,768,96]{2,1,0:T(8,128)} %copy.251) | copy-start | bytes 1769476
  886.8 28.8 %copy-start.38 = (f32[2,96,768]{2,1,0:T(8,128)S(1)}, f32[2,96,768]{2,1,0:T(8,128)}, u32[]{:S(2)}) copy-start(f32[2,96,768]{2,1,0:T(8,128)} %param.35) | copy-start | bytes 1769476
  886.8 28.8 %copy-start.56 = (f32[2,96,768]{2,1,0:T(8,128)S(1)}, f32[2,96,768]{2,1,0:T(8,128)}, u32[]{:S(2)}) copy-start(f32[2,96,768]{2,1,0:T(8,128)} %param.49) | copy-start | bytes 1769476
  886.8 28.8 %copy-start.57 = (f32[2,96,768]{2,1,0:T(8,128)S(1)}, f32[2,96,768]{2,1,0:T(8,128)}, u32[]{:S(2)}) copy-start(f32[2,96,768]{2,1,0:T(8,128)} %param.42) | copy-start | bytes 1769476
  886.8 28.8 %copy-start.58 = (f32[2,96,768]{2,1,0:T(8,128)S(1)}, f32[2,96,768]{2,1,0:T(8,128)}, u32[]{:S(2)}) copy-start(f32[2,96,768]{2,1,0:T(8,128)} %get-tuple-element.99) | copy-start | bytes 1769476
  (108 other events, 330.4 us)

commit v4 on v3

--- a/solution.py
+++ b/solution.py
@@ -126,46 +126,55 @@
     return own, other
 
 
+def head_mask(lanes, head):
+    return lax.broadcasted_iota(jnp.int32, (1, lanes), 1) // DH == head
+
+
 def forward_kernel(has_bias, causal, centre, scal, q_ref, kvo_ref, kvt_ref, *rest):
     if has_bias:
         rel_ref, mixed_ref, lse_ref, so_ref, st_ref = rest
     else:
         mixed_ref, lse_ref = rest
-    core, key_len, head = scal[0], scal[1], pl.program_id(1)
+    core, key_len = scal[0], scal[1]
     q_rows, k_rows = q_ref.shape[1], kvo_ref.shape[1]
     lanes = q_ref.shape[2]
-    lane_mask = lax.broadcasted_iota(jnp.int32, (1, lanes), 1) // DH == head
+    heads = lanes // DH
     if has_bias:
         own, other = bases_of(lanes, k_rows, core, centre)
-        so_ref[...] = bias_strip(rel_ref[0], own, so_ref.shape[1])
-        st_ref[...] = bias_strip(rel_ref[0], other, st_ref.shape[1])
+        for head in range(heads):
+            so_ref[head] = bias_strip(rel_ref[head], own, so_ref.shape[2])
+            st_ref[head] = bias_strip(rel_ref[head], other, st_ref.shape[2])
+    own_values, oth_values = kvo_ref[0, :, lanes:].T, kvt_ref[0, :, lanes:].T
     step = min(CHUNK, q_rows)
     for col in range(0, q_rows, step):
-        queries = jnp.where(lane_mask, q_ref[0, col : col + step, :], 0.0).astype(bf16)
-        own_s = part_scores(
-            kvo_ref[0, :, :lanes], queries, so_ref if has_bias else None,
-            col, 0, core, key_len, causal,
-        )
-        oth_s = part_scores(
-            kvt_ref[0, :, :lanes], queries, st_ref if has_bias else None,
-            col, 1, core, key_len, causal,
-        )
-        top = jnp.maximum(
-            jnp.max(own_s, axis=0, keepdims=True), jnp.max(oth_s, axis=0, keepdims=True)
-        )
-        own_e, oth_e = jnp.exp(own_s - top), jnp.exp(oth_s - top)
-        total = jnp.sum(own_e, axis=0, keepdims=True) + jnp.sum(oth_e, axis=0, keepdims=True)
-        inverse = 1.0 / total
-        mixed = dot(kvo_ref[0, :, lanes:], (own_e * inverse).astype(bf16), 0, 0)
-        mixed = mixed + dot(kvt_ref[0, :, lanes:], (oth_e * inverse).astype(bf16), 0, 0)
-        mixed = mixed.T.astype(bf16)
-        mixed_ref[0, col : col + step, :] = jnp.where(
-            lane_mask, mixed, mixed_ref[0, col : col + step, :]
-        )
-        lse_ref[0, 0, :, col : col + step] = top + jnp.log(total)
-
-
-def turned(i, j):
+        mixed = []
+        for head in range(heads):
+            mask = head_mask(lanes, head)
+            queries = jnp.where(mask, q_ref[0, col : col + step, :], 0.0).astype(bf16)
+            own_s = part_scores(
+                kvo_ref[0, :, :lanes], queries, so_ref.at[head] if has_bias else None,
+                col, 0, core, key_len, causal,
+            )
+            oth_s = part_scores(
+                kvt_ref[0, :, :lanes], queries, st_ref.at[head] if has_bias else None,
+                col, 1, core, key_len, causal,
+            )
+            top = jnp.maximum(
+                jnp.max(own_s, axis=0, keepdims=True), jnp.max(oth_s, axis=0, keepdims=True)
+            )
+            own_e, oth_e = jnp.exp(own_s - top), jnp.exp(oth_s - top)
+            total = jnp.sum(own_e, axis=0, keepdims=True) + jnp.sum(oth_e, axis=0, keepdims=True)
+            inverse = 1.0 / total
+            rows = slice(head * DH, (head + 1) * DH)
+            mixed.append(
+                dot(own_values[rows], (own_e * inverse).astype(bf16), 1, 0)
+                + dot(oth_values[rows], (oth_e * inverse).astype(bf16), 1, 0)
+            )
+            lse_ref[0, head, :, col : col + step] = top + jnp.log(total)
+        mixed_ref[0, col : col + step, :] = jnp.concatenate(mixed, axis=0).T.astype(bf16)
+
+
+def turned(i):
     return (i + 1 - 2 * (i % 2), 0, 0)
 
 
@@ -177,23 +186,23 @@
     width = q_rows + (k_rows // 128 - 1) * 128
     in_specs = [
         pl.BlockSpec(memory_space=pltpu.SMEM),
-        pl.BlockSpec((1, q_rows, lanes), lambda i, j: (i, 0, 0)),
-        pl.BlockSpec((1, k_rows, 2 * lanes), lambda i, j: (i, 0, 0)),
+        pl.BlockSpec((1, q_rows, lanes), lambda i: (i, 0, 0)),
+        pl.BlockSpec((1, k_rows, 2 * lanes), lambda i: (i, 0, 0)),
         pl.BlockSpec((1, k_rows, 2 * lanes), turned),
     ]
     args = [scal, q, kvo, kvt]
     scratch = []
     if has_bias:
-        in_specs.append(pl.BlockSpec((1, 1, rel_rows.shape[2]), lambda i, j: (i * heads + j, 0, 0)))
+        in_specs.append(pl.BlockSpec((heads, 1, rel_rows.shape[2]), lambda i: (i, 0, 0)))
         args.append(rel_rows)
-        scratch = [pltpu.VMEM((128, width), f32)] * 2
+        scratch = [pltpu.VMEM((heads, 128, width), f32)] * 2
     return pl.pallas_call(
         functools.partial(forward_kernel, has_bias, causal, centre),
-        grid=(groups, heads),
+        grid=(groups,),
         in_specs=in_specs,
         out_specs=[
-            pl.BlockSpec((1, q_rows, lanes), lambda i, j: (i, 0, 0)),
-            pl.BlockSpec((1, 1, 1, q_rows), lambda i, j: (i, j, 0, 0)),
+            pl.BlockSpec((1, q_rows, lanes), lambda i: (i, 0, 0)),
+            pl.BlockSpec((1, heads, 1, q_rows), lambda i: (i, 0, 0, 0)),
         ],
         out_shape=[
             jax.ShapeDtypeStruct((groups, q_rows, lanes), bf16),
@@ -215,70 +224,67 @@
 def backward_kernel(has_bias, causal, centre, scal, q_ref, kvo_ref, kvt_ref, up_ref, lse_ref, *rest):
     if has_bias:
         rel_ref, dq_ref, dkvo_ref, dkvt_ref, drel_ref, so_ref, st_ref, go_ref, gt_ref = rest[:9]
-        dq_acc, ko_acc, vo_acc, kt_acc, vt_acc = rest[9:]
+        ko_acc, vo_acc, kt_acc, vt_acc = rest[9:]
     else:
-        dq_ref, dkvo_ref, dkvt_ref, dq_acc, ko_acc, vo_acc, kt_acc, vt_acc = rest
-    core, key_len, head = scal[0], scal[1], pl.program_id(1)
+        dq_ref, dkvo_ref, dkvt_ref, ko_acc, vo_acc, kt_acc, vt_acc = rest
+    core, key_len = scal[0], scal[1]
     q_rows, k_rows = q_ref.shape[1], kvo_ref.shape[1]
     lanes = q_ref.shape[2]
-    lane_mask = lax.broadcasted_iota(jnp.int32, (1, lanes), 1) // DH == head
+    heads = lanes // DH
     if has_bias:
         own, other = bases_of(lanes, k_rows, core, centre)
-        so_ref[...] = bias_strip(rel_ref[0], own, so_ref.shape[1])
-        st_ref[...] = bias_strip(rel_ref[0], other, st_ref.shape[1])
+        for head in range(heads):
+            so_ref[head] = bias_strip(rel_ref[head], own, so_ref.shape[2])
+            st_ref[head] = bias_strip(rel_ref[head], other, st_ref.shape[2])
         go_ref[...] = jnp.zeros_like(go_ref)
         gt_ref[...] = jnp.zeros_like(gt_ref)
-
-    @pl.when(head == 0)
-    def clear():
-        for acc in (ko_acc, vo_acc, kt_acc, vt_acc):
-            acc[...] = jnp.zeros_like(acc)
-
+    for acc in (ko_acc, vo_acc, kt_acc, vt_acc):
+        acc[...] = jnp.zeros_like(acc)
+    own_keys, oth_keys = kvo_ref[0, :, :lanes].T, kvt_ref[0, :, :lanes].T
     step = min(CHUNK, q_rows)
     for col in range(0, q_rows, step):
-        queries = jnp.where(lane_mask, q_ref[0, col : col + step, :], 0.0).astype(bf16)
-        ups = jnp.where(lane_mask, up_ref[0, col : col + step, :], 0.0).astype(bf16)
-        lse = lse_ref[0, 0, :, col : col + step]
-        sides = []
-        delta = jnp.zeros((1, step), f32)
-        for part, kv_ref, s_ref, k_acc, v_acc in (
-            (0, kvo_ref, so_ref if has_bias else None, ko_acc, vo_acc),
-            (1, kvt_ref, st_ref if has_bias else None, kt_acc, vt_acc),
-        ):
-            scores = part_scores(
-                kv_ref[0, :, :lanes], queries, s_ref, col, part, core, key_len, causal
-            )
-            probs = jnp.exp(scores - lse)
-            v_acc[...] += dot(probs.astype(bf16), ups, 1, 0)
-            dprobs = dot(kv_ref[0, :, lanes:], ups, 1, 1).astype(bf16).astype(f32)
-            delta = delta + jnp.sum(probs * dprobs, axis=0, keepdims=True)
-            sides.append((probs, dprobs))
-        dq = jnp.zeros((lanes, step), f32)
-        for (probs, dprobs), kv_ref, g_ref, k_acc in (
-            (sides[0], kvo_ref, go_ref if has_bias else None, ko_acc),
-            (sides[1], kvt_ref, gt_ref if has_bias else None, kt_acc),
-        ):
-            ds = (probs * (dprobs - delta)).astype(bf16)
-            k_acc[...] += dot(ds, queries, 1, 0)
-            dq = dq + dot(kv_ref[0, :, :lanes], ds, 0, 0)
-            if has_bias:
-                wide_ds = ds.astype(f32)
-                blocks = k_rows // 128
-                for j in range(blocks):
-                    at = (blocks - 1 - j) * 128 + col
-                    g_ref[:, at : at + step] += wide_ds[j * 128 : (j + 1) * 128]
-        dq_acc[col : col + step, :] = jnp.where(
-            lane_mask, dq.T, dq_acc[col : col + step, :]
-        )
+        all_dq = []
+        for head in range(heads):
+            mask = head_mask(lanes, head)
+            queries = jnp.where(mask, q_ref[0, col : col + step, :], 0.0).astype(bf16)
+            ups = jnp.where(mask, up_ref[0, col : col + step, :], 0.0).astype(bf16)
+            lse = lse_ref[0, head, :, col : col + step]
+            sides = []
+            delta = jnp.zeros((1, step), f32)
+            for part, kv_ref, s_ref, v_acc in (
+                (0, kvo_ref, so_ref.at[head] if has_bias else None, vo_acc),
+                (1, kvt_ref, st_ref.at[head] if has_bias else None, vt_acc),
+            ):
+                scores = part_scores(
+                    kv_ref[0, :, :lanes], queries, s_ref, col, part, core, key_len, causal
+                )
+                probs = jnp.exp(scores - lse)
+                v_acc[...] += dot(probs.astype(bf16), ups, 1, 0)
+                dprobs = dot(kv_ref[0, :, lanes:], ups, 1, 1).astype(bf16).astype(f32)
+                delta = delta + jnp.sum(probs * dprobs, axis=0, keepdims=True)
+                sides.append((probs, dprobs))
+            dq = jnp.zeros((DH, step), f32)
+            for (probs, dprobs), keys, g_ref, k_acc in (
+                (sides[0], own_keys, go_ref if has_bias else None, ko_acc),
+                (sides[1], oth_keys, gt_ref if has_bias else None, kt_acc),
+            ):
+                ds = (probs * (dprobs - delta)).astype(bf16)
+                k_acc[...] += dot(ds, queries, 1, 0)
+                dq = dq + dot(keys[head * DH : (head + 1) * DH], ds, 1, 0)
+                if has_bias:
+                    wide_ds = ds.astype(f32)
+                    blocks = k_rows // 128
+                    for j in range(blocks):
+                        at = (blocks - 1 - j) * 128 + col
+                        g_ref[head, :, at : at + step] += wide_ds[j * 128 : (j + 1) * 128]
+            all_dq.append(dq)
+        dq_ref[0, col : col + step, :] = jnp.concatenate(all_dq, axis=0).T.astype(bf16)
     if has_bias:
-        drel_ref[0, 0, 0] = fold(go_ref[...])
-        drel_ref[0, 0, 1] = fold(gt_ref[...])
-
-    @pl.when(head == pl.num_programs(1) - 1)
-    def write():
-        dq_ref[0] = dq_acc[...].astype(bf16)
-        dkvo_ref[0] = jnp.concatenate([ko_acc[...], vo_acc[...]], axis=1)
-        dkvt_ref[0] = jnp.concatenate([kt_acc[...], vt_acc[...]], axis=1).astype(bf16)
+        for head in range(heads):
+            drel_ref[0, head, 0] = fold(go_ref[head])
+            drel_ref[0, head, 1] = fold(gt_ref[head])
+    dkvo_ref[0] = jnp.concatenate([ko_acc[...], vo_acc[...]], axis=1)
+    dkvt_ref[0] = jnp.concatenate([kt_acc[...], vt_acc[...]], axis=1).astype(bf16)
 
 
 def attend_back(scal, q, kvo, kvt, up, lse, rel_rows, centre, causal):
@@ -288,14 +294,14 @@
     has_bias = rel_rows is not None
     width = q_rows + (k_rows // 128 - 1) * 128
     gwidth = width + 128
-    per_group = lambda i, j: (i, 0, 0)
+    per_group = lambda i: (i, 0, 0)
     in_specs = [
         pl.BlockSpec(memory_space=pltpu.SMEM),
         pl.BlockSpec((1, q_rows, lanes), per_group),
         pl.BlockSpec((1, k_rows, 2 * lanes), per_group),
         pl.BlockSpec((1, k_rows, 2 * lanes), turned),
         pl.BlockSpec((1, q_rows, lanes), per_group),
-        pl.BlockSpec((1, 1, 1, q_rows), lambda i, j: (i, j, 0, 0)),
+        pl.BlockSpec((1, heads, 1, q_rows), lambda i: (i, 0, 0, 0)),
     ]
     args = [scal, q, kvo, kvt, up, lse]
     out_specs = [
@@ -310,15 +316,16 @@
     ]
     scratch = []
     if has_bias:
-        in_specs.append(pl.BlockSpec((1, 1, rel_rows.shape[2]), lambda i, j: (i * heads + j, 0, 0)))
+        in_specs.append(pl.BlockSpec((heads, 1, rel_rows.shape[2]), lambda i: (i, 0, 0)))
         args.append(rel_rows)
-        out_specs.append(pl.BlockSpec((1, 1, 2, 8, gwidth), lambda i, j: (i, j, 0, 0, 0)))
+        out_specs.append(pl.BlockSpec((1, heads, 2, 8, gwidth), lambda i: (i, 0, 0, 0, 0)))
         out_shape.append(jax.ShapeDtypeStruct((groups, heads, 2, 8, gwidth), f32))
-        scratch = [pltpu.VMEM((128, width), f32)] * 2 + [pltpu.VMEM((128, gwidth), f32)] * 2
-    scratch = scratch + [pltpu.VMEM((q_rows, lanes), f32)] + [pltpu.VMEM((k_rows, lanes), f32)] * 4
+        scratch = [pltpu.VMEM((heads, 128, width), f32)] * 2
+        scratch = scratch + [pltpu.VMEM((heads, 128, gwidth), f32)] * 2
+    scratch = scratch + [pltpu.VMEM((k_rows, lanes), f32)] * 4
     return pl.pallas_call(
         functools.partial(backward_kernel, has_bias, causal, centre),
-        grid=(groups, heads),
+        grid=(groups,),
         in_specs=in_specs,
         out_specs=out_specs,
         out_shape=out_shape,
@@ -383,14 +390,15 @@
 
 
 START_ORDER = (
-    (0, 1), (1, 0), (2, 0), (0, 2), (9, 7), (1, 1), (5, 0),
-    (0, 3), (1, 2), (2, 1), (3, 0), (2, 2), (4, 0), (9, 3), (9, 5),
-    (3, 1), (9, 1), (5, 1), (1, 3), (8, 1), (9, 6), (3, 2), (2, 3),
-    (4, 1), (6, 0), (4, 2), (1, 5), (8, 3), (3, 3), (6, 1), (0, 5),
-    (4, 3), (7, 3), (8, 2), (5, 2), (9, 2), (7, 1), (3, 5), (5, 3),
-    (6, 2), (9, 4), (7, 2), (4, 5), (8, 0), (6, 3), (9, 0), (7, 0),
-    (2, 5), (5, 5), (6, 5),
+    (9, 7), (0, 1), (1, 0), (0, 2), (9, 3), (2, 0), (1, 1), (6, 1),
+    (1, 2), (0, 3), (4, 0), (2, 1), (3, 0), (2, 2), (1, 3), (3, 1),
+    (6, 2), (5, 0), (8, 3), (3, 2), (0, 5), (9, 5), (4, 1), (9, 1),
+    (2, 3), (9, 6), (8, 1), (9, 2), (4, 2), (8, 2), (9, 4), (3, 3),
+    (6, 3), (1, 5), (5, 1), (7, 3), (4, 3), (9, 0), (7, 1), (5, 2),
+    (7, 2), (5, 3), (2, 5), (3, 5), (4, 5), (8, 0), (6, 5), (5, 5),
+    (7, 0),
 )
+OTHER_WAY = 6
 
 
 def start_kernel(
@@ -421,23 +429,31 @@
     vocab = table_in.shape[0]
 
     def own(j):
-        return pltpu.make_async_copy(shard_ref.at[j], full_refs[j].at[0, z2, z1, x], own_sem.at[j])
+        return pltpu.make_async_copy(
+            shard_ref.at[j], full_refs[j].at[0, 0, z2, z1, x], own_sem.at[j]
+        )
 
     def copy(j, stage):
-        if stage == 0:
-            src, dst, peer = shard_ref.at[j], full_refs[j].at[0, z2, z1, x], at_z2
-        elif stage == 1:
-            src = dst = full_refs[j].at[0, :, z1, x]
-            peer = at_z1
-        elif stage == 2:
-            src = dst = full_refs[j].at[0, :, :, x]
-            peer = at_x
-        elif stage == 3:
-            src, dst, peer = full_refs[j].at[0], full_refs[j].at[2], at_y
-        elif stage == 4:
-            src, dst, peer = full_refs[j].at[0], full_refs[j].at[1], at_core
+        full, shard = full_refs[j], shard_ref.at[j]
+        mine = full.at[0, 0, z2, z1, x]
+        if j == OTHER_WAY:
+            src, dst, peer = (
+                (shard, mine, at_x),
+                (full.at[0, 0, z2, z1], full.at[1, 0, z2, z1], at_y),
+                (full.at[:, 0, z2, z1], full.at[:, 0, z2, z1], at_z1),
+                (full.at[:, 0, z2], full.at[:, 0, z2], at_z2),
+                None,
+                (full.at[:, 0], full.at[:, 1], at_core),
+            )[stage]
         else:
-            src, dst, peer = full_refs[j].at[2], full_refs[j].at[3], at_core
+            src, dst, peer = (
+                (shard, mine, at_z2),
+                (full.at[0, 0, :, z1, x], full.at[0, 0, :, z1, x], at_z1),
+                (full.at[0, 0, :, :, x], full.at[0, 0, :, :, x], at_x),
+                (full.at[0, 0], full.at[1, 0], at_y),
+                (full.at[0, 0], full.at[0, 1], at_core),
+                (full.at[1, 0], full.at[1, 1], at_core),
+            )[stage]
         return remote(src, dst, w_send.at[j, stage], w_recv.at[j, stage], peer)
 
     def advance(j, stage):
@@ -446,7 +462,7 @@
         if stage > 0:
             copy(j, {5: 3}.get(stage, stage - 1)).wait_recv()
         copy(j, stage).start()
-        if stage == 3:
+        if stage == 3 and j != OTHER_WAY:
             copy(j, 4).start()
 
     def ids_copy(r):
@@ -473,6 +489,7 @@
     for j in range(units):
         own(j).start()
     advance(0, 0)
+    advance(6, 0)
     for r in range(1, 8):
         ids_copy(r).start()
     for g in range(1, 4):
@@ -541,9 +558,10 @@
     for g, index in enumerate((narrow, at_core[1], at_y[1], at_both[1])):
         small_sorted[index] = small_all[g]
     for j in range(units):
-        for stage in range(6):
+        core_stages = (5,) if j == OTHER_WAY else (4, 5)
+        for stage in (0, 1, 2, 3, *core_stages):
             copy(j, stage).wait_send()
-        for stage in (4, 5):
+        for stage in core_stages:
             copy(j, stage).wait_recv()
     for r in range(1, 8):
         ids_copy(r).wait_send()
@@ -563,7 +581,7 @@
         functools.partial(start_kernel, units),
         in_specs=[vmem, vmem, any_space, any_space],
         out_specs=[any_space] * units + [vmem] * 5,
-        out_shape=[jax.ShapeDtypeStruct((4, 2, 2, 2, slim, columns), bf16)] * units
+        out_shape=[jax.ShapeDtypeStruct((2, 2, 2, 2, 2, slim, columns), bf16)] * units
         + [
             jax.ShapeDtypeStruct((rows, width), bf16),
             jax.ShapeDtypeStruct((padded, width), bf16),

time: 933 us -> 879 us (0.942)
  Pallas kernels: 707 us -> 653 us
    pallas_call x3, Pallas kernels: 73.4 us -> 52 us  [attend_back(): pl.pallas_call(functools.partial(backward_kernel, has_bias, causal, centr...]
    pallas_call x1, Pallas kernels: 228 us -> 209 us  [start_phase(): pl.pallas_call(functools.partial(start_kernel, units), in_specs=[vmem, vm...]
    pallas_call x3, Pallas kernels: 45 us -> 29.5 us  [attend(): pl.pallas_call(functools.partial(forward_kernel, has_bias, causal, centre...]
  transfers between devices with their start and end apart: 6 -> 6, of which waited for: 1 -> 1; matrix products, arithmetic and copies ran while one was open for 7% -> 7% of each run, Pallas kernels for 4% -> 2%
where the time goes in v4:
time: 879 us; the launch traced here: 868 us
  Pallas kernels  653 us (74%)
  matrix products  94.1 us (11%)
  other arithmetic  64.3 us (7%)
  local copies, waits for them, and re-layouts  47.1 us (5%)
    pallas_call x1, Pallas kernels, end_phase(): pl.pallas_call(functools.partial(end_kernel, kinds, places), in_specs=[an...  283 us
    pallas_call x1, Pallas kernels, start_phase(): pl.pallas_call(functools.partial(start_kernel, units), in_specs=[vmem, vm...  209 us
    pallas_call x1, Pallas kernels, head_phase(): pl.pallas_call(functools.partial(head_kernel, vocab), in_specs=[vmem] * 5...  79.8 us
    pallas_call x3, Pallas kernels, attend_back(): pl.pallas_call(functools.partial(backward_kernel, has_bias, causal, centr...  52 us
    dot_general x13, matrix products, project(): return jnp.einsum('rk,nkc->nrc', rows, weights, preferred_element_type=f32)  50 us
    dot_general x13, matrix products, project_back(): return jnp.einsum('nrc,nkc->rk', grads, weights, preferred_element_type=f32)  42.1 us
    add x7, other arithmetic, body(): average_decay * avgs[index] + (1.0 - average_decay) * weight  36.2 us
    pallas_call x3, Pallas kernels, attend(): pl.pallas_call(functools.partial(forward_kernel, has_bias, causal, centre...  29.5 us
  transfers between devices with their start and end apart: 6, of which 1 were waited for; matrix products, arithmetic and copies ran while one was open for 7% of the time, Pallas kernels for 2%

profile of v4, /device:TPU:0, one launch (start us, length us, event | category | flops | bytes accessed | tf_op | source)
XLA Modules:
  0.0 867.8 jit_solution(4707669759706923276)
XLA Ops:
  7.5 208.8 %shard_map.442 = (bf16[2,2,2,2,2,96,768]{6,5,4,3,2,1,0:T(8,128)(2,1)}, bf16[2,2,2,2,2,96,768]{6,5,4,3,2,1,0:T(8,128)(2,1)}, bf16[2,2,2,2,2,96,768]{6,5,4,3,2,1,0...) custom-call(s32[1,640]{1,0:T(1,128)S(1)} %broadcast_in_dim.14.ids_re, ...), custom_call_target="tpu_custom_call" | custom-call | flops 32212254720 | bytes 33030144 | tf_op jit(solution)/shard_map/pallas_call | solution.py:580
  217.2 4.9 fusion.64.kvo_ref
  222.8 2.9 fusion.95.kvo_ref
  226.0 3.4 convolution_convert_fusion.1
  236.0 2.8 fusion.135
  238.8 17.3 %shard_map.444 = (bf16[4,512,192]{2,1,0:T(8,128)(2,1)S(1)}, f32[4,3,1,512]{3,2,1,0:T(1,128)S(1)}) custom-call(s32[2]{0:T(128)S(1)} %pad_add_fusion.1.scal, bf16[4,512,192]{2,1,0:T(8,128)(2,1)S(1)} %bitcast.347, bf16[4,512,384]{2,1,0:T(8,128)(2,1)} %fusion.64.kvo_ref, bf16[4,512,384]{2,1,0:T(8,128)(2,1)} %collective-permute-done.1.kvt_ref, ...), custom_call_target="tpu_custom_call" | custom-call | tf_op jit(solution)/shard_map/pallas_call | solution.py:199
  256.1 3.0 multiply_reduce_fusion.1
  259.5 5.6 fusion.10
  265.2 2.7 multiply_reduce_fusion
  283.9 4.2 shard_map.443
  292.0 2.8 fusion.141
  295.9 7.9 shard_map.445
  306.5 4.7 fusion.60
  313.7 79.8 %shard_map.446 = (f32[128,768]{1,0:T(8,128)}, bf16[4096,768]{1,0:T(8,128)(2,1)}, f32[1,128]{1,0:T(1,128)}) custom-call(bf16[128,768]{1,0:T(8,128)(2,1)} %multiply_convert_fusion.2.final_ref, bf16[4096,768]{1,0:T(8,128)(2,1)} %get-tuple-element.76.table_ref, s32[8,128]{1,0:T(8,128)} %get-tuple-element.279.target_ref, f32[1,128]{1,0:T(1,128)} %slice.388.weight_ref, ...), custom_call_target="tpu_custom_call" | custom-call | flops 19327352832 | bytes 20971520 | tf_op jit(solution)/shard_map/pallas_call | solution.py:795
  396.3 4.0 fusion.35.refs_11_
  400.3 4.9 multiply_reduce_fusion.2
  406.9 3.2 fusion.144
  413.5 13.4 %shard_map.447 = (bf16[4,128,192]{2,1,0:T(8,128)(2,1)S(1)}, f32[4,512,384]{2,1,0:T(8,128)S(1)}, bf16[4,512,384]{2,1,0:T(8,128)(2,1)}) custom-call(s32[2]{0:T(128)S(1)} %pad_add_fusion.1.scal, bf16[4,128,192]{2,1,0:T(8,128)(2,1)S(1)} %bitcast.353, bf16[4,512,384]{2,1,0:T(8,128)(2,1)} %fusion.61.kvo_ref, bf16[4,512,384]{2,1,0:T(8,128)(2,1)} %collective-permute-done.2.kvt_ref, ...), custom_call_target="tpu_custom_call" | custom-call | tf_op jit(solution)/shard_map/pallas_call | solution.py:326
  427.0 4.0 multiply_reduce_fusion.3
  432.6 3.2 fusion.138
  436.9 9.9 %shard_map.448 = (bf16[4,128,192]{2,1,0:T(8,128)(2,1)S(1)}, f32[4,128,384]{2,1,0:T(8,128)S(1)}, bf16[4,128,384]{2,1,0:T(8,128)(2,1)}, f32[4,3,2,8,256]{4,3,2,1,0:T(8,128)S(1)}) custom-call(s32[2]{0:T(128)S(1)} %pad_add_fusion.1.scal, bf16[4,128,192]{2,1,0:T(8,128)(2,1)S(1)} %bitcast.351, bf16[4,128,384]{2,1,0:T(8,128)(2,1)S(1)} %fusion.95.kvo_ref, ...), custom_call_target="tpu_custom_call" | custom-call | tf_op jit(solution)/shard_map/pallas_call | solution.py:326
  453.3 3.1 fusion.110
  456.4 2.8 fusion.170
  461.4 5.1 fusion.40
  468.0 6.1 fusion.6.refs_19_
  474.1 2.8 fusion.46
  479.7 3.8 convolution_convert_fusion
  485.0 28.8 %shard_map.449 = (bf16[4,512,192]{2,1,0:T(8,128)(2,1)S(1)}, f32[4,512,384]{2,1,0:T(8,128)S(1)}, bf16[4,512,384]{2,1,0:T(8,128)(2,1)}, f32[4,3,2,8,1024]{4,3,2,1,0:T(8,128)S(1)}) custom-call(s32[2]{0:T(128)S(1)} %pad_add_fusion.1.scal, bf16[4,512,192]{2,1,0:T(8,128)(2,1)S(1)} %bitcast.348, bf16[4,512,384]{2,1,0:T(8,128)(2,1)} %fusion.64.kvo_ref, ...), custom_call_target="tpu_custom_call" | custom-call | tf_op jit(solution)/shard_map/pallas_call | solution.py:326
  524.5 4.5 fusion.55
  533.3 282.6 %shard_map.450 = (f32[3,96,576]{2,1,0:T(8,128)}, f32[3,192,96]{2,1,0:T(8,128)}, f32[2,96,768]{2,1,0:T(8,128)}, f32[2,768,96]{2,1,0:T(8,128)}, bf16[4,1024,768]{2...) custom-call(bf16[128,768]{1,0:T(8,128)(2,1)} %copy-done.68, ...), custom_call_target="tpu_custom_call" | custom-call | flops 32212254720 | bytes 104857600 | tf_op jit(solution)/shard_map/pallas_call | solution.py:1163
  823.7 2.8 multiply_add_fusion.1
  832.1 28.8 %multiply_add_fusion = (f32[4016,768]{1,0:T(8,128)}, f32[4016,768]{1,0:T(8,128)}, f32[4016,768]{1,0:T(8,128)}) fusion(f32[4016,768]{1,0:T(8,128)} %param.51, f32[4016,768]{1,0:T(8,128)} %table_in.1, f32[4016,768]{1,0:T(8,128)} %param.44, f32[]{:T(128)S(6)} %min.3, bf16[4096,768]{1,0:T(8,128)(2,1)} %bitcast.360), kind=kLoop, calls=%fused_computation.3 | loop fusion | flops 33927168 | bytes 80191488 | tf_op jit(solution)/shard_map/add | solution.py:1532
  (497 shorter events, 96.7 us)
Async XLA Ops:
  217.1 8.9 %copy-start.48 = (bf16[512,768]{1,0:T(8,128)(2,1)}, bf16[512,768]{1,0:T(8,128)(2,1)S(1)}, u32[]{:S(2)}) copy-start(bf16[512,768]{1,0:T(8,128)(2,1)S(1)} %fusion.52.refs_9_) | copy-start | bytes 2359300
  222.1 16.7 %collective-permute-start.1 = (bf16[4,512,384]{2,1,0:T(8,128)(2,1)}, bf16[4,512,384]{2,1,0:T(8,128)(2,1)}, u32[]{:S(2)}, u32[]{:S(2)}) collective-permute-start(bf16[4,512,384]{2,1,0:T(8,128)(2,1)} %fusion.64.kvo_ref), channel_id=1, source_target_pairs={{0,1},{1,0},{2,3},{3,2},{4,5},{5,4},{6,7},{7,6},{8,9},{9,8},{10,11... | collective-permute-start | bytes 4718600 | tf_op jit(solution)/shard_map/ppermute | solution.py:33
  225.8 58.1 %collective-permute-start = (bf16[4,128,384]{2,1,0:T(8,128)(2,1)S(1)}, bf16[4,128,384]{2,1,0:T(8,128)(2,1)S(1)}, u32[]{:S(2)}, u32[]{:S(2)}) collective-permute-start(bf16[4,128,384]{2,1,0:T(8,128)(2,1)S(1)} %fusion.95.kvo_ref), channel_id=1, source_target_pairs={{0,1},{1,0},{2,3},{3,2},{4,5},{5,4},{6,7},{7,6},{8,9},{9,8},{10,11... | collective-permute-start | bytes 1179656 | tf_op jit(solution)/shard_map/ppermute | solution.py:33
  233.3 26.0 %copy-start.73 = (f32[768]{0:T(1024)}, f32[768]{0:T(1024)S(1)}, u32[]{:S(2)}) copy-start(f32[768]{0:T(1024)S(1)} %mul.834) | copy-start | bytes 9220
  233.3 34.6 %copy-start.70 = (f32[768]{0:T(1024)}, f32[768]{0:T(1024)S(1)}, u32[]{:S(2)}) copy-start(f32[768]{0:T(1024)S(1)} %mul.844) | copy-start | bytes 9220
  271.2 24.6 %collective-permute-start.2 = (bf16[4,512,384]{2,1,0:T(8,128)(2,1)}, bf16[4,512,384]{2,1,0:T(8,128)(2,1)}, u32[]{:S(2)}, u32[]{:S(2)}) collective-permute-start(bf16[4,512,384]{2,1,0:T(8,128)(2,1)} %fusion.61.kvo_ref), channel_id=1, source_target_pairs={{0,1},{1,0},{2,3},{3,2},{4,5},{5,4},{6,7},{7,6},{8,9},{9,8},{10,11... | collective-permute-start | bytes 4718600 | tf_op jit(solution)/shard_map/ppermute | solution.py:33
  295.9 8.0 copy-start.31
  303.9 7.3 slice-start
  413.5 13.4 %copy-start.32 = (f32[128,768]{1,0:T(8,128)S(1)}, f32[128,768]{1,0:T(8,128)}, u32[]{:S(2)}) copy-start(f32[128,768]{1,0:T(8,128)} %copy-done.30) | copy-start | bytes 1179652
  413.5 13.4 %copy-start.78 = (f32[768]{0:T(1024)S(1)}, f32[768]{0:T(1024)}, u32[]{:S(2)}) copy-start(f32[768]{0:T(1024)} %mul.822) | copy-start | bytes 9220
  413.5 13.4 %copy-start.110 = (f32[128]{0:T(128)S(1)}, f32[128]{0:T(128)}, u32[]{:S(2)}) copy-start(f32[128]{0:T(128)} %copy-done.109) | copy-start | bytes 1540
  435.8 14.1 %copy-start.92 = (f32[768]{0:T(1024)S(1)}, f32[768]{0:T(1024)}, u32[]{:S(2)}) copy-start(f32[768]{0:T(1024)} %get-tuple-element.186) | copy-start | bytes 9220
  436.9 13.0 %copy-start.104 = (f32[768]{0:T(1024)S(1)}, f32[768]{0:T(1024)}, u32[]{:S(2)}) copy-start(f32[768]{0:T(1024)} %get-tuple-element.184) | copy-start | bytes 9220
  436.9 13.0 %copy-start.94 = (f32[768]{0:T(1024)S(1)}, f32[768]{0:T(1024)}, u32[]{:S(2)}) copy-start(f32[768]{0:T(1024)} %get-tuple-element.182) | copy-start | bytes 9220
  436.9 13.4 %copy-start.26 = (pred[2047,32]{1,0:T(8,128)(4,1)S(1)}, pred[2047,32]{1,0:T(8,128)(4,1)}, u32[]{:S(2)}) copy-start(pred[2047,32]{1,0:T(8,128)(4,1)} %copy-done.25) | copy-start | bytes 196516
  449.2 10.1 %collective-permute-start.3 = (bf16[4,512,384]{2,1,0:T(8,128)(2,1)}, bf16[4,512,384]{2,1,0:T(8,128)(2,1)}, u32[]{:S(2)}, u32[]{:S(2)}) collective-permute-start(bf16[4,512,384]{2,1,0:T(8,128)(2,1)} %get-tuple-element.81), channel_id=1, source_target_pairs={{0,1},{1,0},{2,3},{3,2},{4,5},{5,4},{6,7},{7,6},{8,9},{9,8},{10,11... | collective-permute-start | bytes 4718600 | tf_op jit(solution)/shard_map/ppermute | solution.py:33
  449.3 3.8 collective-permute-start.4
  459.3 8.6 slice-start.10
  459.3 8.5 slice-start.12
  466.6 7.5 slice-start.6
  485.0 30.1 %copy-start.42 = (f32[128,768]{1,0:T(8,128)S(1)}, f32[128,768]{1,0:T(8,128)}, u32[]{:S(2)}) copy-start(f32[128,768]{1,0:T(8,128)} %get-tuple-element.219) | copy-start | bytes 1179652
  485.0 30.1 %copy-start.60 = (f32[128,768]{1,0:T(8,128)S(1)}, f32[128,768]{1,0:T(8,128)}, u32[]{:S(2)}) copy-start(f32[128,768]{1,0:T(8,128)} %get-tuple-element.277) | copy-start | bytes 1179652
  514.8 7.8 collective-permute-start.5
  533.3 288.6 %copy-start.96 = (f32[2,32,3]{1,0,2:T(2,128)S(1)}, f32[2,32,3]{1,0,2:T(2,128)}, u32[]{:S(2)}) copy-start(f32[2,32,3]{1,0,2:T(2,128)} %param.39) | copy-start | bytes 2308
  533.3 288.6 %copy-start.105 = (f32[2,32,3]{1,0,2:T(2,128)S(1)}, f32[2,32,3]{1,0,2:T(2,128)}, u32[]{:S(2)}) copy-start(f32[2,32,3]{1,0,2:T(2,128)} %param.53) | copy-start | bytes 2308
  533.3 288.6 %copy-start.106 = (f32[2,32,3]{1,0,2:T(2,128)S(1)}, f32[2,32,3]{1,0,2:T(2,128)}, u32[]{:S(2)}) copy-start(f32[2,32,3]{1,0,2:T(2,128)} %param.46) | copy-start | bytes 2308
  533.3 290.4 %copy-start.33 = (f32[2,768,96]{2,1,0:T(8,128)S(1)}, f32[2,768,96]{2,1,0:T(8,128)}, u32[]{:S(2)}) copy-start(f32[2,768,96]{2,1,0:T(8,128)} %copy.252) | copy-start | bytes 1769476
  533.3 290.4 %copy-start.34 = (f32[2,768,96]{2,1,0:T(8,128)S(1)}, f32[2,768,96]{2,1,0:T(8,128)}, u32[]{:S(2)}) copy-start(f32[2,768,96]{2,1,0:T(8,128)} %copy.251) | copy-start | bytes 1769476
  832.1 28.8 %copy-start.38 = (f32[2,96,768]{2,1,0:T(8,128)S(1)}, f32[2,96,768]{2,1,0:T(8,128)}, u32[]{:S(2)}) copy-start(f32[2,96,768]{2,1,0:T(8,128)} %param.35) | copy-start | bytes 1769476
  832.1 28.8 %copy-start.56 = (f32[2,96,768]{2,1,0:T(8,128)S(1)}, f32[2,96,768]{2,1,0:T(8,128)}, u32[]{:S(2)}) copy-start(f32[2,96,768]{2,1,0:T(8,128)} %param.49) | copy-start | bytes 1769476
  832.1 28.8 %copy-start.57 = (f32[2,96,768]{2,1,0:T(8,128)S(1)}, f32[2,96,768]{2,1,0:T(8,128)}, u32[]{:S(2)}) copy-start(f32[2,96,768]{2,1,0:T(8,128)} %param.42) | copy-start | bytes 1769476
  832.1 28.8 %copy-start.58 = (f32[2,96,768]{2,1,0:T(8,128)S(1)}, f32[2,96,768]{2,1,0:T(8,128)}, u32[]{:S(2)}) copy-start(f32[2,96,768]{2,1,0:T(8,128)} %get-tuple-element.99) | copy-start | bytes 1769476
  (108 other events, 330.8 us)

commit v5 on v4

--- a/solution.py
+++ b/solution.py
@@ -830,15 +830,17 @@
 
 
 HELD = 4
-X_FIRST = (5, 6, )
+X_FIRST = (6, )
+Z_FIRST = (5, )
 END_ORDER = (
-    (0, 0), (1, 0), (0, 1), (6, 3), (1, 1), (6, 5), (9, 0), (0, 2),
-    (1, 2), (2, 0), (0, 3), (6, 6), (1, 3), (2, 1), (3, 0), (9, 1),
-    (0, 4), (6, 7), (1, 4), (3, 1), (0, 5), (1, 5), (7, 0), (7, 1),
-    (2, 2), (7, 2), (7, 3), (2, 5), (8, 0), (2, 3), (3, 2), (0, 6),
-    (4, 1), (8, 1), (4, 0), (1, 6), (3, 5), (2, 6), (3, 3), (4, 5),
-    (5, 5), (8, 2), (5, 1), (4, 3), (3, 6), (4, 2), (2, 4), (4, 6),
-    (5, 3), (3, 4), (5, 6), (5, 2), (4, 4), (8, 3), (5, 4), (5, 0),
+    (0, 0), (1, 0), (6, 3), (0, 1), (1, 1), (6, 5), (6, 6), (2, 0),
+    (9, 0), (0, 2), (1, 2), (0, 3), (1, 3), (2, 1), (3, 0), (9, 1),
+    (0, 4), (1, 4), (6, 7), (3, 1), (0, 5), (1, 5), (2, 2), (7, 0),
+    (7, 1), (8, 0), (3, 2), (0, 6), (8, 1), (2, 3), (7, 2), (1, 6),
+    (4, 2), (8, 2), (7, 3), (8, 4), (2, 5), (2, 4), (8, 5), (2, 6),
+    (3, 3), (4, 1), (8, 3), (3, 5), (3, 4), (5, 1), (4, 0), (4, 4),
+    (8, 6), (4, 3), (3, 6), (4, 6), (5, 0), (5, 3), (5, 2), (5, 4),
+    (4, 5), (8, 7), (5, 6), (5, 5),
 )
 
 
@@ -931,6 +933,13 @@
         slot = j % HELD
         if hop_at == 0:
             src, dst, peer = send_c, c_in.at[j], narrow_peer(1)
+        elif j in Z_FIRST:
+            src, dst, peer = (
+                (held.at[slot, :, 1 - z2], y_in.at[j], wide_peer(4)),
+                (held.at[slot, :, z2, 1 - z1], x_in.at[j], wide_peer(2)),
+                (x_in.at[j, :, 1 - x], z1_in.at[j], wide_peer(1)),
+                (z1_in.at[j, 1], z2_in.at[j], narrow_peer(2)),
+            )[hop_at - 1]
         elif hop_at == 1 and j in X_FIRST:
             src, dst, peer = held.at[slot, :, :, :, 1 - x], y_in.at[j], wide_peer(1)
         elif hop_at == 1:
@@ -975,9 +984,9 @@
         staged(c_in.at[j], stage)
         for side in (1, 0):
             held[j % HELD, side] = added(held[j % HELD, side], stage[side])
-            if side == 1 and j not in X_FIRST:
+            if side == 1 and j not in X_FIRST + Z_FIRST:
                 w_copy(j, 1).start()
-        if j in X_FIRST:
+        if j in X_FIRST + Z_FIRST:
             w_copy(j, 1).start()
 
     def after_first(j):
@@ -988,23 +997,29 @@
                 held[j % HELD, side, :, :, x] = added(held[j % HELD, side, :, :, x], stage[0, side])
                 if side == 1:
                     w_copy(j, 2).start()
+        elif j in Z_FIRST:
+            held[j % HELD, :, z2] = added(held[j % HELD, :, z2], stage[0])
+            w_copy(j, 2).start()
         else:
             held[j % HELD, 0] = added(held[j % HELD, 0], stage[0])
             w_copy(j, 2).start()
 
     def after_second(j):
         w_copy(j, 2).wait()
-        x_in[j] = added(x_in[j], held[j % HELD, 0, :, :, x])
+        if j in Z_FIRST:
+            x_in[j] = added(x_in[j], held[j % HELD, :, z2, z1])
+        else:
+            x_in[j] = added(x_in[j], held[j % HELD, 0, :, :, x])
         w_copy(j, 3).start()
 
     def after_z1(j):
         w_copy(j, 3).wait()
-        z1_in[j] = added(z1_in[j], x_in[j, :, z1])
+        z1_in[j] = added(z1_in[j], x_in[j, :, x if j in Z_FIRST else z1])
         w_copy(j, 4).start()
 
     def after_z2(j):
         w_copy(j, 4).wait()
-        total = z2_in[j].astype(f32) + z1_in[j, z2].astype(f32)
+        total = z2_in[j].astype(f32) + z1_in[j, 0 if j in Z_FIRST else z2].astype(f32)
         note(total)
         what, layer = places[j]
         if what == 0:
@@ -1031,40 +1046,43 @@
     tokens = gathered.shape[1]
     step = 256
 
+    half = quarter // 2
+    per = half // step
+
     def scatter_rows(part):
         def chunk(k, unused):
-            per = quarter // step
-            at = pl.ds(pl.multiple_of(k % per * step, step), step)
-            slot = lax.broadcasted_iota(jnp.int32, (step, 1), 0) + k * step
+            which = 2 * (part % 2) + k // per
+            first = part // 2 * half + k % per * step
+            at = pl.ds(pl.multiple_of(first, step), step)
+            slot = lax.broadcasted_iota(jnp.int32, (step, 1), 0) + which * quarter + first
             hot = jnp.concatenate(
                 [(slot == ids_ref[r]).astype(f32).astype(bf16) for r in range(8)], axis=1
             )
-            total = table_vm[k // per, at, :].astype(f32)
+            total = table_vm[which, at, :].astype(f32)
             total = total + dot(hot, gathered[...].reshape(8 * tokens, width), 1, 0)
-            table_vm[k // per, at, :] = total.astype(bf16)
+            table_vm[which, at, :] = total.astype(bf16)
             return unused
 
-        count = quarter // step
-        lax.fori_loop(part * count, (part + 1) * count, chunk, 0)
-
-    def t_copy(at):
-        if at == 0:
-            src, dst, peer = table_vm.at[1 - core], table_c.at[0], narrow_peer(1)
-        elif at == 1:
-            src, dst, peer = table_vm.at[3 - core], table_c.at[1], narrow_peer(1)
-        elif at == 2:
-            src, dst, peer = table_vm.at[2 * (1 - y) + core], table_y, narrow_peer(2)
-        elif at == 3:
-            src, dst, peer = table_vm.at[narrow], table_out.at[narrow], narrow_peer(2)
-        elif at == 4:
-            src, dst, peer = table_vm.at[narrow], table_out.at[narrow], narrow_peer(1)
-        else:
-            there = 2 * (1 - y) + core
-            src, dst, peer = table_out.at[there], table_out.at[there], narrow_peer(1)
-        return remote(src, dst, t_send.at[at], t_recv.at[at], peer)
-
-    def own_quarter():
-        return pltpu.make_async_copy(table_vm.at[narrow], table_out.at[narrow], own_sem.at[0])
+        lax.fori_loop(0, 2 * per, chunk, 0)
+
+    def t_copy(number):
+        at, part = number % 6, pl.ds(number // 6 * half, half)
+        there = 2 * (1 - y) + core
+        src, dst, peer = (
+            (table_vm.at[1 - core, part], table_c.at[0, part], narrow_peer(1)),
+            (table_vm.at[3 - core, part], table_c.at[1, part], narrow_peer(1)),
+            (table_vm.at[there, part], table_y.at[part], narrow_peer(2)),
+            (table_vm.at[narrow, part], table_out.at[narrow, part], narrow_peer(2)),
+            (table_vm.at[narrow, part], table_out.at[narrow, part], narrow_peer(1)),
+            (table_out.at[there, part], table_out.at[there, part], narrow_peer(1)),
+        )[at]
+        return remote(src, dst, t_send.at[number], t_recv.at[number], peer)
+
+    def own_half(side):
+        part = pl.ds(side * half, half)
+        return pltpu.make_async_copy(
+            table_vm.at[narrow, part], table_out.at[narrow, part], own_sem.at[3 + side]
+        )
 
     def head_load():
         return pltpu.make_async_copy(head_ref, table_vm, own_sem.at[1])
@@ -1082,28 +1100,30 @@
     for r in (1, 4, 2):
         row_copy(r).start()
 
-    def table_step(at):
+    def table_step(index):
         there = 2 * (1 - y) + core
+        at, side = index % 4, index // 4
+        part, base = slice(side * half, (side + 1) * half), 6 * side
         if at == 0:
-            t_copy(0).start()
-            t_copy(1).start()
+            t_copy(base).start()
+            t_copy(base + 1).start()
         elif at == 1:
-            for side in range(2):
-                t_copy(side).wait_recv()
-            table_vm[there] = added(table_vm[there], table_c[1 - y])
-            t_copy(2).start()
-            table_vm[narrow] = added(table_vm[narrow], table_c[y])
+            t_copy(base).wait_recv()
+            t_copy(base + 1).wait_recv()
+            table_vm[there, part] = added(table_vm[there, part], table_c[1 - y, part])
+            t_copy(base + 2).start()
+            table_vm[narrow, part] = added(table_vm[narrow, part], table_c[y, part])
         elif at == 2:
-            t_copy(2).wait()
-            part = added(table_vm[narrow], table_y[...])
-            table_vm[narrow] = part
-            t_copy(3).start()
-            t_copy(4).start()
-            own_quarter().start()
-            note(part.astype(f32))
+            t_copy(base + 2).wait()
+            total = added(table_vm[narrow, part], table_y[part])
+            table_vm[narrow, part] = total
+            t_copy(base + 3).start()
+            t_copy(base + 4).start()
+            own_half(side).start()
+            note(total.astype(f32))
         else:
-            t_copy(3).wait_recv()
-            t_copy(5).start()
+            t_copy(base + 3).wait_recv()
+            t_copy(base + 5).start()
 
     arrived = []
 
@@ -1137,11 +1157,12 @@
         small_copy(16, square_all.at[0], square_all.at[r], r, wide_peer(r)).start()
     spread_next(16, square_all, square_next)
     collect(16, square_next, square_out)
-    t_copy(4).wait_recv()
-    t_copy(5).wait_recv()
-    for at in (0, 1, 3, 4, 5):
-        t_copy(at).wait_send()
-    own_quarter().wait()
+    for side in range(2):
+        for at in (4, 5):
+            t_copy(6 * side + at).wait_recv()
+        for at in (0, 1, 3, 4, 5):
+            t_copy(6 * side + at).wait_send()
+        own_half(side).wait()
     w_copy(units - 1, 0).wait_send()
     for r in range(1, 8):
         row_copy(r).wait_send()
@@ -1202,11 +1223,11 @@
             dma((units, 5)),
             dma((8,)),
             dma((8,)),
-            dma((6,)),
-            dma((6,)),
+            dma((12,)),
+            dma((12,)),
             dma((32,)),
             dma((32,)),
-            dma((3,)),
+            dma((5,)),
         ],
         compiler_params=pltpu.CompilerParams(
             collective_id=1, has_side_effects=True, vmem_limit_bytes=62 * 2**20

time: 879 us -> 855 us (0.973)
  Pallas kernels: 653 us -> 629 us
    pallas_call x1, Pallas kernels: 283 us -> 259 us  [end_phase(): pl.pallas_call(functools.partial(end_kernel, kinds, places), in_specs=[an...]
  transfers between devices with their start and end apart: 6 -> 6, of which waited for: 1 -> 1; matrix products, arithmetic and copies ran while one was open for 7% -> 8% of each run, Pallas kernels for 2% -> 3%
where the time goes in v5:
time: 855 us; the launch traced here: 844 us
  Pallas kernels  629 us (74%)
  matrix products  94.1 us (11%)
  other arithmetic  64.1 us (7%)
  local copies, waits for them, and re-layouts  47.1 us (6%)
    pallas_call x1, Pallas kernels, end_phase(): pl.pallas_call(functools.partial(end_kernel, kinds, places), in_specs=[an...  259 us
    pallas_call x1, Pallas kernels, start_phase(): pl.pallas_call(functools.partial(start_kernel, units), in_specs=[vmem, vm...  209 us
    pallas_call x1, Pallas kernels, head_phase(): pl.pallas_call(functools.partial(head_kernel, vocab), in_specs=[vmem] * 5...  79.8 us
    pallas_call x3, Pallas kernels, attend_back(): pl.pallas_call(functools.partial(backward_kernel, has_bias, causal, centr...  52 us
    dot_general x13, matrix products, project(): return jnp.einsum('rk,nkc->nrc', rows, weights, preferred_element_type=f32)  50 us
    dot_general x13, matrix products, project_back(): return jnp.einsum('nrc,nkc->rk', grads, weights, preferred_element_type=f32)  42.1 us
    add x7, other arithmetic, body(): average_decay * avgs[index] + (1.0 - average_decay) * weight  35.9 us
    pallas_call x3, Pallas kernels, attend(): pl.pallas_call(functools.partial(forward_kernel, has_bias, causal, centre...  29.5 us
  transfers between devices with their start and end apart: 6, of which 1 were waited for; matrix products, arithmetic and copies ran while one was open for 8% of the time, Pallas kernels for 3%

profile of v5, /device:TPU:0, one launch (start us, length us, event | category | flops | bytes accessed | tf_op | source)
XLA Modules:
  0.0 844.2 jit_solution(6532454637848678591)
XLA Ops:
  7.5 208.8 %shard_map.442 = (bf16[2,2,2,2,2,96,768]{6,5,4,3,2,1,0:T(8,128)(2,1)}, bf16[2,2,2,2,2,96,768]{6,5,4,3,2,1,0:T(8,128)(2,1)}, bf16[2,2,2,2,2,96,768]{6,5,4,3,2,1,0...) custom-call(s32[1,640]{1,0:T(1,128)S(1)} %broadcast_in_dim.14.ids_re, ...), custom_call_target="tpu_custom_call" | custom-call | flops 32212254720 | bytes 33030144 | tf_op jit(solution)/shard_map/pallas_call | solution.py:580
  217.2 4.9 fusion.64.kvo_ref
  222.8 2.9 fusion.95.kvo_ref
  226.0 3.4 convolution_convert_fusion.1
  236.0 2.8 fusion.135
  238.8 17.3 %shard_map.444 = (bf16[4,512,192]{2,1,0:T(8,128)(2,1)S(1)}, f32[4,3,1,512]{3,2,1,0:T(1,128)S(1)}) custom-call(s32[2]{0:T(128)S(1)} %pad_add_fusion.1.scal, bf16[4,512,192]{2,1,0:T(8,128)(2,1)S(1)} %bitcast.347, bf16[4,512,384]{2,1,0:T(8,128)(2,1)} %fusion.64.kvo_ref, bf16[4,512,384]{2,1,0:T(8,128)(2,1)} %collective-permute-done.1.kvt_ref, ...), custom_call_target="tpu_custom_call" | custom-call | tf_op jit(solution)/shard_map/pallas_call | solution.py:199
  256.1 3.0 multiply_reduce_fusion.1
  259.5 5.6 fusion.10
  265.2 2.7 multiply_reduce_fusion
  283.9 4.2 shard_map.443
  292.0 2.8 fusion.141
  295.9 7.9 shard_map.445
  306.5 4.7 fusion.60
  313.7 79.8 %shard_map.446 = (f32[128,768]{1,0:T(8,128)}, bf16[4096,768]{1,0:T(8,128)(2,1)}, f32[1,128]{1,0:T(1,128)}) custom-call(bf16[128,768]{1,0:T(8,128)(2,1)} %multiply_convert_fusion.2.final_ref, bf16[4096,768]{1,0:T(8,128)(2,1)} %get-tuple-element.76.table_ref, s32[8,128]{1,0:T(8,128)} %get-tuple-element.279.target_ref, f32[1,128]{1,0:T(1,128)} %slice.388.weight_ref, ...), custom_call_target="tpu_custom_call" | custom-call | flops 19327352832 | bytes 20971520 | tf_op jit(solution)/shard_map/pallas_call | solution.py:795
  396.3 4.0 fusion.35.refs_11_
  400.3 4.9 multiply_reduce_fusion.2
  406.9 3.2 fusion.144
  413.5 13.4 %shard_map.447 = (bf16[4,128,192]{2,1,0:T(8,128)(2,1)S(1)}, f32[4,512,384]{2,1,0:T(8,128)S(1)}, bf16[4,512,384]{2,1,0:T(8,128)(2,1)}) custom-call(s32[2]{0:T(128)S(1)} %pad_add_fusion.1.scal, bf16[4,128,192]{2,1,0:T(8,128)(2,1)S(1)} %bitcast.353, bf16[4,512,384]{2,1,0:T(8,128)(2,1)} %fusion.61.kvo_ref, bf16[4,512,384]{2,1,0:T(8,128)(2,1)} %collective-permute-done.2.kvt_ref, ...), custom_call_target="tpu_custom_call" | custom-call | tf_op jit(solution)/shard_map/pallas_call | solution.py:326
  427.0 4.0 multiply_reduce_fusion.3
  432.6 3.2 fusion.138
  436.9 9.9 %shard_map.448 = (bf16[4,128,192]{2,1,0:T(8,128)(2,1)S(1)}, f32[4,128,384]{2,1,0:T(8,128)S(1)}, bf16[4,128,384]{2,1,0:T(8,128)(2,1)}, f32[4,3,2,8,256]{4,3,2,1,0:T(8,128)S(1)}) custom-call(s32[2]{0:T(128)S(1)} %pad_add_fusion.1.scal, bf16[4,128,192]{2,1,0:T(8,128)(2,1)S(1)} %bitcast.351, bf16[4,128,384]{2,1,0:T(8,128)(2,1)S(1)} %fusion.95.kvo_ref, ...), custom_call_target="tpu_custom_call" | custom-call | tf_op jit(solution)/shard_map/pallas_call | solution.py:326
  453.3 3.1 fusion.110
  456.4 2.8 fusion.170
  461.4 5.1 fusion.40
  468.0 6.1 fusion.6.refs_19_
  474.1 2.8 fusion.46
  479.7 3.8 convolution_convert_fusion
  485.0 28.8 %shard_map.449 = (bf16[4,512,192]{2,1,0:T(8,128)(2,1)S(1)}, f32[4,512,384]{2,1,0:T(8,128)S(1)}, bf16[4,512,384]{2,1,0:T(8,128)(2,1)}, f32[4,3,2,8,1024]{4,3,2,1,0:T(8,128)S(1)}) custom-call(s32[2]{0:T(128)S(1)} %pad_add_fusion.1.scal, bf16[4,512,192]{2,1,0:T(8,128)(2,1)S(1)} %bitcast.348, bf16[4,512,384]{2,1,0:T(8,128)(2,1)} %fusion.64.kvo_ref, ...), custom_call_target="tpu_custom_call" | custom-call | tf_op jit(solution)/shard_map/pallas_call | solution.py:326
  524.5 4.5 fusion.55
  533.3 259.3 %shard_map.450 = (f32[3,96,576]{2,1,0:T(8,128)}, f32[3,192,96]{2,1,0:T(8,128)}, f32[2,96,768]{2,1,0:T(8,128)}, f32[2,768,96]{2,1,0:T(8,128)}, bf16[4,1024,768]{2...) custom-call(bf16[128,768]{1,0:T(8,128)(2,1)} %copy-done.68, ...), custom_call_target="tpu_custom_call" | custom-call | flops 32212254720 | bytes 104857600 | tf_op jit(solution)/shard_map/pallas_call | solution.py:1184
  800.4 2.8 multiply_add_fusion.1
  808.8 28.5 %multiply_add_fusion = (f32[4016,768]{1,0:T(8,128)}, f32[4016,768]{1,0:T(8,128)}, f32[4016,768]{1,0:T(8,128)}) fusion(f32[4016,768]{1,0:T(8,128)} %param.51, f32[4016,768]{1,0:T(8,128)} %table_in.1, f32[4016,768]{1,0:T(8,128)} %param.44, f32[]{:T(128)S(6)} %min.3, bf16[4096,768]{1,0:T(8,128)(2,1)} %bitcast.360), kind=kLoop, calls=%fused_computation.3 | loop fusion | flops 33927168 | bytes 80191488 | tf_op jit(solution)/shard_map/add | solution.py:1553
  (497 shorter events, 96.7 us)
Async XLA Ops:
  217.1 8.9 %copy-start.48 = (bf16[512,768]{1,0:T(8,128)(2,1)}, bf16[512,768]{1,0:T(8,128)(2,1)S(1)}, u32[]{:S(2)}) copy-start(bf16[512,768]{1,0:T(8,128)(2,1)S(1)} %fusion.52.refs_9_) | copy-start | bytes 2359300
  222.1 16.7 %collective-permute-start.1 = (bf16[4,512,384]{2,1,0:T(8,128)(2,1)}, bf16[4,512,384]{2,1,0:T(8,128)(2,1)}, u32[]{:S(2)}, u32[]{:S(2)}) collective-permute-start(bf16[4,512,384]{2,1,0:T(8,128)(2,1)} %fusion.64.kvo_ref), channel_id=1, source_target_pairs={{0,1},{1,0},{2,3},{3,2},{4,5},{5,4},{6,7},{7,6},{8,9},{9,8},{10,11... | collective-permute-start | bytes 4718600 | tf_op jit(solution)/shard_map/ppermute | solution.py:33
  225.8 58.1 %collective-permute-start = (bf16[4,128,384]{2,1,0:T(8,128)(2,1)S(1)}, bf16[4,128,384]{2,1,0:T(8,128)(2,1)S(1)}, u32[]{:S(2)}, u32[]{:S(2)}) collective-permute-start(bf16[4,128,384]{2,1,0:T(8,128)(2,1)S(1)} %fusion.95.kvo_ref), channel_id=1, source_target_pairs={{0,1},{1,0},{2,3},{3,2},{4,5},{5,4},{6,7},{7,6},{8,9},{9,8},{10,11... | collective-permute-start | bytes 1179656 | tf_op jit(solution)/shard_map/ppermute | solution.py:33
  233.3 26.0 %copy-start.73 = (f32[768]{0:T(1024)}, f32[768]{0:T(1024)S(1)}, u32[]{:S(2)}) copy-start(f32[768]{0:T(1024)S(1)} %mul.834) | copy-start | bytes 9220
  233.3 34.6 %copy-start.70 = (f32[768]{0:T(1024)}, f32[768]{0:T(1024)S(1)}, u32[]{:S(2)}) copy-start(f32[768]{0:T(1024)S(1)} %mul.844) | copy-start | bytes 9220
  271.2 24.6 %collective-permute-start.2 = (bf16[4,512,384]{2,1,0:T(8,128)(2,1)}, bf16[4,512,384]{2,1,0:T(8,128)(2,1)}, u32[]{:S(2)}, u32[]{:S(2)}) collective-permute-start(bf16[4,512,384]{2,1,0:T(8,128)(2,1)} %fusion.61.kvo_ref), channel_id=1, source_target_pairs={{0,1},{1,0},{2,3},{3,2},{4,5},{5,4},{6,7},{7,6},{8,9},{9,8},{10,11... | collective-permute-start | bytes 4718600 | tf_op jit(solution)/shard_map/ppermute | solution.py:33
  295.9 8.0 copy-start.31
  303.9 7.3 slice-start
  413.5 13.4 %copy-start.32 = (f32[128,768]{1,0:T(8,128)S(1)}, f32[128,768]{1,0:T(8,128)}, u32[]{:S(2)}) copy-start(f32[128,768]{1,0:T(8,128)} %copy-done.30) | copy-start | bytes 1179652
  413.5 13.4 %copy-start.78 = (f32[768]{0:T(1024)S(1)}, f32[768]{0:T(1024)}, u32[]{:S(2)}) copy-start(f32[768]{0:T(1024)} %mul.822) | copy-start | bytes 9220
  413.5 13.4 %copy-start.110 = (f32[128]{0:T(128)S(1)}, f32[128]{0:T(128)}, u32[]{:S(2)}) copy-start(f32[128]{0:T(128)} %copy-done.109) | copy-start | bytes 1540
  435.8 14.1 %copy-start.92 = (f32[768]{0:T(1024)S(1)}, f32[768]{0:T(1024)}, u32[]{:S(2)}) copy-start(f32[768]{0:T(1024)} %get-tuple-element.186) | copy-start | bytes 9220
  436.9 13.0 %copy-start.104 = (f32[768]{0:T(1024)S(1)}, f32[768]{0:T(1024)}, u32[]{:S(2)}) copy-start(f32[768]{0:T(1024)} %get-tuple-element.184) | copy-start | bytes 9220
  436.9 13.0 %copy-start.94 = (f32[768]{0:T(1024)S(1)}, f32[768]{0:T(1024)}, u32[]{:S(2)}) copy-start(f32[768]{0:T(1024)} %get-tuple-element.182) | copy-start | bytes 9220
  436.9 13.4 %copy-start.26 = (pred[2047,32]{1,0:T(8,128)(4,1)S(1)}, pred[2047,32]{1,0:T(8,128)(4,1)}, u32[]{:S(2)}) copy-start(pred[2047,32]{1,0:T(8,128)(4,1)} %copy-done.25) | copy-start | bytes 196516
  449.2 10.1 %collective-permute-start.3 = (bf16[4,512,384]{2,1,0:T(8,128)(2,1)}, bf16[4,512,384]{2,1,0:T(8,128)(2,1)}, u32[]{:S(2)}, u32[]{:S(2)}) collective-permute-start(bf16[4,512,384]{2,1,0:T(8,128)(2,1)} %get-tuple-element.81), channel_id=1, source_target_pairs={{0,1},{1,0},{2,3},{3,2},{4,5},{5,4},{6,7},{7,6},{8,9},{9,8},{10,11... | collective-permute-start | bytes 4718600 | tf_op jit(solution)/shard_map/ppermute | solution.py:33
  449.3 3.8 collective-permute-start.4
  459.3 8.6 %slice-start.10 = ((s8[4718592]{0:T(1024)(128)(4,1)}), s8[4194304]{0:T(1024)(128)(4,1)S(1)}, s32[]{:S(2)}) async-start(s8[4718592]{0:T(1024)(128)(4,1)} %bitcast.439), calls=%async_computation.10 | async-start | bytes 8388608
  459.3 8.5 %slice-start.12 = ((s8[6291456]{0:T(1024)(128)(4,1)}), s8[4194304]{0:T(1024)(128)(4,1)S(1)}, s32[]{:S(2)}) async-start(s8[6291456]{0:T(1024)(128)(4,1)} %bitcast.448), calls=%async_computation.12 | async-start | bytes 8388608
  466.6 7.5 slice-start.6
  485.0 30.1 %copy-start.42 = (f32[128,768]{1,0:T(8,128)S(1)}, f32[128,768]{1,0:T(8,128)}, u32[]{:S(2)}) copy-start(f32[128,768]{1,0:T(8,128)} %get-tuple-element.219) | copy-start | bytes 1179652
  485.0 30.1 %copy-start.60 = (f32[128,768]{1,0:T(8,128)S(1)}, f32[128,768]{1,0:T(8,128)}, u32[]{:S(2)}) copy-start(f32[128,768]{1,0:T(8,128)} %get-tuple-element.277) | copy-start | bytes 1179652
  514.8 7.8 collective-permute-start.5
  533.3 265.3 %copy-start.96 = (f32[2,32,3]{1,0,2:T(2,128)S(1)}, f32[2,32,3]{1,0,2:T(2,128)}, u32[]{:S(2)}) copy-start(f32[2,32,3]{1,0,2:T(2,128)} %param.39) | copy-start | bytes 2308
  533.3 265.3 %copy-start.105 = (f32[2,32,3]{1,0,2:T(2,128)S(1)}, f32[2,32,3]{1,0,2:T(2,128)}, u32[]{:S(2)}) copy-start(f32[2,32,3]{1,0,2:T(2,128)} %param.53) | copy-start | bytes 2308
  533.3 265.3 %copy-start.106 = (f32[2,32,3]{1,0,2:T(2,128)S(1)}, f32[2,32,3]{1,0,2:T(2,128)}, u32[]{:S(2)}) copy-start(f32[2,32,3]{1,0,2:T(2,128)} %param.46) | copy-start | bytes 2308
  533.3 267.1 %copy-start.33 = (f32[2,768,96]{2,1,0:T(8,128)S(1)}, f32[2,768,96]{2,1,0:T(8,128)}, u32[]{:S(2)}) copy-start(f32[2,768,96]{2,1,0:T(8,128)} %copy.252) | copy-start | bytes 1769476
  533.3 267.1 %copy-start.34 = (f32[2,768,96]{2,1,0:T(8,128)S(1)}, f32[2,768,96]{2,1,0:T(8,128)}, u32[]{:S(2)}) copy-start(f32[2,768,96]{2,1,0:T(8,128)} %copy.251) | copy-start | bytes 1769476
  808.8 28.5 %copy-start.38 = (f32[2,96,768]{2,1,0:T(8,128)S(1)}, f32[2,96,768]{2,1,0:T(8,128)}, u32[]{:S(2)}) copy-start(f32[2,96,768]{2,1,0:T(8,128)} %param.35) | copy-start | bytes 1769476
  808.8 28.5 %copy-start.56 = (f32[2,96,768]{2,1,0:T(8,128)S(1)}, f32[2,96,768]{2,1,0:T(8,128)}, u32[]{:S(2)}) copy-start(f32[2,96,768]{2,1,0:T(8,128)} %param.49) | copy-start | bytes 1769476
  808.8 28.5 %copy-start.57 = (f32[2,96,768]{2,1,0:T(8,128)S(1)}, f32[2,96,768]{2,1,0:T(8,128)}, u32[]{:S(2)}) copy-start(f32[2,96,768]{2,1,0:T(8,128)} %param.42) | copy-start | bytes 1769476
  808.8 28.5 %copy-start.58 = (f32[2,96,768]{2,1,0:T(8,128)S(1)}, f32[2,96,768]{2,1,0:T(8,128)}, u32[]{:S(2)}) copy-start(f32[2,96,768]{2,1,0:T(8,128)} %get-tuple-element.99) | copy-start | bytes 1769476
  (108 other events, 330.8 us)
